TPU v7x, 128 devices: a whole 4x4x4 slice. The times are simulated.
128 devices in a mesh: blk: 16 (over x_hi, z, core), rep: 8 (over y, x_lo).
Axes of the slice: x: 4 (x_hi: 2, x_lo: 2; x = x_hi * 2 + x_lo), y: 4, z: 4, core: 2. Of those that a mesh axis runs over, the one named last changes fastest.
Arguments:
- features: bfloat16 [65536, 128], P(('blk', 'rep')), may hold values from -6 to 6
- cotangent: bfloat16 [65536, 128], P(('blk', 'rep')), may hold values from -6 to 6
- w_self: bfloat16 [128, 128], replicated, may hold values from -0.5 to 0.5
- w_neigh: bfloat16 [128, 128], replicated, may hold values from -0.5 to 0.5
- out_bias: float32 [128], replicated, may hold values from -3 to 3
- tile_values: bfloat16 [16, 8, 16, 32, 128, 128], P('blk', 'rep'), may hold values from 0 to 12, as said below
- dest_tile: int32 [16, 8, 16, 32], P('blk', 'rep'), may hold values from 0 to 31
- src_tile: int32 [16, 8, 16, 32], P('blk', 'rep'), may hold values from 0 to 3
- tile_count: int32 [16, 8, 16], P('blk', 'rep'), may hold values from 0 to 32, as said below
Outputs:
- activated: bfloat16 [65536, 128], P(('blk', 'rep'))
- grad_features: float32 [65536, 128], P(('blk', 'rep'))
- grad_w_self: float32 [128, 128], replicated
- grad_w_neigh: float32 [128, 128], replicated
- grad_bias: float32 [128], replicated
Inputs may be any that keep to these rules, and one draw needn't show every extreme that they name: `tile_values`: every entry is positive. `tile_count`: for every destination partition and member, the count for the source partition equal to the destination partition is 32.
All inputs are finite; a program needn't handle non-finite values.
Results may differ from a plain program's by a relative error of at most 0.007.
Values may be sent and summed in bfloat16 or wider, within the bound.
No kernel may reach another device: no remote copies, remote signals or barrier semaphores. Data moves between devices by JAX's collectives and lax.ppermute only.
A program may use at most 128 MiB of HBM per device.

v0:
```python
import jax
import jax.numpy as jnp
from jax import lax
from jax.sharding import PartitionSpec as P


def passed_along(value, axis, steps):
    count = lax.axis_size(axis)
    pairs = [(source, (source + steps) % count) for source in range(count)]
    return lax.ppermute(value, axis, pairs)


def slot_data(tiles, source):
    tile_values, dest_tile, src_tile, tile_count = tiles
    values = lax.dynamic_index_in_dim(tile_values[0, 0], source, 0, keepdims=False)
    dests = lax.dynamic_index_in_dim(dest_tile[0, 0], source, 0, keepdims=False)
    sources = lax.dynamic_index_in_dim(src_tile[0, 0], source, 0, keepdims=False)
    limit = lax.dynamic_index_in_dim(tile_count[0, 0], source, 0, keepdims=False)
    live = (jnp.arange(dests.shape[0], dtype=jnp.int32) < limit).astype(jnp.float32)
    return (values, dests, sources, live)


def forward_terms(tiles, block, source, totals):
    values, dests, sources, live = slot_data(tiles, source)
    tile_edge = values.shape[-1]
    width = block.shape[1]
    picked = block.reshape(-1, tile_edge, width)[sources]
    products = jnp.einsum("knm,kmf->knf", values, picked, preferred_element_type=jnp.float32)
    row_sums = jnp.einsum(
        "knm,m->kn",
        values,
        jnp.ones((tile_edge,), jnp.bfloat16),
        preferred_element_type=jnp.float32,
    )
    new_sums = totals[0].at[dests].add(products * live[:, None, None])
    new_degs = totals[1].at[dests].add(row_sums * live[:, None])
    return (new_sums, new_degs)


def backward_terms(tiles, spread, source, node_rows):
    values, dests, sources, live = slot_data(tiles, source)
    tile_edge = values.shape[-1]
    width = spread.shape[-1]
    picked = spread[dests]
    products = jnp.einsum("knm,knf->kmf", values, picked, preferred_element_type=jnp.float32)
    col_count = node_rows // tile_edge
    result = (
        jnp.zeros((col_count, tile_edge, width), jnp.float32)
        .at[sources]
        .add(products * live[:, None, None])
    )
    return result.reshape(node_rows, width)


def shards(
    features, cotangent, w_self, w_neigh, out_bias, tile_values, dest_tile, src_tile, tile_count
):
    tiles = (tile_values, dest_tile, src_tile, tile_count)
    cycle_size = lax.axis_size("blk")
    group = lax.axis_size("rep")
    here = lax.axis_index("blk")
    node_rows, width = features.shape
    tile_edge = tile_values.shape[-1]
    dest_count = group * node_rows // tile_edge
    totals = (
        jnp.zeros((dest_count, tile_edge, width), jnp.float32),
        jnp.zeros((dest_count, tile_edge), jnp.float32),
    )
    totals = forward_terms(tiles, features, here, totals)

    def visit_next(offset, carry):
        block, sums = carry
        block = passed_along(block, "blk", 1)
        return (block, forward_terms(tiles, block, (here - offset) % cycle_size, sums))

    block, totals = lax.fori_loop(1, cycle_size, visit_next, (features, totals))
    neighbour_sum, degree = (
        lax.psum_scatter(totals[0].reshape(-1, width), "rep", scatter_dimension=0, tiled=True),
        lax.psum_scatter(totals[1].reshape(-1), "rep", scatter_dimension=0, tiled=True),
    )
    scale = lax.rsqrt(1.0 + degree)[:, None]
    neighbour_mean = (neighbour_sum * scale).astype(jnp.bfloat16)
    pre = (
        jnp.dot(features, w_self, preferred_element_type=jnp.float32)
        + jnp.dot(neighbour_mean, w_neigh, preferred_element_type=jnp.float32)
        + out_bias
    )
    activated = jax.nn.silu(pre).astype(jnp.bfloat16)
    sigma = jax.nn.sigmoid(pre)
    grad_pre = (cotangent.astype(jnp.float32) * sigma * (1.0 + pre * (1.0 - sigma))).astype(
        jnp.bfloat16
    )
    contract = (((0,), (0,)), ((), ()))
    local_self = lax.dot_general(features, grad_pre, contract, preferred_element_type=jnp.float32)
    local_neigh = lax.dot_general(
        neighbour_mean, grad_pre, contract, preferred_element_type=jnp.float32
    )
    local_bias = jnp.sum(grad_pre.astype(jnp.float32), axis=0)
    grad_w_self, grad_w_neigh, grad_bias = lax.psum(
        (local_self, local_neigh, local_bias), ("blk", "rep")
    )
    sum_grad = (jnp.dot(grad_pre, w_neigh.T, preferred_element_type=jnp.float32) * scale).astype(
        jnp.bfloat16
    )
    spread = lax.all_gather(sum_grad, "rep", axis=0, tiled=True).reshape(
        dest_count, tile_edge, width
    )
    empty = jnp.zeros((node_rows, width), jnp.float32)

    def pass_one(offset, carry):
        carry = carry + backward_terms(tiles, spread, (here + 1 + offset) % cycle_size, node_rows)
        return passed_along(carry, "blk", -1)

    incoming = lax.fori_loop(0, cycle_size - 1, pass_one, empty)
    incoming = incoming + backward_terms(tiles, spread, here, node_rows)
    grad_features = jnp.dot(grad_pre, w_self.T, preferred_element_type=jnp.float32) + incoming
    return (activated, grad_features, grad_w_self, grad_w_neigh, grad_bias)


def solution(mesh):
    placed = (
        P(("blk", "rep"), None),
        P(("blk", "rep"), None),
        P(),
        P(),
        P(),
        P("blk", "rep", None, None, None, None),
        P("blk", "rep", None, None),
        P("blk", "rep", None, None),
        P("blk", "rep", None),
    )
    return jax.shard_map(
        shards,
        mesh=mesh,
        in_specs=placed,
        out_specs=(P(("blk", "rep"), None), P(("blk", "rep"), None), P(), P(), P()),
        check_vma=False,
    )
```

profile of v0, /device:TPU:0, one launch (start us, length us, event | category | flops | bytes accessed | tf_op | source)
XLA Modules:
  0.0 803.4 jit_solution(10513309264213310145)
XLA Ops:
  18.1 6.2 scatter_fusion.2
  24.3 250.2 %while.34 = (s32[]{:T(128)}, bf16[512,128]{1,0:T(8,128)(2,1)S(1)}, f32[32,128,128]{2,1,0:T(8,128)}, f32[32,128]{1,0:T(8,128)S(1)}, s32[]{:T(128)}, /*index=5*/s3...) while((s32[]{:T(128)}, bf16[512,128]{1,0:T(8,128)(2,1)S(1)}, ...), condition=%wide.region_5.6_spmd, body=%wide.region_2.5_spmd.sunk | while | flops 136324368 | bytes 14473180 | solution.py:76
  35.3 6.1 scatter_fusion
  51.9 6.1 scatter_fusion
  68.5 6.2 scatter_fusion
  85.2 6.1 scatter_fusion
  101.9 6.1 scatter_fusion
  118.5 6.1 scatter_fusion
  135.1 6.0 scatter_fusion
  151.7 6.1 scatter_fusion
  168.4 6.1 scatter_fusion
  185.0 6.1 scatter_fusion
  201.6 6.2 scatter_fusion
  218.3 6.2 scatter_fusion
  235.0 6.1 scatter_fusion
  251.6 6.1 scatter_fusion
  268.3 6.1 scatter_fusion
  276.3 35.3 %all-reduce = f32[4096]{0:T(1024)S(1)} all-reduce(f32[4096]{0:T(1024)S(1)} %bitcast.129), channel_id=3, replica_groups=mesh['blk'=16,'rep'=8] {'rep'}, use_global_device_ids=true, to_apply=%region_7.8.clone | all-reduce | flops 4096 | bytes 32768
  311.9 14.7 %reduce-scatter.2.cloned.1.call-done = f32[512,128]{1,0:T(8,128)} async-done(((f32[4096,128]{1,0:T(8,128)}), f32[512,128]{1,0:T(8,128)}) %reduce-scatter.2.cloned.1.call-update) | async-done | bytes 262160 | tf_op jit(solution)/shard_map/reduce_scatter | solution.py:78
  331.3 64.8 %psum.23 = f32[128]{0:T(128)} all-reduce(f32[128]{0:T(128)S(1)} %get-tuple-element.493), channel_id=1, replica_groups=mesh['blk'=16,'rep'=8] {'blk','rep'}, use_global_device_ids=true, to_apply=%region_15.16 | all-reduce | flops 128 | bytes 1024 | tf_op jit(solution)/shard_map/psum | solution.py:99
  396.1 75.9 %all-reduce.4.cloned.1.call-done = (f32[128,128]{0,1:T(8,128)}, f32[128,128]{1,0:T(8,128)}) async-done(((f32[128,128]{0,1:T(8,128)}, f32[128,128]{1,0:T(8,128)}), (f32[128,128]{0,1:T(8,128)}, f32[128,128]{1,0:T(8,128)})) %all-reduce.4.cloned.1.call-update) | async-done | bytes 131088 | tf_op jit(solution)/shard_map/psum | solution.py:99
  473.5 38.3 %all-gather.2.cloned.1.call-done = bf16[4096,128]{1,0:T(8,128)(2,1)} async-done(((bf16[512,128]{1,0:T(8,128)(2,1)}), bf16[4096,128]{1,0:T(8,128)(2,1)}) %all-gather.2.cloned.1.call-update) | async-done | bytes 1048592 | tf_op jit(solution)/shard_map/all_gather | solution.py:105
  519.0 274.4 %while.35 = (s32[]{:T(128)}, f32[512,128]{1,0:T(8,128)}, s32[]{:T(128)}, s32[1,1,16,32]{3,2,1,0:T(8,128)}, bf16[1,1,16,32,128,128]{5,4,3,2,1,0:T(8,128)(2,1)}, /...) while((s32[]{:T(128)}, f32[512,128]{1,0:T(8,128)}, ...), condition=%wide.region_10.11_spmd, body=%wide.region_8.10_spmd.sunk | while | flops 135333136 | bytes 16782868 | solution.py:114
  540.7 5.6 collective-permute-start.1
  559.4 5.6 collective-permute-start.1
  578.0 5.6 collective-permute-start.1
  596.7 5.6 collective-permute-start.1
  615.4 5.6 collective-permute-start.1
  634.0 5.6 collective-permute-start.1
  652.7 5.6 collective-permute-start.1
  708.6 5.6 collective-permute-start.1
  746.0 5.6 collective-permute-start.1
  (434 shorter events, 409.3 us)
Async XLA Ops:
  7.2 319.3 %reduce-scatter.2.cloned.1.call-start = ((), (), s32[]{:S(2)}) async-start(), calls=%async_computation.1 | async-start | bytes 2359296 | tf_op jit(solution)/shard_map/reduce_scatter | solution.py:78
  24.3 8.6 %collective-permute-start = (bf16[512,128]{1,0:T(8,128)(2,1)S(1)}, bf16[512,128]{1,0:T(8,128)(2,1)S(1)}, u32[]{:S(2)}, u32[]{:S(2)}) collective-permute-start(bf16[512,128]{1,0:T(8,128)(2,1)S(1)} %get-tuple-element.628), channel_id=1, source_target_pairs={{0,8},{8,16},{16,24},{24,32},{32,40},{40,48},{48,56},{56,64},{64,7... | collective-permute-start | bytes 393224 | tf_op jit(solution)/shard_map/while/body/eval_jaxpr/ppermute | solution.py:10
  41.4 8.1 %collective-permute-start = (bf16[512,128]{1,0:T(8,128)(2,1)S(1)}, bf16[512,128]{1,0:T(8,128)(2,1)S(1)}, u32[]{:S(2)}, u32[]{:S(2)}) collective-permute-start(bf16[512,128]{1,0:T(8,128)(2,1)S(1)} %get-tuple-element.628), channel_id=1, source_target_pairs={{0,8},{8,16},{16,24},{24,32},{32,40},{40,48},{48,56},{56,64},{64,7... | collective-permute-start | bytes 393224 | tf_op jit(solution)/shard_map/while/body/eval_jaxpr/ppermute | solution.py:10
  58.0 8.1 %collective-permute-start = (bf16[512,128]{1,0:T(8,128)(2,1)S(1)}, bf16[512,128]{1,0:T(8,128)(2,1)S(1)}, u32[]{:S(2)}, u32[]{:S(2)}) collective-permute-start(bf16[512,128]{1,0:T(8,128)(2,1)S(1)} %get-tuple-element.628), channel_id=1, source_target_pairs={{0,8},{8,16},{16,24},{24,32},{32,40},{40,48},{48,56},{56,64},{64,7... | collective-permute-start | bytes 393224 | tf_op jit(solution)/shard_map/while/body/eval_jaxpr/ppermute | solution.py:10
  74.7 8.1 %collective-permute-start = (bf16[512,128]{1,0:T(8,128)(2,1)S(1)}, bf16[512,128]{1,0:T(8,128)(2,1)S(1)}, u32[]{:S(2)}, u32[]{:S(2)}) collective-permute-start(bf16[512,128]{1,0:T(8,128)(2,1)S(1)} %get-tuple-element.628), channel_id=1, source_target_pairs={{0,8},{8,16},{16,24},{24,32},{32,40},{40,48},{48,56},{56,64},{64,7... | collective-permute-start | bytes 393224 | tf_op jit(solution)/shard_map/while/body/eval_jaxpr/ppermute | solution.py:10
  91.4 8.1 %collective-permute-start = (bf16[512,128]{1,0:T(8,128)(2,1)S(1)}, bf16[512,128]{1,0:T(8,128)(2,1)S(1)}, u32[]{:S(2)}, u32[]{:S(2)}) collective-permute-start(bf16[512,128]{1,0:T(8,128)(2,1)S(1)} %get-tuple-element.628), channel_id=1, source_target_pairs={{0,8},{8,16},{16,24},{24,32},{32,40},{40,48},{48,56},{56,64},{64,7... | collective-permute-start | bytes 393224 | tf_op jit(solution)/shard_map/while/body/eval_jaxpr/ppermute | solution.py:10
  108.0 8.1 %collective-permute-start = (bf16[512,128]{1,0:T(8,128)(2,1)S(1)}, bf16[512,128]{1,0:T(8,128)(2,1)S(1)}, u32[]{:S(2)}, u32[]{:S(2)}) collective-permute-start(bf16[512,128]{1,0:T(8,128)(2,1)S(1)} %get-tuple-element.628), channel_id=1, source_target_pairs={{0,8},{8,16},{16,24},{24,32},{32,40},{40,48},{48,56},{56,64},{64,7... | collective-permute-start | bytes 393224 | tf_op jit(solution)/shard_map/while/body/eval_jaxpr/ppermute | solution.py:10
  124.6 8.1 %collective-permute-start = (bf16[512,128]{1,0:T(8,128)(2,1)S(1)}, bf16[512,128]{1,0:T(8,128)(2,1)S(1)}, u32[]{:S(2)}, u32[]{:S(2)}) collective-permute-start(bf16[512,128]{1,0:T(8,128)(2,1)S(1)} %get-tuple-element.628), channel_id=1, source_target_pairs={{0,8},{8,16},{16,24},{24,32},{32,40},{40,48},{48,56},{56,64},{64,7... | collective-permute-start | bytes 393224 | tf_op jit(solution)/shard_map/while/body/eval_jaxpr/ppermute | solution.py:10
  141.2 8.1 %collective-permute-start = (bf16[512,128]{1,0:T(8,128)(2,1)S(1)}, bf16[512,128]{1,0:T(8,128)(2,1)S(1)}, u32[]{:S(2)}, u32[]{:S(2)}) collective-permute-start(bf16[512,128]{1,0:T(8,128)(2,1)S(1)} %get-tuple-element.628), channel_id=1, source_target_pairs={{0,8},{8,16},{16,24},{24,32},{32,40},{40,48},{48,56},{56,64},{64,7... | collective-permute-start | bytes 393224 | tf_op jit(solution)/shard_map/while/body/eval_jaxpr/ppermute | solution.py:10
  157.9 8.1 %collective-permute-start = (bf16[512,128]{1,0:T(8,128)(2,1)S(1)}, bf16[512,128]{1,0:T(8,128)(2,1)S(1)}, u32[]{:S(2)}, u32[]{:S(2)}) collective-permute-start(bf16[512,128]{1,0:T(8,128)(2,1)S(1)} %get-tuple-element.628), channel_id=1, source_target_pairs={{0,8},{8,16},{16,24},{24,32},{32,40},{40,48},{48,56},{56,64},{64,7... | collective-permute-start | bytes 393224 | tf_op jit(solution)/shard_map/while/body/eval_jaxpr/ppermute | solution.py:10
  174.5 8.1 %collective-permute-start = (bf16[512,128]{1,0:T(8,128)(2,1)S(1)}, bf16[512,128]{1,0:T(8,128)(2,1)S(1)}, u32[]{:S(2)}, u32[]{:S(2)}) collective-permute-start(bf16[512,128]{1,0:T(8,128)(2,1)S(1)} %get-tuple-element.628), channel_id=1, source_target_pairs={{0,8},{8,16},{16,24},{24,32},{32,40},{40,48},{48,56},{56,64},{64,7... | collective-permute-start | bytes 393224 | tf_op jit(solution)/shard_map/while/body/eval_jaxpr/ppermute | solution.py:10
  191.1 8.1 %collective-permute-start = (bf16[512,128]{1,0:T(8,128)(2,1)S(1)}, bf16[512,128]{1,0:T(8,128)(2,1)S(1)}, u32[]{:S(2)}, u32[]{:S(2)}) collective-permute-start(bf16[512,128]{1,0:T(8,128)(2,1)S(1)} %get-tuple-element.628), channel_id=1, source_target_pairs={{0,8},{8,16},{16,24},{24,32},{32,40},{40,48},{48,56},{56,64},{64,7... | collective-permute-start | bytes 393224 | tf_op jit(solution)/shard_map/while/body/eval_jaxpr/ppermute | solution.py:10
  207.8 8.1 %collective-permute-start = (bf16[512,128]{1,0:T(8,128)(2,1)S(1)}, bf16[512,128]{1,0:T(8,128)(2,1)S(1)}, u32[]{:S(2)}, u32[]{:S(2)}) collective-permute-start(bf16[512,128]{1,0:T(8,128)(2,1)S(1)} %get-tuple-element.628), channel_id=1, source_target_pairs={{0,8},{8,16},{16,24},{24,32},{32,40},{40,48},{48,56},{56,64},{64,7... | collective-permute-start | bytes 393224 | tf_op jit(solution)/shard_map/while/body/eval_jaxpr/ppermute | solution.py:10
  224.5 8.1 %collective-permute-start = (bf16[512,128]{1,0:T(8,128)(2,1)S(1)}, bf16[512,128]{1,0:T(8,128)(2,1)S(1)}, u32[]{:S(2)}, u32[]{:S(2)}) collective-permute-start(bf16[512,128]{1,0:T(8,128)(2,1)S(1)} %get-tuple-element.628), channel_id=1, source_target_pairs={{0,8},{8,16},{16,24},{24,32},{32,40},{40,48},{48,56},{56,64},{64,7... | collective-permute-start | bytes 393224 | tf_op jit(solution)/shard_map/while/body/eval_jaxpr/ppermute | solution.py:10
  241.1 8.1 %collective-permute-start = (bf16[512,128]{1,0:T(8,128)(2,1)S(1)}, bf16[512,128]{1,0:T(8,128)(2,1)S(1)}, u32[]{:S(2)}, u32[]{:S(2)}) collective-permute-start(bf16[512,128]{1,0:T(8,128)(2,1)S(1)} %get-tuple-element.628), channel_id=1, source_target_pairs={{0,8},{8,16},{16,24},{24,32},{32,40},{40,48},{48,56},{56,64},{64,7... | collective-permute-start | bytes 393224 | tf_op jit(solution)/shard_map/while/body/eval_jaxpr/ppermute | solution.py:10
  257.8 8.1 %collective-permute-start = (bf16[512,128]{1,0:T(8,128)(2,1)S(1)}, bf16[512,128]{1,0:T(8,128)(2,1)S(1)}, u32[]{:S(2)}, u32[]{:S(2)}) collective-permute-start(bf16[512,128]{1,0:T(8,128)(2,1)S(1)} %get-tuple-element.628), channel_id=1, source_target_pairs={{0,8},{8,16},{16,24},{24,32},{32,40},{40,48},{48,56},{56,64},{64,7... | collective-permute-start | bytes 393224 | tf_op jit(solution)/shard_map/while/body/eval_jaxpr/ppermute | solution.py:10
  274.5 197.5 %all-reduce.4.cloned.1.call-start = ((), (), s32[]{:S(2)}) async-start(), calls=%async_computation.3 | async-start | bytes 262144 | tf_op jit(solution)/shard_map/psum | solution.py:99
  330.4 181.5 %all-gather.2.cloned.1.call-start = ((), (), s32[]{:S(2)}) async-start(), calls=%async_computation.2 | async-start | bytes 1179648 | tf_op jit(solution)/shard_map/all_gather | solution.py:105
  540.7 9.5 %collective-permute-start.1 = (f32[512,128]{1,0:T(8,128)S(1)}, f32[512,128]{1,0:T(8,128)S(1)}, u32[]{:S(2)}, u32[]{:S(2)}) collective-permute-start(f32[512,128]{1,0:T(8,128)S(1)} %bitcast_add_fusion.3), channel_id=1, source_target_pairs={{0,120},{8,0},{16,8},{24,16},{32,24},{40,32},{48,40},{56,48},{64,5... | collective-permute-start | bytes 786440 | tf_op jit(solution)/shard_map/while/body/eval_jaxpr/ppermute | solution.py:10
  559.4 9.5 %collective-permute-start.1 = (f32[512,128]{1,0:T(8,128)S(1)}, f32[512,128]{1,0:T(8,128)S(1)}, u32[]{:S(2)}, u32[]{:S(2)}) collective-permute-start(f32[512,128]{1,0:T(8,128)S(1)} %bitcast_add_fusion.3), channel_id=1, source_target_pairs={{0,120},{8,0},{16,8},{24,16},{32,24},{40,32},{48,40},{56,48},{64,5... | collective-permute-start | bytes 786440 | tf_op jit(solution)/shard_map/while/body/eval_jaxpr/ppermute | solution.py:10
  578.0 9.5 %collective-permute-start.1 = (f32[512,128]{1,0:T(8,128)S(1)}, f32[512,128]{1,0:T(8,128)S(1)}, u32[]{:S(2)}, u32[]{:S(2)}) collective-permute-start(f32[512,128]{1,0:T(8,128)S(1)} %bitcast_add_fusion.3), channel_id=1, source_target_pairs={{0,120},{8,0},{16,8},{24,16},{32,24},{40,32},{48,40},{56,48},{64,5... | collective-permute-start | bytes 786440 | tf_op jit(solution)/shard_map/while/body/eval_jaxpr/ppermute | solution.py:10
  596.7 9.5 %collective-permute-start.1 = (f32[512,128]{1,0:T(8,128)S(1)}, f32[512,128]{1,0:T(8,128)S(1)}, u32[]{:S(2)}, u32[]{:S(2)}) collective-permute-start(f32[512,128]{1,0:T(8,128)S(1)} %bitcast_add_fusion.3), channel_id=1, source_target_pairs={{0,120},{8,0},{16,8},{24,16},{32,24},{40,32},{48,40},{56,48},{64,5... | collective-permute-start | bytes 786440 | tf_op jit(solution)/shard_map/while/body/eval_jaxpr/ppermute | solution.py:10
  615.4 9.5 %collective-permute-start.1 = (f32[512,128]{1,0:T(8,128)S(1)}, f32[512,128]{1,0:T(8,128)S(1)}, u32[]{:S(2)}, u32[]{:S(2)}) collective-permute-start(f32[512,128]{1,0:T(8,128)S(1)} %bitcast_add_fusion.3), channel_id=1, source_target_pairs={{0,120},{8,0},{16,8},{24,16},{32,24},{40,32},{48,40},{56,48},{64,5... | collective-permute-start | bytes 786440 | tf_op jit(solution)/shard_map/while/body/eval_jaxpr/ppermute | solution.py:10
  634.0 9.5 %collective-permute-start.1 = (f32[512,128]{1,0:T(8,128)S(1)}, f32[512,128]{1,0:T(8,128)S(1)}, u32[]{:S(2)}, u32[]{:S(2)}) collective-permute-start(f32[512,128]{1,0:T(8,128)S(1)} %bitcast_add_fusion.3), channel_id=1, source_target_pairs={{0,120},{8,0},{16,8},{24,16},{32,24},{40,32},{48,40},{56,48},{64,5... | collective-permute-start | bytes 786440 | tf_op jit(solution)/shard_map/while/body/eval_jaxpr/ppermute | solution.py:10
  652.7 9.5 %collective-permute-start.1 = (f32[512,128]{1,0:T(8,128)S(1)}, f32[512,128]{1,0:T(8,128)S(1)}, u32[]{:S(2)}, u32[]{:S(2)}) collective-permute-start(f32[512,128]{1,0:T(8,128)S(1)} %bitcast_add_fusion.3), channel_id=1, source_target_pairs={{0,120},{8,0},{16,8},{24,16},{32,24},{40,32},{48,40},{56,48},{64,5... | collective-permute-start | bytes 786440 | tf_op jit(solution)/shard_map/while/body/eval_jaxpr/ppermute | solution.py:10
  671.3 9.5 %collective-permute-start.1 = (f32[512,128]{1,0:T(8,128)S(1)}, f32[512,128]{1,0:T(8,128)S(1)}, u32[]{:S(2)}, u32[]{:S(2)}) collective-permute-start(f32[512,128]{1,0:T(8,128)S(1)} %bitcast_add_fusion.3), channel_id=1, source_target_pairs={{0,120},{8,0},{16,8},{24,16},{32,24},{40,32},{48,40},{56,48},{64,5... | collective-permute-start | bytes 786440 | tf_op jit(solution)/shard_map/while/body/eval_jaxpr/ppermute | solution.py:10
  690.0 9.5 %collective-permute-start.1 = (f32[512,128]{1,0:T(8,128)S(1)}, f32[512,128]{1,0:T(8,128)S(1)}, u32[]{:S(2)}, u32[]{:S(2)}) collective-permute-start(f32[512,128]{1,0:T(8,128)S(1)} %bitcast_add_fusion.3), channel_id=1, source_target_pairs={{0,120},{8,0},{16,8},{24,16},{32,24},{40,32},{48,40},{56,48},{64,5... | collective-permute-start | bytes 786440 | tf_op jit(solution)/shard_map/while/body/eval_jaxpr/ppermute | solution.py:10
  708.6 9.5 %collective-permute-start.1 = (f32[512,128]{1,0:T(8,128)S(1)}, f32[512,128]{1,0:T(8,128)S(1)}, u32[]{:S(2)}, u32[]{:S(2)}) collective-permute-start(f32[512,128]{1,0:T(8,128)S(1)} %bitcast_add_fusion.3), channel_id=1, source_target_pairs={{0,120},{8,0},{16,8},{24,16},{32,24},{40,32},{48,40},{56,48},{64,5... | collective-permute-start | bytes 786440 | tf_op jit(solution)/shard_map/while/body/eval_jaxpr/ppermute | solution.py:10
  727.3 9.5 %collective-permute-start.1 = (f32[512,128]{1,0:T(8,128)S(1)}, f32[512,128]{1,0:T(8,128)S(1)}, u32[]{:S(2)}, u32[]{:S(2)}) collective-permute-start(f32[512,128]{1,0:T(8,128)S(1)} %bitcast_add_fusion.3), channel_id=1, source_target_pairs={{0,120},{8,0},{16,8},{24,16},{32,24},{40,32},{48,40},{56,48},{64,5... | collective-permute-start | bytes 786440 | tf_op jit(solution)/shard_map/while/body/eval_jaxpr/ppermute | solution.py:10
  746.0 9.5 %collective-permute-start.1 = (f32[512,128]{1,0:T(8,128)S(1)}, f32[512,128]{1,0:T(8,128)S(1)}, u32[]{:S(2)}, u32[]{:S(2)}) collective-permute-start(f32[512,128]{1,0:T(8,128)S(1)} %bitcast_add_fusion.3), channel_id=1, source_target_pairs={{0,120},{8,0},{16,8},{24,16},{32,24},{40,32},{48,40},{56,48},{64,5... | collective-permute-start | bytes 786440 | tf_op jit(solution)/shard_map/while/body/eval_jaxpr/ppermute | solution.py:10
  764.6 9.5 %collective-permute-start.1 = (f32[512,128]{1,0:T(8,128)S(1)}, f32[512,128]{1,0:T(8,128)S(1)}, u32[]{:S(2)}, u32[]{:S(2)}) collective-permute-start(f32[512,128]{1,0:T(8,128)S(1)} %bitcast_add_fusion.3), channel_id=1, source_target_pairs={{0,120},{8,0},{16,8},{24,16},{32,24},{40,32},{48,40},{56,48},{64,5... | collective-permute-start | bytes 786440 | tf_op jit(solution)/shard_map/while/body/eval_jaxpr/ppermute | solution.py:10
  783.3 9.5 %collective-permute-start.1 = (f32[512,128]{1,0:T(8,128)S(1)}, f32[512,128]{1,0:T(8,128)S(1)}, u32[]{:S(2)}, u32[]{:S(2)}) collective-permute-start(f32[512,128]{1,0:T(8,128)S(1)} %bitcast_add_fusion.3), channel_id=1, source_target_pairs={{0,120},{8,0},{16,8},{24,16},{32,24},{40,32},{48,40},{56,48},{64,5... | collective-permute-start | bytes 786440 | tf_op jit(solution)/shard_map/while/body/eval_jaxpr/ppermute | solution.py:10
  (41 other events, 1024.9 us)
Sparse Core Ops, SparseCore 0:
  274.6 51.8 reduce-scatter.1
  332.0 139.9 all-reduce.3
  474.3 37.5 all-gather.1
where the time goes:
time: 811 us; the launch traced here: 803 us
  waiting for transfers between devices  242 us (30%)
  other arithmetic  197 us (24%)
  blocking collectives  100 us (12%)
  matrix products  87 us (11%)
  local copies, waits for them, and re-layouts  80.9 us (10%)
  starting transfers between devices  79.5 us (10%)
  between operations  14.6 us (2%)
    ppermute x30, waiting for transfers between devices, passed_along(): return lax.ppermute(value, axis, pairs)  113 us
    scatter-add x16, other arithmetic, forward_terms(): new_sums = totals[0].at[dests].add(products * live[:, None, None])  98 us
    ppermute x30, starting transfers between devices, passed_along(): return lax.ppermute(value, axis, pairs)  79.4 us
    psum x1, waiting for transfers between devices, shards(): lax.psum((local_self, local_neigh, local_bias), ('blk', 'rep'))  75.9 us
    psum x1, blocking collectives, shards(): lax.psum((local_self, local_neigh, local_bias), ('blk', 'rep'))  64.8 us
    scatter-add x16, other arithmetic, backward_terms(): result = jnp.zeros((col_count, tile_edge, width), jnp.float32).at[sources...  42.5 us
    all_gather x1, waiting for transfers between devices, shards(): lax.all_gather(sum_grad, 'rep', axis=0, tiled=True)  38.3 us
    unnamed x1, blocking collectives  35.3 us
  transfers between devices with their start and end apart: 33, of which 33 were waited for; matrix products, arithmetic and copies ran while one was open for 9% of the time, Pallas kernels for 0%

commit v1 on v0

v1 whole, which is shorter than its diff:
```python
import functools

import jax
import jax.numpy as jnp
from jax import lax
from jax.experimental import pallas as pl
from jax.experimental.pallas import tpu as pltpu
from jax.sharding import PartitionSpec as P

f32, bf16 = jnp.float32, jnp.bfloat16
T = 128
SLOTS = 32
NSRC = 4
NDST = 32
REP = 8
CH = 8
U = 4
DEG = 16
WROWS = 40
WX = 2 * WROWS
SMEM = pl.BlockSpec(memory_space=pltpu.SMEM)
VMEM = pl.BlockSpec(memory_space=pltpu.VMEM)
ANY = pl.BlockSpec(memory_space=pl.ANY)


def params(mib=40):
    return pltpu.CompilerParams(vmem_limit_bytes=mib * 1024 * 1024)


def blk_at(dx, dz, dc):
    here = lax.axis_index("blk")
    x, z, c = here // 8, (here // 2) % 4, here % 2
    return (x + dx) % 2 * 8 + (z + dz) % 4 * 2 + (c + dc) % 2


def moved(value, dx, dz, dc):
    pairs = []
    for i in range(16):
        x, z, c = i // 8, (i // 2) % 4, i % 2
        pairs.append((i, (x + dx) % 2 * 8 + (z + dz) % 4 * 2 + (c + dc) % 2))
    return lax.ppermute(value, "blk", pairs)


def high_low(v):
    high = v.astype(bf16)
    return high, (v - high.astype(f32)).astype(bf16)


def start_copies(tiles, buf, sem, p, j, count):
    def go(c, _):
        pltpu.make_async_copy(
            tiles.at[p, pl.ds(c * CH, CH)], buf.at[j, pl.ds(c * CH, CH)], sem.at[j, c]
        ).start()
        return 0

    lax.fori_loop(0, (count + CH - 1) // CH, go, 0)


def walk(tiles, buf, sem, p, j, count, group):
    def chunk(c, _):
        pltpu.make_async_copy(
            tiles.at[p, pl.ds(c * CH, CH)], buf.at[j, pl.ds(c * CH, CH)], sem.at[j, c]
        ).wait()
        left = jnp.minimum(count - c * CH, CH)
        lax.fori_loop(0, (left + U - 1) // U, lambda g, _: (group(c * CH + g * U), 0)[1], 0)
        return 0

    lax.fori_loop(0, (count + CH - 1) // CH, chunk, 0)


def degree_kernel(dests, counts, tiles, deg_out, buf, acc, sem):
    acc[...] = jnp.zeros_like(acc)
    ones = jnp.ones((8, T), bf16)
    for p in range(16):
        start_copies(tiles, buf, sem, p, p, counts[p])
    for p in range(16):
        count = counts[p]

        def group(first):
            sums, places = [], []
            for u in range(U):
                k = first + u
                places.append(jnp.where(k < count, dests[p * SLOTS + k], NDST))
                sums.append(
                    lax.dot_general(
                        ones, buf[p, k], (((1,), (1,)), ((), ())), preferred_element_type=f32
                    )
                )
            for u in range(U):
                acc[places[u]] += sums[u]

        walk(tiles, buf, sem, p, p, count, group)
    for d in range(NDST):
        deg_out[d : d + 1, :] = acc[d, 0:1, :]


def degrees(dests, counts, tiles):
    return pl.pallas_call(
        degree_kernel,
        name="degrees",
        out_shape=jax.ShapeDtypeStruct((NDST, T), f32),
        in_specs=[SMEM, SMEM, ANY],
        out_specs=VMEM,
        scratch_shapes=[
            pltpu.VMEM((16, SLOTS, T, T), bf16),
            pltpu.VMEM((NDST + 1, 8, T), f32),
            pltpu.SemaphoreType.DMA((16, SLOTS // CH)),
        ],
        compiler_params=params(),
        cost_estimate=pl.CostEstimate(flops=10**9, bytes_accessed=12 * 10**6, transcendentals=0),
    )(dests, counts, tiles)


def forward_kernel(places, first, last, *refs):
    n = len(places)
    dests, srcs, counts, tiles, deg, *refs = refs
    feats, refs = refs[:n], refs[n:]
    if not first:
        (acc_in, out, buf, acc, sem) = refs
    else:
        (out, buf, acc, sem) = refs
    parts = [blk_at(*w) for w in places]
    for j, p in enumerate(parts):
        start_copies(tiles, buf, sem, p, j, counts[p])
    if first:
        acc[...] = jnp.zeros_like(acc)
    else:
        acc[0:NDST] = acc_in[...]
    for j, p in enumerate(parts):
        count = counts[p]
        feat, row0 = feats[j]

        def group(k0):
            sums, where = [], []
            for u in range(U):
                k = k0 + u
                where.append(jnp.where(k < count, dests[p * SLOTS + k], NDST))
                row = pl.multiple_of(row0 + srcs[p * SLOTS + k] * T, T)
                sums.append(
                    jnp.dot(buf[j, k], feat[pl.ds(row, T), :], preferred_element_type=f32)
                )
            for u in range(U):
                acc[where[u]] += sums[u]

        walk(tiles, buf, sem, p, j, count, group)
    if not last:
        out[...] = acc[0:NDST]
    else:
        for m in range(REP):
            out[m, 0 : NSRC * T, :] = acc[m * NSRC : (m + 1) * NSRC].reshape(NSRC * T, T).astype(bf16)
            high, low = high_low(deg[m * NSRC : (m + 1) * NSRC, :])
            out[m, NSRC * T :, :] = jnp.concatenate(
                [high, low, jnp.zeros((DEG - 2 * NSRC, T), bf16)], axis=0
            )


def forward(places, blocks, dests, srcs, counts, tiles, deg, acc, last):
    n = len(places)
    first = acc is None
    rows = NSRC * T

    def kernel(*refs):
        head, refs = refs[:5], refs[5:]
        held, refs = refs[: len(blocks)], refs[len(blocks) :]
        feats = [
            (ref, i * rows) for ref, b in zip(held, blocks) for i in range(b.shape[0] // rows)
        ]
        forward_kernel(places, first, last, *head, *feats, *refs)

    if last:
        shape = jax.ShapeDtypeStruct((REP, rows + DEG, T), bf16)
    else:
        shape = jax.ShapeDtypeStruct((NDST, T, T), f32)
    extra = () if first else (acc,)
    return pl.pallas_call(
        kernel,
        name="forward_last" if last else "forward_first",
        out_shape=shape,
        in_specs=[SMEM, SMEM, SMEM, ANY, VMEM] + [VMEM] * (len(blocks) + len(extra)),
        out_specs=VMEM,
        scratch_shapes=[
            pltpu.VMEM((n, SLOTS, T, T), bf16),
            pltpu.VMEM((NDST + 1, T, T), f32),
            pltpu.SemaphoreType.DMA((n, SLOTS // CH)),
        ],
        compiler_params=params(),
        cost_estimate=pl.CostEstimate(
            flops=n * 17 * 2 * T**3, bytes_accessed=n * 17 * T * T * 2, transcendentals=0
        ),
    )(dests, srcs, counts, tiles, deg, *blocks, *extra)


def dense_kernel(recv, features, cotangent, w_self, w_neigh, bias, act, payload, self_t):
    rows = NSRC * T
    total = recv[0, 0:rows, :].astype(f32)
    deg = jnp.zeros((NSRC, T), f32)
    for m in range(REP):
        if m:
            total += recv[m, 0:rows, :].astype(f32)
        extra = recv[m, rows:, :].astype(f32)
        deg += extra[0:NSRC] + extra[NSRC : 2 * NSRC]
    scale = lax.rsqrt(1.0 + deg)
    eye = lax.broadcasted_iota(jnp.int32, (T, T), 0) == lax.broadcasted_iota(jnp.int32, (T, T), 1)
    columns = [
        jnp.sum(jnp.where(eye, scale[i : i + 1, :], 0.0), axis=1, keepdims=True) for i in range(NSRC)
    ]
    mean = (total * jnp.concatenate(columns, axis=0)).astype(bf16)
    feat = features[...]
    pre = (
        jnp.dot(feat, w_self[...], preferred_element_type=f32)
        + jnp.dot(mean, w_neigh[...], preferred_element_type=f32)
        + bias[...]
    )
    sigma = jax.nn.sigmoid(pre)
    act[...] = (pre * sigma).astype(bf16)
    grad = (cotangent[...].astype(f32) * sigma * (1.0 + pre * (1.0 - sigma))).astype(bf16)
    down = (((0,), (0,)), ((), ()))
    across = (((1,), (1,)), ((), ()))
    g_self = lax.dot_general(feat, grad, down, preferred_element_type=f32)
    g_neigh = lax.dot_general(mean, grad, down, preferred_element_type=f32)
    g_bias = jnp.sum(grad.astype(f32), axis=0, keepdims=True)
    sum_t = lax.dot_general(w_neigh[...], grad, across, preferred_element_type=f32)
    own_t = lax.dot_general(w_self[...], grad, across, preferred_element_type=f32)
    spread = []
    for i in range(NSRC):
        part = slice(i * T, (i + 1) * T)
        spread.append((sum_t[:, part] * scale[i : i + 1, :]).astype(bf16))
        self_t[i] = own_t[:, part]
    bias_rows = jnp.broadcast_to(g_bias, (8, T))
    for m in range(REP):
        for i in range(NSRC):
            payload[m, i * T : (i + 1) * T, :] = spread[i]
        piece = slice(m * 16, (m + 1) * 16)
        segment = jnp.concatenate([g_self[piece], g_neigh[piece], bias_rows], axis=0)
        payload[m, rows:, :] = jnp.concatenate(high_low(segment), axis=0)


def dense(recv, features, cotangent, w_self, w_neigh, bias):
    rows = NSRC * T
    return pl.pallas_call(
        dense_kernel,
        name="dense",
        out_shape=(
            jax.ShapeDtypeStruct((rows, T), bf16),
            jax.ShapeDtypeStruct((REP, rows + WX, T), bf16),
            jax.ShapeDtypeStruct((NSRC, T, T), f32),
        ),
        in_specs=[VMEM] * 6,
        out_specs=(VMEM, VMEM, VMEM),
        compiler_params=params(),
    )(recv, features, cotangent, w_self, w_neigh, bias.reshape(1, T))


def segment_of(rows):
    wide = rows.astype(f32)
    return wide[0:WROWS] + wide[WROWS:]


def backward_kernel(dz, first, dests, srcs, counts, tiles, recv, send, keep, buf, acc, sem):
    rows = NSRC * T
    places = [(0, dz, 1), (1, dz, 1), (0, dz, 0), (1, dz, 0)]
    parts = [blk_at(*w) for w in places]
    for j, p in enumerate(parts):
        start_copies(tiles, buf, sem, p, j, counts[p])
    acc[...] = jnp.zeros_like(acc)
    if first:
        total = segment_of(recv[0, rows:, :])
        for m in range(1, REP):
            total += segment_of(recv[m, rows:, :])
        send[2 * rows :, :] = jnp.concatenate(high_low(total), axis=0)
    for j, p in enumerate(parts):
        count = counts[p]

        def group(k0):
            sums, where = [], []
            for u in range(U):
                k = k0 + u
                where.append(jnp.where(k < count, srcs[p * SLOTS + k], NSRC))
                d = dests[p * SLOTS + k]
                row = pl.multiple_of(d % NSRC * T, T)
                sums.append(
                    jnp.dot(recv[d // NSRC, pl.ds(row, T), :], buf[j, k], preferred_element_type=f32)
                )
            for u in range(U):
                acc[j, where[u]] += sums[u]

        walk(tiles, buf, sem, p, j, count, group)
        whole = acc[j, 0:NSRC].reshape(rows, T)
        if j < 2:
            send[j * rows : (j + 1) * rows, :] = whole.astype(bf16)
        else:
            keep[(j - 2) * rows : (j - 1) * rows, :] = whole


def backward(dz, first, dests, srcs, counts, tiles, recv):
    rows = NSRC * T
    return pl.pallas_call(
        functools.partial(backward_kernel, dz, first),
        name=f"backward_z{dz}",
        out_shape=(
            jax.ShapeDtypeStruct((2 * rows + (WX if first else 0), T), bf16),
            jax.ShapeDtypeStruct((2 * rows, T), f32),
        ),
        in_specs=[SMEM, SMEM, SMEM, ANY, VMEM],
        out_specs=(VMEM, VMEM),
        scratch_shapes=[
            pltpu.VMEM((4, SLOTS, T, T), bf16),
            pltpu.VMEM((4, NSRC + 1, T, T), f32),
            pltpu.SemaphoreType.DMA((4, SLOTS // CH)),
        ],
        compiler_params=params(),
        cost_estimate=pl.CostEstimate(
            flops=4 * 17 * 2 * T**3, bytes_accessed=4 * 17 * T * T * 2, transcendentals=0
        ),
    )(dests, srcs, counts, tiles, recv)


def join_kernel(keep, got, seg, mine, out):
    rows = 2 * NSRC * T
    out[0:rows, :] = (keep[...] + got[0:rows, :].astype(f32)).astype(bf16)
    if mine is None:
        out[rows:, :] = seg[...]
    else:
        total = segment_of(mine[rows:, :]) + segment_of(got[rows:, :])
        out[rows:, :] = jnp.concatenate(high_low(total), axis=0)


def join(keep, got, seg=None, mine=None):
    rows = 2 * NSRC * T
    if mine is not None:
        body = lambda k, g, m, o: join_kernel(k, g, None, m, o)
        operands = (keep, got, mine)
    else:
        body = lambda k, g, s, o: join_kernel(k, g, s, None, o)
        operands = (keep, got, seg)
    return pl.pallas_call(
        body,
        name="join",
        out_shape=jax.ShapeDtypeStruct((rows + WX, T), bf16),
        in_specs=[VMEM] * 3,
        out_specs=VMEM,
        compiler_params=params(16),
    )(*operands)


def sum_kernel(keep, got, za, zb, zc, seg, near, far):
    rows = NSRC * T

    def total(lo, hi):
        v = keep[lo:hi, :] + got[lo:hi, :].astype(f32)
        for ref in (za, zb, zc):
            v += ref[lo:hi, :].astype(f32)
        return v

    near[0:rows, :] = total(0, rows)
    far[0:rows, :] = total(rows, 2 * rows).astype(bf16)
    s = segment_of(seg[...])
    for ref in (za, zb, zc):
        s += segment_of(ref[2 * rows :, :])
    near[rows:, :] = s
    far[rows:, :] = jnp.concatenate(high_low(s), axis=0)


def sum_up(keep, got, za, zb, zc, seg):
    rows = NSRC * T
    return pl.pallas_call(
        sum_kernel,
        name="sum_up",
        out_shape=(
            jax.ShapeDtypeStruct((rows + WROWS, T), f32),
            jax.ShapeDtypeStruct((rows + WX, T), bf16),
        ),
        in_specs=[VMEM] * 6,
        out_specs=(VMEM, VMEM),
        compiler_params=params(16),
    )(keep, got, za, zb, zc, seg)


def final_kernel(near, far, self_t, out, seg):
    rows = NSRC * T
    for i in range(NSRC):
        part = slice(i * T, (i + 1) * T)
        block = near[part, :] + far[part, :].astype(f32) + self_t[i]
        out[part, :] = block.T
    seg[...] = near[rows:, :] + segment_of(far[rows:, :])


def final(near, far, self_t):
    rows = NSRC * T
    return pl.pallas_call(
        final_kernel,
        name="final",
        out_shape=(
            jax.ShapeDtypeStruct((rows, T), f32),
            jax.ShapeDtypeStruct((WROWS, T), f32),
        ),
        in_specs=[VMEM] * 3,
        out_specs=(VMEM, VMEM),
        compiler_params=params(16),
    )(near, far, self_t)


def shards(
    features, cotangent, w_self, w_neigh, out_bias, tile_values, dest_tile, src_tile, tile_count
):
    tiles = tile_values[0, 0]
    dests, srcs, counts = dest_tile.reshape(-1), src_tile.reshape(-1), tile_count.reshape(-1)
    rows = NSRC * T

    opposite = moved(features, 1, 0, 0)
    pair = jnp.concatenate([features, opposite], axis=0)
    za, zb, zc = moved(pair, 0, 2, 0), moved(pair, 0, 1, 0), moved(pair, 0, 3, 0)
    deg = degrees(dests, counts, tiles)
    held = (pair, za, zb, zc)
    others = tuple(moved(h, 0, 0, 1) for h in held)
    near_places = [(x, z, 0) for z in (0, -2, -1, -3) for x in (0, 1)]
    far_places = [(x, z, 1) for z in (0, -2, -1, -3) for x in (0, 1)]
    acc = forward(near_places, held, dests, srcs, counts, tiles, deg, None, False)
    sums = forward(far_places, others, dests, srcs, counts, tiles, deg, acc, True)
    recv = lax.all_to_all(sums, "rep", 0, 0)

    act, payload, self_t = dense(recv, features, cotangent, w_self, w_neigh, out_bias)
    spread = lax.all_to_all(payload, "rep", 0, 0)

    seg = None
    joined = []
    for dz in (2, 1, 3, 0):
        send, keep = backward(dz, dz == 2, dests, srcs, counts, tiles, spread)
        got = moved(send, 0, 0, 1)
        if dz == 0:
            break
        if seg is None:
            out = join(keep, got, mine=send)
            seg = out[2 * rows :]
        else:
            out = join(keep, got, seg=seg)
        joined.append(moved(out, 0, dz, 0))
    near, far = sum_up(keep, got, *joined, seg)
    grad_features, segment = final(near, moved(far, 1, 0, 0), self_t)
    weights = lax.all_to_all(jnp.broadcast_to(segment[None, 0:32], (REP, 32, T)), "rep", 0, 0)
    grad_w_self = weights[:, 0:16].reshape(T, T)
    grad_w_neigh = weights[:, 16:32].reshape(T, T)
    return (act, grad_features, grad_w_self, grad_w_neigh, segment[32])


def solution(mesh):
    placed = (
        P(("blk", "rep"), None),
        P(("blk", "rep"), None),
        P(),
        P(),
        P(),
        P("blk", "rep", None, None, None, None),
        P("blk", "rep", None, None),
        P("blk", "rep", None, None),
        P("blk", "rep", None),
    )
    return jax.shard_map(
        shards,
        mesh=mesh,
        in_specs=placed,
        out_specs=(P(("blk", "rep"), None), P(("blk", "rep"), None), P(), P(), P()),
        check_vma=False,
    )
```

time: 811 us -> 164 us (0.20); the launches traced: 803 us -> 166 us
  waiting for transfers between devices: 242 us -> 30.8 us
  other arithmetic: 197 us -> 0 us
  matrix products: 87 us -> 0 us
  local copies, waits for them, and re-layouts: 80.9 us -> 5.04 us
  starting transfers between devices: 79.5 us -> 22.1 us
  Pallas kernels: 0 us -> 56.9 us
  blocking collectives: 100 us -> 50.1 us
  between operations: 14.6 us -> 0.89 us
    scatter-add x48 -> x0, other arithmetic: 153 us -> none  [the longest x16 98 us: forward_terms(): new_sums = totals[0].at[dests].add(products * live[:, None, None])]
    ppermute x30 -> x16, waiting for transfers between devices: 113 us -> 24.6 us  [moved(): return lax.ppermute(value, 'blk', pairs)]
    dot_general x54 -> x0, matrix products: 87 us -> none  [the longest x16 28.4 us: backward_terms(): jnp.einsum('knm,knf->kmf', values, picked, preferred_element_type=jnp.flo...]
    psum x1 -> x0, waiting for transfers between devices: 75.9 us -> none  [shards(): lax.psum((local_self, local_neigh, local_bias), ('blk', 'rep'))]
    psum x1 -> x0, blocking collectives: 64.8 us -> none  [shards(): lax.psum((local_self, local_neigh, local_bias), ('blk', 'rep'))]
    ppermute x30 -> x16, starting transfers between devices: 79.4 us -> 15.8 us  [moved(): return lax.ppermute(value, 'blk', pairs)]
    pallas_call x0 -> x13, Pallas kernels: none -> 56.9 us  [the longest x4 20.9 us: backward(): pl.pallas_call(functools.partial(backward_kernel, dz, first), name=f'back...]
    all_to_all x0 -> x2, blocking collectives: none -> 50.1 us  [the longest x1 29.7 us: shards(): recv = lax.all_to_all(sums, 'rep', 0, 0)]
  transfers between devices with their start and end apart: 33 -> 17, of which waited for: 33 -> 9; matrix products, arithmetic and copies ran while one was open for 9% -> 2% of each run, Pallas kernels for 0% -> 26%
where the time goes in v1:
time: 164 us; the launch traced here: 166 us
  Pallas kernels  56.9 us (35%)
  blocking collectives  50.1 us (31%)
  waiting for transfers between devices  30.8 us (19%)
  starting transfers between devices  22.1 us (13%)
  local copies, waits for them, and re-layouts  5.04 us (3%)
    all_to_all x1, blocking collectives, shards(): recv = lax.all_to_all(sums, 'rep', 0, 0)  29.7 us
    ppermute x16, waiting for transfers between devices, moved(): return lax.ppermute(value, 'blk', pairs)  24.6 us
    pallas_call x4, Pallas kernels, backward(): pl.pallas_call(functools.partial(backward_kernel, dz, first), name=f'back...  20.9 us
    all_to_all x1, blocking collectives, shards(): spread = lax.all_to_all(payload, 'rep', 0, 0)  20.4 us
    pallas_call x2, Pallas kernels, forward(): pl.pallas_call(kernel, name='forward_last' if last else 'forward_first',...  18.2 us
    ppermute x16, starting transfers between devices, moved(): return lax.ppermute(value, 'blk', pairs)  15.8 us
    pallas_call x1, Pallas kernels, degrees(): pl.pallas_call(degree_kernel, name='degrees', out_shape=jax.ShapeDtypeStr...  15.4 us
    all_to_all x1, starting transfers between devices, shards(): lax.all_to_all(jnp.broadcast_to(segment[None, 0:32], (REP, 32, T)), 'rep'...  6.33 us
  transfers between devices with their start and end apart: 17, of which 9 were waited for; matrix products, arithmetic and copies ran while one was open for 2% of the time, Pallas kernels for 26%

profile of v1, /device:TPU:0, one launch (start us, length us, event | category | flops | bytes accessed | tf_op | source)
XLA Modules:
  0.0 165.8 jit_solution(16776359208860909326)
XLA Ops:
  0.6 3.2 %collective-permute-start = (bf16[512,128]{1,0:T(8,128)(2,1)}, bf16[512,128]{1,0:T(8,128)(2,1)S(1)}, u32[]{:S(2)}, u32[]{:S(2)}) collective-permute-start(bf16[512,128]{1,0:T(8,128)(2,1)} %features.1), channel_id=1, source_target_pairs={{0,64},{8,72},{16,80},{24,88},{32,96},{40,104},{48,112},{56,120},{... | collective-permute-start | bytes 393224 | tf_op jit(solution)/shard_map/ppermute | solution.py:41
  3.8 0.9 constant_dynamic-update-slice_fusion.1
  4.8 2.8 %collective-permute-done = bf16[512,128]{1,0:T(8,128)(2,1)S(1)} collective-permute-done((bf16[512,128]{1,0:T(8,128)(2,1)}, bf16[512,128]{1,0:T(8,128)(2,1)S(1)}, u32[]{:S(2)}, u32[]{:S(2)}) %collective-permute-start) | collective-permute-done | bytes 131104 | tf_op jit(solution)/shard_map/ppermute | solution.py:41
  7.5 4.2 %collective-permute-start.2 = (bf16[1024,128]{1,0:T(8,128)(2,1)S(1)}, bf16[1024,128]{1,0:T(8,128)(2,1)S(1)}, u32[]{:S(2)}, u32[]{:S(2)}) collective-permute-start(bf16[1024,128]{1,0:T(8,128)(2,1)S(1)} %constant_dynamic-update-slice_fusion.refs_5_), channel_id=1, source_target_pairs={{0,32},{8,40},{16,48},{24,56},{32,0},{40,8},{48,16},{56,24},{64,96... | collective-permute-start | bytes 786440 | tf_op jit(solution)/shard_map/ppermute | solution.py:41
  11.7 1.0 collective-permute-start.4
  12.7 2.2 %collective-permute-start.6 = (bf16[1024,128]{1,0:T(8,128)(2,1)S(1)}, bf16[1024,128]{1,0:T(8,128)(2,1)S(1)}, u32[]{:S(2)}, u32[]{:S(2)}) collective-permute-start(bf16[1024,128]{1,0:T(8,128)(2,1)S(1)} %constant_dynamic-update-slice_fusion.refs_5_), channel_id=1, source_target_pairs={{0,48},{8,56},{16,0},{24,8},{32,16},{40,24},{48,32},{56,40},{64,11... | collective-permute-start | bytes 786440 | tf_op jit(solution)/shard_map/ppermute | solution.py:41
  15.0 4.0 %collective-permute-done.2.refs_6_ = bf16[1024,128]{1,0:T(8,128)(2,1)S(1)} collective-permute-done((bf16[1024,128]{1,0:T(8,128)(2,1)S(1)}, bf16[1024,128]{1,0:T(8,128)(2,1)S(1)}, u32[]{:S(2)}, u32[]{:S(2)}) %collective-permute-start.2) | collective-permute-done | bytes 262176 | tf_op jit(solution)/shard_map/ppermute | solution.py:41
  18.9 3.8 %collective-permute-done.4.refs_7_ = bf16[1024,128]{1,0:T(8,128)(2,1)S(1)} collective-permute-done((bf16[1024,128]{1,0:T(8,128)(2,1)S(1)}, bf16[1024,128]{1,0:T(8,128)(2,1)S(1)}, u32[]{:S(2)}, u32[]{:S(2)}) %collective-permute-start.4) | collective-permute-done | bytes 262176 | tf_op jit(solution)/shard_map/ppermute | solution.py:41
  22.8 0.7 collective-permute-done.6.refs_8_
  23.5 0.8 reshape.29.dests.refs_0_
  24.3 0.8 reshape.30.refs_1_.srcs
  25.7 15.4 %degrees.1.refs_4_ = f32[32,128]{1,0:T(8,128)S(1)} custom-call(s32[512]{0:T(512)S(1)} %reshape.29.dests.refs_0_, s32[16]{0:T(128)S(1)} %bitcast.11, bf16[16,32,128,128]{3,2,1,0:T(8,128)(2,1)} %bitcast.19), custom_call_target="tpu_custom_call" | custom-call | flops 1000000000 | bytes 12000000 | tf_op jit(solution)/shard_map/degrees/pallas_call | solution.py:98
  41.2 10.3 %forward_first.1.refs_9_ = f32[32,128,128]{2,1,0:T(8,128)S(1)} custom-call(s32[512]{0:T(512)S(1)} %reshape.29.dests.refs_0_, s32[512]{0:T(512)S(1)} %reshape.30.refs_1_.srcs, s32[16]{0:T(128)S(1)} %bitcast.12, bf16[16,32,128,128]{3,2,1,0:T(8,128)(2,1)} %bitcast.20, f32[32,128]{1,0:T(8,128)S(1)} %degrees.1.refs_4_, ...), custom_call_target="tpu_custom_call" | custom-call | flops 570425344 | bytes 4456448 | tf_op jit(solution)/shard_map/forward_first/pallas_call | solution.py:175
  51.6 7.8 %forward_last.1 = bf16[8,528,128]{2,1,0:T(8,128)(2,1)S(1)} custom-call(s32[512]{0:T(512)S(1)} %reshape.29.dests.refs_0_, s32[512]{0:T(512)S(1)} %reshape.30.refs_1_.srcs, s32[16]{0:T(128)S(1)} %bitcast.13, bf16[16,32,128,128]{3,2,1,0:T(8,128)(2,1)} %bitcast.21, f32[32,128]{1,0:T(8,128)S(1)} %degrees.1.refs_4_, ...), custom_call_target="tpu_custom_call" | custom-call | flops 570425344 | bytes 4456448 | tf_op jit(solution)/shard_map/forward_last/pallas_call | solution.py:175
  59.4 29.7 %all_to_all.15.recv = bf16[8,528,128]{2,1,0:T(8,128)(2,1)S(1)} all-to-all(bf16[8,528,128]{2,1,0:T(8,128)(2,1)S(1)} %forward_last.1), channel_id=1, replica_groups=mesh['blk'=16,'rep'=8] {'rep'}, dimensions={0} | all-to-all | bytes 2162688 | tf_op jit(solution)/shard_map/all_to_all | solution.py:420
  89.2 1.2 dense.1
  90.4 20.4 %all_to_all.16.recv = bf16[8,592,128]{2,1,0:T(8,128)(2,1)S(1)} all-to-all(bf16[8,592,128]{2,1,0:T(8,128)(2,1)S(1)} %get-tuple-element.21), channel_id=1, replica_groups=mesh['blk'=16,'rep'=8] {'rep'}, dimensions={0} | all-to-all | bytes 2424832 | tf_op jit(solution)/shard_map/all_to_all | solution.py:423
  110.8 4.3 %backward_z2.1 = (bf16[1104,128]{1,0:T(8,128)(2,1)S(1)}, f32[1024,128]{1,0:T(8,128)S(1)}) custom-call(s32[512]{0:T(512)S(1)} %reshape.29.dests.refs_0_, s32[512]{0:T(512)S(1)} %reshape.30.refs_1_.srcs, s32[16]{0:T(128)S(1)} %bitcast.14, bf16[16,32,128,128]{3,2,1,0:T(8,128)(2,1)} %bitcast.22, bf16[8,592,128]{2,1,0:T(8,128)(2,1)S(1)} %all_to_all.16.recv), custom_call_target="tpu_custom_call" | custom-call | flops 285212672 | bytes 2228224 | tf_op jit(solution)/shard_map/backward_z2/pallas_call | solution.py:297
  115.2 5.8 %backward_z3.1 = (bf16[1024,128]{1,0:T(8,128)(2,1)S(1)}, f32[1024,128]{1,0:T(8,128)S(1)}) custom-call(s32[512]{0:T(512)S(1)} %reshape.29.dests.refs_0_, s32[512]{0:T(512)S(1)} %reshape.30.refs_1_.srcs, s32[16]{0:T(128)S(1)} %bitcast.15, bf16[16,32,128,128]{3,2,1,0:T(8,128)(2,1)} %bitcast.23, bf16[8,592,128]{2,1,0:T(8,128)(2,1)S(1)} %all_to_all.16.recv), custom_call_target="tpu_custom_call" | custom-call | flops 285212672 | bytes 2228224 | tf_op jit(solution)/shard_map/backward_z3/pallas_call | solution.py:297
  121.1 4.9 %backward_z1.1 = (bf16[1024,128]{1,0:T(8,128)(2,1)S(1)}, f32[1024,128]{1,0:T(8,128)S(1)}) custom-call(s32[512]{0:T(512)S(1)} %reshape.29.dests.refs_0_, s32[512]{0:T(512)S(1)} %reshape.30.refs_1_.srcs, s32[16]{0:T(128)S(1)} %bitcast.16, bf16[16,32,128,128]{3,2,1,0:T(8,128)(2,1)} %bitcast.24, bf16[8,592,128]{2,1,0:T(8,128)(2,1)S(1)} %all_to_all.16.recv), custom_call_target="tpu_custom_call" | custom-call | flops 285212672 | bytes 2228224 | tf_op jit(solution)/shard_map/backward_z1/pallas_call | solution.py:297
  126.4 3.8 %collective-permute-start.14 = (bf16[1104,128]{1,0:T(8,128)(2,1)S(1)}, bf16[1104,128]{1,0:T(8,128)(2,1)S(1)}, u32[]{:S(2)}, u32[]{:S(2)}) collective-permute-start(bf16[1104,128]{1,0:T(8,128)(2,1)S(1)} %join.5), channel_id=1, source_target_pairs={{0,48},{8,56},{16,0},{24,8},{32,16},{40,24},{48,32},{56,40},{64,11... | collective-permute-start | bytes 847880 | tf_op jit(solution)/shard_map/ppermute | solution.py:41
  130.3 5.8 %backward_z0.1 = (bf16[1024,128]{1,0:T(8,128)(2,1)S(1)}, f32[1024,128]{1,0:T(8,128)S(1)}) custom-call(s32[512]{0:T(512)S(1)} %reshape.29.dests.refs_0_, s32[512]{0:T(512)S(1)} %reshape.30.refs_1_.srcs, s32[16]{0:T(128)S(1)} %bitcast.17, bf16[16,32,128,128]{3,2,1,0:T(8,128)(2,1)} %bitcast.25, bf16[8,592,128]{2,1,0:T(8,128)(2,1)S(1)} %all_to_all.16.recv), custom_call_target="tpu_custom_call" | custom-call | flops 285212672 | bytes 2228224 | tf_op jit(solution)/shard_map/backward_z0/pallas_call | solution.py:297
  136.2 1.5 collective-permute-done.8.got
  137.8 2.6 %collective-permute-done.14.zc = bf16[1104,128]{1,0:T(8,128)(2,1)S(1)} collective-permute-done((bf16[1104,128]{1,0:T(8,128)(2,1)S(1)}, bf16[1104,128]{1,0:T(8,128)(2,1)S(1)}, u32[]{:S(2)}, u32[]{:S(2)}) %collective-permute-start.14) | collective-permute-done | bytes 282656 | tf_op jit(solution)/shard_map/ppermute | solution.py:41
  140.4 2.6 %collective-permute-done.12.zb = bf16[1104,128]{1,0:T(8,128)(2,1)S(1)} collective-permute-done((bf16[1104,128]{1,0:T(8,128)(2,1)S(1)}, bf16[1104,128]{1,0:T(8,128)(2,1)S(1)}, u32[]{:S(2)}, u32[]{:S(2)}) %collective-permute-start.12) | collective-permute-done | bytes 282656 | tf_op jit(solution)/shard_map/ppermute | solution.py:41
  143.2 0.9 collective-permute-start.15
  144.1 6.5 %collective-permute-done.15.far = bf16[592,128]{1,0:T(8,128)(2,1)S(1)} collective-permute-done((bf16[592,128]{1,0:T(8,128)(2,1)S(1)}, bf16[592,128]{1,0:T(8,128)(2,1)S(1)}, u32[]{:S(2)}, u32[]{:S(2)}) %collective-permute-start.15) | collective-permute-done | bytes 151584 | tf_op jit(solution)/shard_map/ppermute | solution.py:41
  150.6 0.8 final.1
  151.5 0.7 broadcast_in_dim.2
  152.1 6.3 %all-to-all-start.2 = ((f32[8,32,128]{2,1,0:T(8,128)}), f32[8,32,128]{2,1,0:T(8,128)S(1)}, u32[]{:S(2)}, u32[]{:S(2)}) async-start(f32[8,32,128]{2,1,0:T(8,128)} %broadcast_in_dim.2), calls=%async_computation.2 | async-start | bytes 262144 | tf_op jit(solution)/shard_map/all_to_all | solution.py:440
  159.0 6.2 %all-to-all-done.2 = f32[8,32,128]{2,1,0:T(8,128)S(1)} async-done(((f32[8,32,128]{2,1,0:T(8,128)}), f32[8,32,128]{2,1,0:T(8,128)S(1)}, u32[]{:S(2)}, u32[]{:S(2)}) %all-to-all-start.2) | async-done | bytes 131104 | tf_op jit(solution)/shard_map/all_to_all | solution.py:440
  165.2 0.7 fusion
  (40 shorter events, 2.1 us)
Async XLA Ops:
  0.6 6.9 %collective-permute-start = (bf16[512,128]{1,0:T(8,128)(2,1)}, bf16[512,128]{1,0:T(8,128)(2,1)S(1)}, u32[]{:S(2)}, u32[]{:S(2)}) collective-permute-start(bf16[512,128]{1,0:T(8,128)(2,1)} %features.1), channel_id=1, source_target_pairs={{0,64},{8,72},{16,80},{24,88},{32,96},{40,104},{48,112},{56,120},{... | collective-permute-start | bytes 393224 | tf_op jit(solution)/shard_map/ppermute | solution.py:41
  7.5 11.4 %collective-permute-start.2 = (bf16[1024,128]{1,0:T(8,128)(2,1)S(1)}, bf16[1024,128]{1,0:T(8,128)(2,1)S(1)}, u32[]{:S(2)}, u32[]{:S(2)}) collective-permute-start(bf16[1024,128]{1,0:T(8,128)(2,1)S(1)} %constant_dynamic-update-slice_fusion.refs_5_), channel_id=1, source_target_pairs={{0,32},{8,40},{16,48},{24,56},{32,0},{40,8},{48,16},{56,24},{64,96... | collective-permute-start | bytes 786440 | tf_op jit(solution)/shard_map/ppermute | solution.py:41
  11.7 11.1 %collective-permute-start.4 = (bf16[1024,128]{1,0:T(8,128)(2,1)S(1)}, bf16[1024,128]{1,0:T(8,128)(2,1)S(1)}, u32[]{:S(2)}, u32[]{:S(2)}) collective-permute-start(bf16[1024,128]{1,0:T(8,128)(2,1)S(1)} %constant_dynamic-update-slice_fusion.refs_5_), channel_id=1, source_target_pairs={{0,16},{8,24},{16,32},{24,40},{32,48},{40,56},{48,0},{56,8},{64,80... | collective-permute-start | bytes 786440 | tf_op jit(solution)/shard_map/ppermute | solution.py:41
  12.7 10.8 %collective-permute-start.6 = (bf16[1024,128]{1,0:T(8,128)(2,1)S(1)}, bf16[1024,128]{1,0:T(8,128)(2,1)S(1)}, u32[]{:S(2)}, u32[]{:S(2)}) collective-permute-start(bf16[1024,128]{1,0:T(8,128)(2,1)S(1)} %constant_dynamic-update-slice_fusion.refs_5_), channel_id=1, source_target_pairs={{0,48},{8,56},{16,0},{24,8},{32,16},{40,24},{48,32},{56,40},{64,11... | collective-permute-start | bytes 786440 | tf_op jit(solution)/shard_map/ppermute | solution.py:41
  15.0 36.6 %collective-permute-start.1 = (bf16[1024,128]{1,0:T(8,128)(2,1)S(1)}, bf16[1024,128]{1,0:T(8,128)(2,1)S(1)}, u32[]{:S(2)}, u32[]{:S(2)}) collective-permute-start(bf16[1024,128]{1,0:T(8,128)(2,1)S(1)} %constant_dynamic-update-slice_fusion.refs_5_), channel_id=1, source_target_pairs={{0,8},{8,0},{16,24},{24,16},{32,40},{40,32},{48,56},{56,48},{64,72... | collective-permute-start | bytes 786440 | tf_op jit(solution)/shard_map/ppermute | solution.py:41
  18.9 32.6 %collective-permute-start.3 = (bf16[1024,128]{1,0:T(8,128)(2,1)S(1)}, bf16[1024,128]{1,0:T(8,128)(2,1)S(1)}, u32[]{:S(2)}, u32[]{:S(2)}) collective-permute-start(bf16[1024,128]{1,0:T(8,128)(2,1)S(1)} %collective-permute-done.2.refs_6_), channel_id=1, source_target_pairs={{0,8},{8,0},{16,24},{24,16},{32,40},{40,32},{48,56},{56,48},{64,72... | collective-permute-start | bytes 786440 | tf_op jit(solution)/shard_map/ppermute | solution.py:41
  22.8 28.8 %collective-permute-start.5 = (bf16[1024,128]{1,0:T(8,128)(2,1)S(1)}, bf16[1024,128]{1,0:T(8,128)(2,1)S(1)}, u32[]{:S(2)}, u32[]{:S(2)}) collective-permute-start(bf16[1024,128]{1,0:T(8,128)(2,1)S(1)} %collective-permute-done.4.refs_7_), channel_id=1, source_target_pairs={{0,8},{8,0},{16,24},{24,16},{32,40},{40,32},{48,56},{56,48},{64,72... | collective-permute-start | bytes 786440 | tf_op jit(solution)/shard_map/ppermute | solution.py:41
  23.5 28.0 %collective-permute-start.7 = (bf16[1024,128]{1,0:T(8,128)(2,1)S(1)}, bf16[1024,128]{1,0:T(8,128)(2,1)S(1)}, u32[]{:S(2)}, u32[]{:S(2)}) collective-permute-start(bf16[1024,128]{1,0:T(8,128)(2,1)S(1)} %collective-permute-done.6.refs_8_), channel_id=1, source_target_pairs={{0,8},{8,0},{16,24},{24,16},{32,40},{40,32},{48,56},{56,48},{64,72... | collective-permute-start | bytes 786440 | tf_op jit(solution)/shard_map/ppermute | solution.py:41
  25.1 0.7 copy-start.4
  59.4 29.8 %copy-start = (bf16[512,128]{1,0:T(8,128)(2,1)S(1)}, bf16[512,128]{1,0:T(8,128)(2,1)}, u32[]{:S(2)}) copy-start(bf16[512,128]{1,0:T(8,128)(2,1)} %features.1) | copy-start | bytes 393220
  59.4 29.8 %copy-start.1 = (bf16[512,128]{1,0:T(8,128)(2,1)S(1)}, bf16[512,128]{1,0:T(8,128)(2,1)}, u32[]{:S(2)}) copy-start(bf16[512,128]{1,0:T(8,128)(2,1)} %cotangent.1) | copy-start | bytes 393220
  59.4 29.8 %copy-start.2 = (bf16[128,128]{1,0:T(8,128)(2,1)S(1)}, bf16[128,128]{1,0:T(8,128)(2,1)}, u32[]{:S(2)}) copy-start(bf16[128,128]{1,0:T(8,128)(2,1)} %w_self.1) | copy-start | bytes 98308
  59.4 29.8 %copy-start.3 = (bf16[128,128]{1,0:T(8,128)(2,1)S(1)}, bf16[128,128]{1,0:T(8,128)(2,1)}, u32[]{:S(2)}) copy-start(bf16[128,128]{1,0:T(8,128)(2,1)} %w_neigh.1) | copy-start | bytes 98308
  59.4 29.8 %copy-start.6 = (f32[128]{0:T(128)S(1)}, f32[128]{0:T(128)}, u32[]{:S(2)}) copy-start(f32[128]{0:T(128)} %param.13) | copy-start | bytes 1540
  90.4 20.4 %copy-start.5 = (s32[1,1,16]{2,1,0:T(1,128)S(1)}, s32[1,1,16]{2,1,0:T(1,128)}, u32[]{:S(2)}) copy-start(s32[1,1,16]{2,1,0:T(1,128)} %param.17) | copy-start | bytes 196
  115.1 11.0 %collective-permute-start.9 = (bf16[1104,128]{1,0:T(8,128)(2,1)S(1)}, bf16[1104,128]{1,0:T(8,128)(2,1)S(1)}, u32[]{:S(2)}, u32[]{:S(2)}) collective-permute-start(bf16[1104,128]{1,0:T(8,128)(2,1)S(1)} %get-tuple-element.25.m), channel_id=1, source_target_pairs={{0,8},{8,0},{16,24},{24,16},{32,40},{40,32},{48,56},{56,48},{64,72... | collective-permute-start | bytes 847880 | tf_op jit(solution)/shard_map/ppermute | solution.py:41
  121.0 5.3 %collective-permute-start.13 = (bf16[1024,128]{1,0:T(8,128)(2,1)S(1)}, bf16[1024,128]{1,0:T(8,128)(2,1)S(1)}, u32[]{:S(2)}, u32[]{:S(2)}) collective-permute-start(bf16[1024,128]{1,0:T(8,128)(2,1)S(1)} %get-tuple-element.29), channel_id=1, source_target_pairs={{0,8},{8,0},{16,24},{24,16},{32,40},{40,32},{48,56},{56,48},{64,72... | collective-permute-start | bytes 786440 | tf_op jit(solution)/shard_map/ppermute | solution.py:41
  126.0 4.1 %collective-permute-start.11 = (bf16[1024,128]{1,0:T(8,128)(2,1)S(1)}, bf16[1024,128]{1,0:T(8,128)(2,1)S(1)}, u32[]{:S(2)}, u32[]{:S(2)}) collective-permute-start(bf16[1024,128]{1,0:T(8,128)(2,1)S(1)} %get-tuple-element.27), channel_id=1, source_target_pairs={{0,8},{8,0},{16,24},{24,16},{32,40},{40,32},{48,56},{56,48},{64,72... | collective-permute-start | bytes 786440 | tf_op jit(solution)/shard_map/ppermute | solution.py:41
  126.2 16.8 %collective-permute-start.10 = (bf16[1104,128]{1,0:T(8,128)(2,1)S(1)}, bf16[1104,128]{1,0:T(8,128)(2,1)S(1)}, u32[]{:S(2)}, u32[]{:S(2)}) collective-permute-start(bf16[1104,128]{1,0:T(8,128)(2,1)S(1)} %join.3), channel_id=1, source_target_pairs={{0,32},{8,40},{16,48},{24,56},{32,0},{40,8},{48,16},{56,24},{64,96... | collective-permute-start | bytes 847880 | tf_op jit(solution)/shard_map/ppermute | solution.py:41
  126.4 14.0 %collective-permute-start.14 = (bf16[1104,128]{1,0:T(8,128)(2,1)S(1)}, bf16[1104,128]{1,0:T(8,128)(2,1)S(1)}, u32[]{:S(2)}, u32[]{:S(2)}) collective-permute-start(bf16[1104,128]{1,0:T(8,128)(2,1)S(1)} %join.5), channel_id=1, source_target_pairs={{0,48},{8,56},{16,0},{24,8},{32,16},{40,24},{48,32},{56,40},{64,11... | collective-permute-start | bytes 847880 | tf_op jit(solution)/shard_map/ppermute | solution.py:41
  130.2 12.8 %collective-permute-start.12 = (bf16[1104,128]{1,0:T(8,128)(2,1)S(1)}, bf16[1104,128]{1,0:T(8,128)(2,1)S(1)}, u32[]{:S(2)}, u32[]{:S(2)}) collective-permute-start(bf16[1104,128]{1,0:T(8,128)(2,1)S(1)} %join.4), channel_id=1, source_target_pairs={{0,16},{8,24},{16,32},{24,40},{32,48},{40,56},{48,0},{56,8},{64,80... | collective-permute-start | bytes 847880 | tf_op jit(solution)/shard_map/ppermute | solution.py:41
  136.2 1.6 collective-permute-start.8
  143.2 7.4 %collective-permute-start.15 = (bf16[592,128]{1,0:T(8,128)(2,1)S(1)}, bf16[592,128]{1,0:T(8,128)(2,1)S(1)}, u32[]{:S(2)}, u32[]{:S(2)}) collective-permute-start(bf16[592,128]{1,0:T(8,128)(2,1)S(1)} %get-tuple-element.31), channel_id=1, source_target_pairs={{0,64},{8,72},{16,80},{24,88},{32,96},{40,104},{48,112},{56,120},{... | collective-permute-start | bytes 454664 | tf_op jit(solution)/shard_map/ppermute | solution.py:41
  152.1 13.0 %all-to-all-start.2 = ((f32[8,32,128]{2,1,0:T(8,128)}), f32[8,32,128]{2,1,0:T(8,128)S(1)}, u32[]{:S(2)}, u32[]{:S(2)}) async-start(f32[8,32,128]{2,1,0:T(8,128)} %broadcast_in_dim.2), calls=%async_computation.2 | async-start | bytes 262144 | tf_op jit(solution)/shard_map/all_to_all | solution.py:440

commit v2 on v0

v2 whole, which is shorter than its diff:
```python
import functools

import jax
import jax.numpy as jnp
from jax import lax
from jax.experimental import pallas as pl
from jax.experimental.pallas import tpu as pltpu
from jax.sharding import PartitionSpec as P

f32, bf16 = jnp.float32, jnp.bfloat16
T = 128
SLOTS = 32
NSRC = 4
NDST = 32
REP = 8
CH = 8
BIG, SMALL = 32, 8
DEG = 16
WROWS = 72
WX = 2 * WROWS
SMEM = pl.BlockSpec(memory_space=pltpu.SMEM)
VMEM = pl.BlockSpec(memory_space=pltpu.VMEM)
ANY = pl.BlockSpec(memory_space=pl.ANY)
HBM = pl.BlockSpec(memory_space=pltpu.HBM)


def params(mib=24):
    return pltpu.CompilerParams(vmem_limit_bytes=mib * 1024 * 1024)


def blk_at(dx, dz, dc):
    here = lax.axis_index("blk")
    x, z, c = here // 8, (here // 2) % 4, here % 2
    return (x + dx) % 2 * 8 + (z + dz) % 4 * 2 + (c + dc) % 2


def moved(value, dx, dz, dc):
    pairs = []
    for i in range(16):
        x, z, c = i // 8, (i // 2) % 4, i % 2
        pairs.append((i, (x + dx) % 2 * 8 + (z + dz) % 4 * 2 + (c + dc) % 2))
    return lax.ppermute(value, "blk", pairs)


def moved_y(value, dy):
    return lax.ppermute(value, "rep", [(i, (i // 2 + dy) % 4 * 2 + i % 2) for i in range(REP)])


def high_low(v):
    high = v.astype(bf16)
    return high, (v - high.astype(f32)).astype(bf16)


def walk(entries, base, count, group):
    def step(first, size):
        group([entries[first + u] for u in range(size)])
        return 0

    whole = count // BIG
    lax.fori_loop(0, whole, lambda g, _: step(base + g * BIG, BIG), 0)
    rest = (count - whole * BIG + SMALL - 1) // SMALL
    lax.fori_loop(0, rest, lambda g, _: step(base + whole * BIG + g * SMALL, SMALL), 0)


STEPS = (2, 1, 3, 0)
CAP = 8 * SLOTS + SMALL


def group_parts(dx):
    return [blk_at(dx, dz, dc) for dc in (0, 1) for dz in STEPS]


def slot_of(entry):
    return entry & 511


def column_of(entry):
    return (entry >> 5) & 127


def dest_of(entry):
    return entry >> 12


def make_plan(dests, srcs, counts, entries, totals):
    none = lax.axis_index("blk") * SLOTS + NSRC * 512 + NDST * 4096
    for dx in range(2):
        end = dx * CAP
        for p in group_parts(dx):

            def put(g, _, p=p, end=end):
                for u in range(8):
                    k = g * 8 + u
                    entries[end + k] = p * SLOTS + k + (srcs[0, 0, p, k] << 9) + (dests[0, 0, p, k] << 12)
                return 0

            count = counts[0, 0, p]
            lax.fori_loop(0, (count + 7) // 8, put, 0)
            end = end + count
        for u in range(SMALL):
            entries[end + u] = none
        totals[dx] = end - dx * CAP


def load_kernel(
    dests_in, srcs_in, counts_in, tiles, after, held, deg_out, entries, totals, acc, sem, dests, srcs, counts, small_sem
):
    pairs = ((counts_in, counts), (dests_in, dests), (srcs_in, srcs))
    small = [pltpu.make_async_copy(a, b, small_sem.at[i]) for i, (a, b) in enumerate(pairs)]
    for copy in small:
        copy.start()
    small[0].wait()

    def each_copy(p, act):
        def go(c, _):
            part = pl.ds(pl.multiple_of(p * SLOTS + c * CH, CH), CH)
            act(pltpu.make_async_copy(tiles.at[p, pl.ds(c * CH, CH)], held.at[part], sem.at[p, c]))
            return 0

        lax.fori_loop(0, (counts[0, 0, p] + CH - 1) // CH, go, 0)

    for p in range(16):
        each_copy(p, lambda copy: copy.start())
    small[1].wait()
    small[2].wait()
    make_plan(dests, srcs, counts, entries, totals)
    acc[...] = jnp.zeros_like(acc)

    def add(p, _):
        each_copy(p, lambda copy: copy.wait())
        count = counts[0, 0, p]

        def step(g, _):
            for u in range(SMALL):
                k = g * SMALL + u
                d = jnp.where(k < count, dests[0, 0, p, k], NDST)
                acc[d] += held[p * SLOTS + k].astype(f32)
            return 0

        lax.fori_loop(0, (count + SMALL - 1) // SMALL, step, 0)
        return 0

    lax.fori_loop(0, 16, add, 0)
    eye = lax.broadcasted_iota(jnp.int32, (T, T), 0) == lax.broadcasted_iota(jnp.int32, (T, T), 1)
    for d in range(NDST):
        column = jnp.sum(acc[d], axis=1, keepdims=True)
        deg_out[d : d + 1, :] = jnp.sum(jnp.where(eye, column, 0.0), axis=0, keepdims=True)


def load(dest_tile, src_tile, tile_count, tiles, after):
    return pl.pallas_call(
        load_kernel,
        name="load",
        out_shape=(
            jax.ShapeDtypeStruct((16 * SLOTS, T, T), bf16),
            jax.ShapeDtypeStruct((NDST, T), f32),
            jax.ShapeDtypeStruct((2 * CAP,), jnp.int32),
            jax.ShapeDtypeStruct((2,), jnp.int32),
        ),
        in_specs=[HBM] * 4 + [ANY],
        out_specs=(VMEM, VMEM, SMEM, SMEM),
        scratch_shapes=[
            pltpu.VMEM((NDST + 1, T, T), f32),
            pltpu.SemaphoreType.DMA((16, SLOTS // CH)),
            pltpu.SMEM(dest_tile.shape, jnp.int32),
            pltpu.SMEM(src_tile.shape, jnp.int32),
            pltpu.SMEM(tile_count.shape, jnp.int32),
            pltpu.SemaphoreType.DMA((3,)),
        ],
        compiler_params=params(),
        cost_estimate=pl.CostEstimate(flops=10**10, bytes_accessed=12 * 10**6, transcendentals=0),
    )(dest_tile, src_tile, tile_count, tiles, after)


def small_call(body, name, shapes, *operands, after=()):
    n = len(operands)
    return pl.pallas_call(
        lambda *refs: body(*refs[:n], *refs[n + len(after) :]),
        name=name,
        out_shape=shapes,
        in_specs=[VMEM] * n + [ANY] * len(after),
        out_specs=VMEM if isinstance(shapes, jax.ShapeDtypeStruct) else (VMEM,) * len(shapes),
        compiler_params=params(8),
    )(*operands, *after)


def glue(parts, after=()):
    def body(*refs):
        *parts, out = refs
        row = 0
        for part in parts:
            out[row : row + part.shape[0], :] = part[...]
            row += part.shape[0]

    shape = jax.ShapeDtypeStruct((sum(p.shape[0] for p in parts), T), bf16)
    return small_call(body, "glue", shape, *parts, after=after)


def forward_kernel(dx, after, entries, totals, tiles, mine, other, *refs):
    rows = NSRC * T
    if dx:
        acc_in, deg, out, acc, feat = refs
        acc[0:NDST] = acc_in[0:NDST]
    else:
        acc, feat = refs
        acc[...] = jnp.zeros_like(acc)
    for j, p in enumerate(group_parts(dx)):
        ref, first = (mine, other)[j // 4], j % 4 * rows
        for t in range(NSRC):
            feat[t * 16 + p] = ref[first + t * T : first + (t + 1) * T, :]

    def group(words):
        sums = [
            jnp.dot(tiles[slot_of(w)], feat[column_of(w)], preferred_element_type=f32) for w in words
        ]
        for w, s in zip(words, sums):
            acc[dest_of(w)] += s

    walk(entries, dx * CAP, totals[dx], group)
    if dx:
        for m in range(REP):
            out[m, 0:rows, :] = acc[m * NSRC : (m + 1) * NSRC].reshape(rows, T).astype(bf16)
            high, low = high_low(deg[m * NSRC : (m + 1) * NSRC, :])
            out[m, rows:, :] = jnp.concatenate(
                [high, low, jnp.zeros((DEG - 2 * NSRC, T), bf16)], axis=0
            )


def forward(dx, after, entries, totals, tiles, mine, other, *extra):
    rows = NSRC * T
    sums = (NDST + 1, T, T)
    if dx:
        shape = jax.ShapeDtypeStruct((REP, rows + DEG, T), bf16)
    else:
        shape = jax.ShapeDtypeStruct(sums, f32)
    return pl.pallas_call(
        functools.partial(forward_kernel, dx),
        name=f"forward_{dx}",
        out_shape=shape,
        in_specs=[ANY, SMEM, SMEM] + [VMEM] * (3 + len(extra)),
        out_specs=VMEM,
        scratch_shapes=([pltpu.VMEM(sums, f32)] if dx else []) + [pltpu.VMEM((80, T, T), bf16)],
        compiler_params=params(),
        cost_estimate=pl.CostEstimate(
            flops=4 * 10**9, bytes_accessed=8 * 17 * T * T * 2, transcendentals=0
        ),
    )(after, entries, totals, tiles, mine, other, *extra)


def dense_kernel(recv, features, cotangent, w_self, w_neigh, bias, act, payload, self_t):
    rows = NSRC * T
    total = recv[0, 0:rows, :].astype(f32)
    deg = jnp.zeros((NSRC, T), f32)
    for m in range(REP):
        if m:
            total += recv[m, 0:rows, :].astype(f32)
        extra = recv[m, rows:, :].astype(f32)
        deg += extra[0:NSRC] + extra[NSRC : 2 * NSRC]
    scale = lax.rsqrt(1.0 + deg)
    eye = lax.broadcasted_iota(jnp.int32, (T, T), 0) == lax.broadcasted_iota(jnp.int32, (T, T), 1)
    columns = [
        jnp.sum(jnp.where(eye, scale[i : i + 1, :], 0.0), axis=1, keepdims=True) for i in range(NSRC)
    ]
    mean = (total * jnp.concatenate(columns, axis=0)).astype(bf16)
    feat = features[...]
    pre = (
        jnp.dot(feat, w_self[...], preferred_element_type=f32)
        + jnp.dot(mean, w_neigh[...], preferred_element_type=f32)
        + bias[...]
    )
    sigma = jax.nn.sigmoid(pre)
    act[...] = (pre * sigma).astype(bf16)
    grad = (cotangent[...].astype(f32) * sigma * (1.0 + pre * (1.0 - sigma))).astype(bf16)
    down = (((0,), (0,)), ((), ()))
    across = (((1,), (1,)), ((), ()))
    g_self = lax.dot_general(feat, grad, down, preferred_element_type=f32)
    g_neigh = lax.dot_general(mean, grad, down, preferred_element_type=f32)
    g_bias = jnp.sum(grad.astype(f32), axis=0, keepdims=True)
    sum_t = lax.dot_general(w_neigh[...], grad, across, preferred_element_type=f32)
    own_t = lax.dot_general(w_self[...], grad, across, preferred_element_type=f32)
    spread = []
    for i in range(NSRC):
        part = slice(i * T, (i + 1) * T)
        spread.append((sum_t[:, part] * scale[i : i + 1, :]).astype(bf16))
        self_t[i] = own_t[:, part]
    bias_rows = jnp.broadcast_to(g_bias, (8, T))
    for m in range(REP):
        for i in range(NSRC):
            payload[m, i * T : (i + 1) * T, :] = spread[i]
        piece = slice(m // 2 * 32, (m // 2 + 1) * 32)
        segment = jnp.concatenate([g_self[piece], g_neigh[piece], bias_rows], axis=0)
        payload[m, rows:, :] = jnp.concatenate(high_low(segment), axis=0)


def dense(recv, features, cotangent, w_self, w_neigh, bias):
    rows = NSRC * T
    return pl.pallas_call(
        dense_kernel,
        name="dense",
        out_shape=(
            jax.ShapeDtypeStruct((rows, T), bf16),
            jax.ShapeDtypeStruct((REP, rows + WX, T), bf16),
            jax.ShapeDtypeStruct((NSRC, T, T), f32),
        ),
        in_specs=[VMEM] * 6,
        out_specs=(VMEM, VMEM, VMEM),
        compiler_params=params(),
    )(recv, features, cotangent, w_self, w_neigh, bias.reshape(1, T))


def segment_of(rows):
    wide = rows.astype(f32)
    return wide[0:WROWS] + wide[WROWS:]


def backward_kernel(entries, totals, tiles, recv, send, keep, acc):
    rows = NSRC * T
    parts = group_parts(1) + group_parts(0)
    acc[...] = jnp.zeros_like(acc)

    def group(words):
        sums = []
        for w in words:
            d = dest_of(w) & (NDST - 1)
            row = pl.multiple_of((d & (NSRC - 1)) << 7, T)
            sums.append(
                jnp.dot(recv[d >> 2, pl.ds(row, T), :], tiles[slot_of(w)], preferred_element_type=f32)
            )
        for w, s in zip(words, sums):
            acc[column_of(w)] += s

    for dx in (1, 0):
        walk(entries, dx * CAP, totals[dx], group)
    for j, p in enumerate(parts):
        first = (j // 8 * 4 + j % 4) * rows
        for t in range(NSRC):
            to = slice(first + t * T, first + (t + 1) * T)
            if j % 8 < 4:
                keep[to, :] = acc[t * 16 + p]
            else:
                send[to, :] = acc[t * 16 + p].astype(bf16)


def backward(entries, totals, tiles, recv):
    rows = NSRC * T
    return pl.pallas_call(
        backward_kernel,
        name="backward",
        out_shape=(
            jax.ShapeDtypeStruct((8 * rows, T), bf16),
            jax.ShapeDtypeStruct((8 * rows, T), f32),
        ),
        in_specs=[SMEM, SMEM, VMEM, VMEM],
        out_specs=(VMEM, VMEM),
        scratch_shapes=[pltpu.VMEM((80, T, T), f32)],
        compiler_params=params(),
        cost_estimate=pl.CostEstimate(
            flops=8 * 10**9, bytes_accessed=16 * 17 * T * T * 2, transcendentals=0
        ),
    )(entries, totals, tiles, recv)


def append(send, seg, seg_got):
    n = send.shape[0]

    def body(send, seg, got, out):
        out[0:n, :] = send[...]
        out[n:, :] = jnp.concatenate(high_low(segment_of(seg[...]) + segment_of(got[...])), axis=0)

    return small_call(body, "append", jax.ShapeDtypeStruct((n + WX, T), bf16), send, seg, seg_got)


def core_sums(keep, got, sent):
    rows = NSRC * T
    high = rows + WX

    def body(keep, got, sent, *out):
        for i, ref in enumerate(out):
            part = slice(i * rows, (i + 1) * rows)
            value = keep[part, :] + got[part, :].astype(f32)
            ref[0:rows, :] = value.astype(ref.dtype)
        total = segment_of(got[8 * rows :, :]) + segment_of(sent[8 * rows :, :])
        total = jnp.concatenate(high_low(total), axis=0)
        for ref in out[0:3]:
            ref[rows:, :] = total

    shapes = [jax.ShapeDtypeStruct((high, T), bf16)] * 3 + [jax.ShapeDtypeStruct((rows, T), f32)]
    shapes += [jax.ShapeDtypeStruct((rows, T), bf16)] * 3 + [jax.ShapeDtypeStruct((rows, T), f32)]
    return small_call(body, "core_sums", tuple(shapes), keep, got, sent)


def member_segments(spread):
    rows = NSRC * T

    def body(spread, out):
        total = segment_of(spread[0, rows:, :])
        for m in range(1, REP):
            total += segment_of(spread[m, rows:, :])
        out[...] = jnp.concatenate(high_low(total), axis=0)

    return small_call(body, "member_segments", jax.ShapeDtypeStruct((WX, T), bf16), spread)


def z_sum(near, *parts):
    rows = NSRC * T

    def body(near, a, b, c, far):
        block = near[...]
        for ref in (a, b, c):
            block += ref[0:rows, :].astype(f32)
        far[...] = block.astype(bf16)

    return small_call(body, "z_sum", jax.ShapeDtypeStruct((rows, T), bf16), near, *parts)


def z_segments(own, *parts, after):
    rows = NSRC * T

    def body(own, a, b, c, pieces, bias):
        total = segment_of(own[rows:, :])
        for ref in (a, b, c):
            total += segment_of(ref[rows:, :])
        pieces[...] = total[0:64]
        bias[...] = total[64:65]

    shapes = (jax.ShapeDtypeStruct((64, T), f32), jax.ShapeDtypeStruct((1, T), f32))
    return small_call(body, "z_segments", shapes, own, *parts, after=after)


def final(pieces, near, self_t, *others):
    rows = NSRC * T

    def body(p0, p1, p2, p3, near, self_t, *refs):
        *others, out, w_self, w_neigh = refs
        for i in range(NSRC):
            part = slice(i * T, (i + 1) * T)
            block = near[part, :] + self_t[i]
            for other in others:
                block += other[part, :].astype(f32)
            out[part, :] = block.T
        y = lax.axis_index("rep") // 2
        for back, piece in enumerate((p0, p1, p2, p3)):
            to = pl.ds(pl.multiple_of((y - back) % 4 * 32, 32), 32)
            w_self[to, :] = piece[0:32]
            w_neigh[to, :] = piece[32:64]

    shapes = (jax.ShapeDtypeStruct((rows, T), f32),) + (jax.ShapeDtypeStruct((T, T), f32),) * 2
    return small_call(body, "final", shapes, *pieces, near, self_t, *others)


def shards(
    features, cotangent, w_self, w_neigh, out_bias, tile_values, dest_tile, src_tile, tile_count
):
    rows = NSRC * T

    opposite = glue([moved(features, 1, 0, 0)])
    near = glue([moved(features, 0, -dz, 0) if dz else features for dz in STEPS])
    far = [moved(opposite, 0, -dz, 0) if dz else opposite for dz in STEPS]
    tiles, deg, entries, totals = load(dest_tile, src_tile, tile_count, tile_values[0, 0], near)
    far = glue(far, (deg,))
    acc = forward(0, far, entries, totals, tiles, near, moved(near, 0, 0, 1))
    sums = forward(1, acc, entries, totals, tiles, far, moved(far, 0, 0, 1), acc, deg)
    recv = lax.all_to_all(sums, "rep", 0, 0)

    act, payload, self_t = dense(recv, features, cotangent, w_self, w_neigh, out_bias)
    spread = lax.all_to_all(payload, "rep", 0, 0)

    seg = member_segments(spread)
    seg_got = moved(seg, 1, 0, 0)
    send, keep = backward(entries, totals, tiles, spread)
    send = append(send, seg, seg_got)
    out = core_sums(keep, moved(send, 0, 0, 1), send)
    far_out, far_block, near_out, near_block = out[0:3], out[3], out[4:7], out[7]
    far_parts = [moved(v, 0, dz, 0) for v, dz in zip(far_out, STEPS)]
    near_parts = [moved(v, 0, dz, 0) for v, dz in zip(near_out, STEPS)]
    far = z_sum(far_block, *far_parts)
    pieces, bias = z_segments(far_out[0], *far_parts, after=(far,))
    pieces = [pieces] + [moved_y(pieces, dy) for dy in (1, 2, 3)]
    grad_features, grad_w_self, grad_w_neigh = final(
        pieces, near_block, self_t, moved(far, 1, 0, 0), *near_parts
    )
    return (act, grad_features, grad_w_self, grad_w_neigh, bias.reshape(T))


def solution(mesh):
    placed = (
        P(("blk", "rep"), None),
        P(("blk", "rep"), None),
        P(),
        P(),
        P(),
        P("blk", "rep", None, None, None, None),
        P("blk", "rep", None, None),
        P("blk", "rep", None, None),
        P("blk", "rep", None),
    )
    return jax.shard_map(
        shards,
        mesh=mesh,
        in_specs=placed,
        out_specs=(P(("blk", "rep"), None), P(("blk", "rep"), None), P(), P(), P()),
        check_vma=False,
    )
```

time: 811 us -> 117 us (0.14)
  waiting for transfers between devices: 242 us -> 17 us
  other arithmetic: 197 us -> 0 us
  matrix products: 87 us -> 0 us
  local copies, waits for them, and re-layouts: 80.9 us -> 2.98 us
  blocking collectives: 100 us -> 44.1 us
  starting transfers between devices: 79.5 us -> 28.8 us
  Pallas kernels: 0 us -> 23.4 us
  between operations: 14.6 us -> 0.84 us
    scatter-add x48 -> x0, other arithmetic: 153 us -> none  [the longest x16 98 us: forward_terms(): new_sums = totals[0].at[dests].add(products * live[:, None, None])]
    ppermute x30 -> x21, waiting for transfers between devices: 113 us -> 17 us  [the longest x18 13 us: moved(): return lax.ppermute(value, 'blk', pairs)]
    dot_general x54 -> x0, matrix products: 87 us -> none  [the longest x16 28.4 us: backward_terms(): jnp.einsum('knm,knf->kmf', values, picked, preferred_element_type=jnp.flo...]
    psum x1 -> x0, waiting for transfers between devices: 75.9 us -> none  [shards(): lax.psum((local_self, local_neigh, local_bias), ('blk', 'rep'))]
    psum x1 -> x0, blocking collectives: 64.8 us -> none  [shards(): lax.psum((local_self, local_neigh, local_bias), ('blk', 'rep'))]
    ppermute x30 -> x21, starting transfers between devices: 79.4 us -> 28.8 us  [the longest x18 24.9 us: moved(): return lax.ppermute(value, 'blk', pairs)]
    gather x32 -> x0, local copies, waits for them, and re-layouts: 44.4 us -> none  [the longest x16 31.6 us: backward_terms(): picked = spread[dests]]
    all_to_all x0 -> x2, blocking collectives: none -> 44.1 us  [the longest x1 22.4 us: shards(): recv = lax.all_to_all(sums, 'rep', 0, 0)]
  transfers between devices with their start and end apart: 33 -> 21, of which waited for: 33 -> 7; matrix products, arithmetic and copies ran while one was open for 9% -> 0% of each run, Pallas kernels for 0% -> 15%
where the time goes in v2:
time: 117 us
  blocking collectives  44.1 us (38%)
  starting transfers between devices  28.8 us (25%)
  Pallas kernels  23.4 us (20%)
  waiting for transfers between devices  17 us (15%)
  local copies, waits for them, and re-layouts  2.98 us (3%)
    ppermute x18, starting transfers between devices, moved(): return lax.ppermute(value, 'blk', pairs)  24.9 us
    all_to_all x1, blocking collectives, shards(): recv = lax.all_to_all(sums, 'rep', 0, 0)  22.4 us
    all_to_all x1, blocking collectives, shards(): spread = lax.all_to_all(payload, 'rep', 0, 0)  21.7 us
    ppermute x18, waiting for transfers between devices, moved(): return lax.ppermute(value, 'blk', pairs)  13 us
    pallas_call x1, Pallas kernels, load(): pl.pallas_call(load_kernel, name='load', out_shape=(jax.ShapeDtypeStruct(...  7.44 us
    pallas_call x2, Pallas kernels, forward(): pl.pallas_call(functools.partial(forward_kernel, dx), name=f'forward_{dx}...  6.71 us
    pallas_call x1, Pallas kernels, backward(): pl.pallas_call(backward_kernel, name='backward', out_shape=(jax.ShapeDtyp...  6.11 us
    ppermute x3, waiting for transfers between devices, moved_y(): lax.ppermute(value, 'rep', [(i, (i // 2 + dy) % 4 * 2 + i % 2) for i in r...  4.08 us
  transfers between devices with their start and end apart: 21, of which 7 were waited for; matrix products, arithmetic and copies ran while one was open for 0% of the time, Pallas kernels for 15%

profile of v2, /device:TPU:0, one launch (start us, length us, event | category | flops | bytes accessed | tf_op | source)
XLA Modules:
  0.0 117.1 jit_solution(18427381276481935786)
XLA Ops:
  0.6 3.2 %collective-permute-start = (bf16[512,128]{1,0:T(8,128)(2,1)}, bf16[512,128]{1,0:T(8,128)(2,1)S(1)}, u32[]{:S(2)}, u32[]{:S(2)}) collective-permute-start(bf16[512,128]{1,0:T(8,128)(2,1)} %features.1), channel_id=1, source_target_pairs={{0,64},{8,72},{16,80},{24,88},{32,96},{40,104},{48,112},{56,120},{... | collective-permute-start | bytes 393224 | tf_op jit(solution)/shard_map/ppermute | solution.py:42
  3.8 1.9 %collective-permute-start.6 = (bf16[512,128]{1,0:T(8,128)(2,1)}, bf16[512,128]{1,0:T(8,128)(2,1)S(1)}, u32[]{:S(2)}, u32[]{:S(2)}) collective-permute-start(bf16[512,128]{1,0:T(8,128)(2,1)} %features.1), channel_id=1, source_target_pairs={{0,16},{8,24},{16,32},{24,40},{32,48},{40,56},{48,0},{56,8},{64,80... | collective-permute-start | bytes 393224 | tf_op jit(solution)/shard_map/ppermute | solution.py:42
  5.7 2.1 %collective-permute-start.5 = (bf16[512,128]{1,0:T(8,128)(2,1)}, bf16[512,128]{1,0:T(8,128)(2,1)S(1)}, u32[]{:S(2)}, u32[]{:S(2)}) collective-permute-start(bf16[512,128]{1,0:T(8,128)(2,1)} %features.1), channel_id=1, source_target_pairs={{0,48},{8,56},{16,0},{24,8},{32,16},{40,24},{48,32},{56,40},{64,11... | collective-permute-start | bytes 393224 | tf_op jit(solution)/shard_map/ppermute | solution.py:42
  7.9 1.9 %collective-permute-start.4 = (bf16[512,128]{1,0:T(8,128)(2,1)}, bf16[512,128]{1,0:T(8,128)(2,1)S(1)}, u32[]{:S(2)}, u32[]{:S(2)}) collective-permute-start(bf16[512,128]{1,0:T(8,128)(2,1)} %features.1), channel_id=1, source_target_pairs={{0,32},{8,40},{16,48},{24,56},{32,0},{40,8},{48,16},{56,24},{64,96... | collective-permute-start | bytes 393224 | tf_op jit(solution)/shard_map/ppermute | solution.py:42
  9.7 1.1 collective-permute-start.3
  10.8 2.2 %collective-permute-start.2 = (bf16[512,128]{1,0:T(8,128)(2,1)S(1)}, bf16[512,128]{1,0:T(8,128)(2,1)S(1)}, u32[]{:S(2)}, u32[]{:S(2)}) collective-permute-start(bf16[512,128]{1,0:T(8,128)(2,1)S(1)} %glue.3.refs_3_), channel_id=1, source_target_pairs={{0,48},{8,56},{16,0},{24,8},{32,16},{40,24},{48,32},{56,40},{64,11... | collective-permute-start | bytes 393224 | tf_op jit(solution)/shard_map/ppermute | solution.py:42
  13.0 0.7 collective-permute-start.1
  13.7 2.7 %collective-permute-done.4.refs_0_ = bf16[512,128]{1,0:T(8,128)(2,1)S(1)} collective-permute-done((bf16[512,128]{1,0:T(8,128)(2,1)}, bf16[512,128]{1,0:T(8,128)(2,1)S(1)}, u32[]{:S(2)}, u32[]{:S(2)}) %collective-permute-start.4) | collective-permute-done | bytes 131104 | tf_op jit(solution)/shard_map/ppermute | solution.py:42
  16.4 0.9 copy-done
  17.4 0.7 copy-done.6
  18.1 0.7 copy-done.7
  18.8 0.7 copy-done.8
  19.5 7.4 %load.1 = (bf16[512,128,128]{2,1,0:T(8,128)(2,1)S(1)}, f32[32,128]{1,0:T(8,128)S(1)}, s32[528]{0:T(1024)S(1)}, s32[2]{0:T(128)S(1)}) custom-call(s32[1,1,16,32]{3,2,1,0:T(8,128)S(1)} %copy-done.6, s32[1,1,16,32]{3,2,1,0:T(8,128)S(1)} %copy-done.7, s32[1,1,16]{2,1,0:T(1,128)S(1)} %copy-done.8, bf16[16,32,128,128]{3,2,1,0:T(8,128)(2,1)} %bitcast.4, ...), custom_call_target="tpu_custom_call" | custom-call | flops 10000000000 | bytes 12000000 | tf_op jit(solution)/shard_map/load/pallas_call | solution.py:151
  27.0 1.2 %collective-permute-start.8 = (bf16[2048,128]{1,0:T(8,128)(2,1)S(1)}, bf16[2048,128]{1,0:T(8,128)(2,1)S(1)}, u32[]{:S(2)}, u32[]{:S(2)}) collective-permute-start(bf16[2048,128]{1,0:T(8,128)(2,1)S(1)} %glue.5.after.mine), channel_id=1, source_target_pairs={{0,8},{8,0},{16,24},{24,16},{32,40},{40,32},{48,56},{56,48},{64,72... | collective-permute-start | bytes 1572872 | tf_op jit(solution)/shard_map/ppermute | solution.py:42
  28.2 3.3 %forward_0.1.after.refs_0_ = f32[33,128,128]{2,1,0:T(8,128)S(1)} custom-call(bf16[2048,128]{1,0:T(8,128)(2,1)S(1)} %glue.5.after.mine, s32[528]{0:T(1024)S(1)} %get-tuple-element.28.entries, s32[2]{0:T(128)S(1)} %get-tuple-element.29.totals, bf16[512,128,128]{2,1,0:T(8,128)(2,1)S(1)} %get-tuple-element.30.tiles, bf16[2048,128]{1,0:T(8,128)(2,1)S(1)} %glue.4.after.mine, ...), custom_call_target="tpu_custom_call" | custom-call | flops 4000000000 | bytes 4456448 | tf_op jit(solution)/shard_map/forward_0/pallas_call | solution.py:236
  31.5 3.4 %forward_1.1 = bf16[8,528,128]{2,1,0:T(8,128)(2,1)S(1)} custom-call(f32[33,128,128]{2,1,0:T(8,128)S(1)} %forward_0.1.after.refs_0_, s32[528]{0:T(1024)S(1)} %get-tuple-element.28.entries, s32[2]{0:T(128)S(1)} %get-tuple-element.29.totals, bf16[512,128,128]{2,1,0:T(8,128)(2,1)S(1)} %get-tuple-element.30.tiles, bf16[2048,128]{1,0:T(8,128)(2,1)S(1)} %glue.5.after.mine, ...), custom_call_target="tpu_custom_call" | custom-call | flops 4000000000 | bytes 4456448 | tf_op jit(solution)/shard_map/forward_1/pallas_call | solution.py:236
  35.0 22.4 %all_to_all.10.recv = bf16[8,528,128]{2,1,0:T(8,128)(2,1)S(1)} all-to-all(bf16[8,528,128]{2,1,0:T(8,128)(2,1)S(1)} %forward_1.1), channel_id=1, replica_groups=mesh['blk'=16,'rep'=8] {'rep'}, dimensions={0} | all-to-all | bytes 2162688 | tf_op jit(solution)/shard_map/all_to_all | solution.py:463
  57.5 1.2 %dense.1 = (bf16[512,128]{1,0:T(8,128)(2,1)}, bf16[8,656,128]{2,1,0:T(8,128)(2,1)S(1)}, f32[4,128,128]{2,1,0:T(8,128)S(1)}) custom-call(bf16[8,528,128]{2,1,0:T(8,128)(2,1)S(1)} %all_to_all.10.recv, bf16[512,128]{1,0:T(8,128)(2,1)S(1)} %copy-done.1, bf16[512,128]{1,0:T(8,128)(2,1)S(1)} %copy-done.2, bf16[128,128]{1,0:T(8,128)(2,1)S(1)} %copy-done.3, ...), custom_call_target="tpu_custom_call" | custom-call | tf_op jit(solution)/shard_map/dense/pallas_call | solution.py:297
  58.7 21.7 %all_to_all.11.recv.refs_0_ = bf16[8,656,128]{2,1,0:T(8,128)(2,1)S(1)} all-to-all(bf16[8,656,128]{2,1,0:T(8,128)(2,1)S(1)} %get-tuple-element.32), channel_id=1, replica_groups=mesh['blk'=16,'rep'=8] {'rep'}, dimensions={0} | all-to-all | bytes 2686976 | tf_op jit(solution)/shard_map/all_to_all | solution.py:466
  80.5 6.1 %backward.1 = (bf16[4096,128]{1,0:T(8,128)(2,1)S(1)}, f32[4096,128]{1,0:T(8,128)S(1)}) custom-call(s32[528]{0:T(1024)S(1)} %get-tuple-element.28.entries, s32[2]{0:T(128)S(1)} %get-tuple-element.29.totals, bf16[512,128,128]{2,1,0:T(8,128)(2,1)S(1)} %get-tuple-element.30.tiles, bf16[8,656,128]{2,1,0:T(8,128)(2,1)S(1)} %all_to_all.11.recv.refs_0_), custom_call_target="tpu_custom_call" | custom-call | flops 8000000000 | bytes 8912896 | tf_op jit(solution)/shard_map/backward/pallas_call | solution.py:346
  86.8 2.7 %collective-permute-done.10.refs_1_ = bf16[4240,128]{1,0:T(8,128)(2,1)S(1)} collective-permute-done((bf16[4240,128]{1,0:T(8,128)(2,1)S(1)}, bf16[4240,128]{1,0:T(8,128)(2,1)S(1)}, u32[]{:S(2)}, u32[]{:S(2)}) %collective-permute-start.10) | collective-permute-done | bytes 1085472 | tf_op jit(solution)/shard_map/ppermute | solution.py:42
  90.1 3.0 %collective-permute-start.13 = (bf16[656,128]{1,0:T(8,128)(2,1)S(1)}, bf16[656,128]{1,0:T(8,128)(2,1)S(1)}, u32[]{:S(2)}, u32[]{:S(2)}) collective-permute-start(bf16[656,128]{1,0:T(8,128)(2,1)S(1)} %get-tuple-element.37), channel_id=1, source_target_pairs={{0,48},{8,56},{16,0},{24,8},{32,16},{40,24},{48,32},{56,40},{64,11... | collective-permute-start | bytes 503816 | tf_op jit(solution)/shard_map/ppermute | solution.py:42
  93.0 3.5 %collective-permute-start.18 = (bf16[512,128]{1,0:T(8,128)(2,1)S(1)}, bf16[512,128]{1,0:T(8,128)(2,1)S(1)}, u32[]{:S(2)}, u32[]{:S(2)}) collective-permute-start(bf16[512,128]{1,0:T(8,128)(2,1)S(1)} %get-tuple-element.42), channel_id=1, source_target_pairs={{0,32},{8,40},{16,48},{24,56},{32,0},{40,8},{48,16},{56,24},{64,96... | collective-permute-start | bytes 393224 | tf_op jit(solution)/shard_map/ppermute | solution.py:42
  96.6 7.3 %collective-permute-done.12.refs_2_ = bf16[656,128]{1,0:T(8,128)(2,1)S(1)} collective-permute-done((bf16[656,128]{1,0:T(8,128)(2,1)S(1)}, bf16[656,128]{1,0:T(8,128)(2,1)S(1)}, u32[]{:S(2)}, u32[]{:S(2)}) %collective-permute-start.12) | collective-permute-done | bytes 167968 | tf_op jit(solution)/shard_map/ppermute | solution.py:42
  104.2 3.5 %collective-permute-start.17 = (bf16[512,128]{1,0:T(8,128)(2,1)S(1)}, bf16[512,128]{1,0:T(8,128)(2,1)S(1)}, u32[]{:S(2)}, u32[]{:S(2)}) collective-permute-start(bf16[512,128]{1,0:T(8,128)(2,1)S(1)} %z_sum.1.refs_4_), channel_id=1, source_target_pairs={{0,64},{8,72},{16,80},{24,88},{32,96},{40,104},{48,112},{56,120},{... | collective-permute-start | bytes 393224 | tf_op jit(solution)/shard_map/ppermute | solution.py:42
  107.8 0.5 z_segments.1
  108.3 0.5 collective-permute-start.16
  108.8 2.3 %collective-permute-start.15 = (f32[64,128]{1,0:T(8,128)S(1)}, f32[64,128]{1,0:T(8,128)S(1)}, u32[]{:S(2)}, u32[]{:S(2)}) collective-permute-start(f32[64,128]{1,0:T(8,128)S(1)} %get-tuple-element.39.refs_0_), channel_id=1, source_target_pairs={{0,4},{1,5},{2,6},{3,7},{4,0},{5,1},{6,2},{7,3},{8,12},{9,13},{10,... | collective-permute-start | bytes 98312 | tf_op jit(solution)/shard_map/ppermute | solution.py:46
  111.1 1.0 collective-permute-start.14
  112.2 2.0 %collective-permute-done.15.refs_2_ = f32[64,128]{1,0:T(8,128)S(1)} collective-permute-done((f32[64,128]{1,0:T(8,128)S(1)}, f32[64,128]{1,0:T(8,128)S(1)}, u32[]{:S(2)}, u32[]{:S(2)}) %collective-permute-start.15) | collective-permute-done | bytes 32800 | tf_op jit(solution)/shard_map/ppermute | solution.py:46
  114.2 2.0 %collective-permute-done.14.refs_1_ = f32[64,128]{1,0:T(8,128)S(1)} collective-permute-done((f32[64,128]{1,0:T(8,128)S(1)}, f32[64,128]{1,0:T(8,128)S(1)}, u32[]{:S(2)}, u32[]{:S(2)}) %collective-permute-start.14) | collective-permute-done | bytes 32800 | tf_op jit(solution)/shard_map/ppermute | solution.py:46
  116.2 0.9 final.1
  (44 shorter events, 1.6 us)
Async XLA Ops:
  0.6 9.1 %collective-permute-start = (bf16[512,128]{1,0:T(8,128)(2,1)}, bf16[512,128]{1,0:T(8,128)(2,1)S(1)}, u32[]{:S(2)}, u32[]{:S(2)}) collective-permute-start(bf16[512,128]{1,0:T(8,128)(2,1)} %features.1), channel_id=1, source_target_pairs={{0,64},{8,72},{16,80},{24,88},{32,96},{40,104},{48,112},{56,120},{... | collective-permute-start | bytes 393224 | tf_op jit(solution)/shard_map/ppermute | solution.py:42
  3.8 9.2 %collective-permute-start.6 = (bf16[512,128]{1,0:T(8,128)(2,1)}, bf16[512,128]{1,0:T(8,128)(2,1)S(1)}, u32[]{:S(2)}, u32[]{:S(2)}) collective-permute-start(bf16[512,128]{1,0:T(8,128)(2,1)} %features.1), channel_id=1, source_target_pairs={{0,16},{8,24},{16,32},{24,40},{32,48},{40,56},{48,0},{56,8},{64,80... | collective-permute-start | bytes 393224 | tf_op jit(solution)/shard_map/ppermute | solution.py:42
  5.7 8.0 %collective-permute-start.5 = (bf16[512,128]{1,0:T(8,128)(2,1)}, bf16[512,128]{1,0:T(8,128)(2,1)S(1)}, u32[]{:S(2)}, u32[]{:S(2)}) collective-permute-start(bf16[512,128]{1,0:T(8,128)(2,1)} %features.1), channel_id=1, source_target_pairs={{0,48},{8,56},{16,0},{24,8},{32,16},{40,24},{48,32},{56,40},{64,11... | collective-permute-start | bytes 393224 | tf_op jit(solution)/shard_map/ppermute | solution.py:42
  7.9 8.5 %collective-permute-start.4 = (bf16[512,128]{1,0:T(8,128)(2,1)}, bf16[512,128]{1,0:T(8,128)(2,1)S(1)}, u32[]{:S(2)}, u32[]{:S(2)}) collective-permute-start(bf16[512,128]{1,0:T(8,128)(2,1)} %features.1), channel_id=1, source_target_pairs={{0,32},{8,40},{16,48},{24,56},{32,0},{40,8},{48,16},{56,24},{64,96... | collective-permute-start | bytes 393224 | tf_op jit(solution)/shard_map/ppermute | solution.py:42
  9.7 17.2 %collective-permute-start.3 = (bf16[512,128]{1,0:T(8,128)(2,1)S(1)}, bf16[512,128]{1,0:T(8,128)(2,1)S(1)}, u32[]{:S(2)}, u32[]{:S(2)}) collective-permute-start(bf16[512,128]{1,0:T(8,128)(2,1)S(1)} %glue.3.refs_3_), channel_id=1, source_target_pairs={{0,16},{8,24},{16,32},{24,40},{32,48},{40,56},{48,0},{56,8},{64,80... | collective-permute-start | bytes 393224 | tf_op jit(solution)/shard_map/ppermute | solution.py:42
  10.8 16.1 %collective-permute-start.2 = (bf16[512,128]{1,0:T(8,128)(2,1)S(1)}, bf16[512,128]{1,0:T(8,128)(2,1)S(1)}, u32[]{:S(2)}, u32[]{:S(2)}) collective-permute-start(bf16[512,128]{1,0:T(8,128)(2,1)S(1)} %glue.3.refs_3_), channel_id=1, source_target_pairs={{0,48},{8,56},{16,0},{24,8},{32,16},{40,24},{48,32},{56,40},{64,11... | collective-permute-start | bytes 393224 | tf_op jit(solution)/shard_map/ppermute | solution.py:42
  13.0 13.9 %collective-permute-start.1 = (bf16[512,128]{1,0:T(8,128)(2,1)S(1)}, bf16[512,128]{1,0:T(8,128)(2,1)S(1)}, u32[]{:S(2)}, u32[]{:S(2)}) collective-permute-start(bf16[512,128]{1,0:T(8,128)(2,1)S(1)} %glue.3.refs_3_), channel_id=1, source_target_pairs={{0,32},{8,40},{16,48},{24,56},{32,0},{40,8},{48,16},{56,24},{64,96... | collective-permute-start | bytes 393224 | tf_op jit(solution)/shard_map/ppermute | solution.py:42
  16.4 0.9 copy-start
  17.3 10.9 %collective-permute-start.7 = (bf16[2048,128]{1,0:T(8,128)(2,1)S(1)}, bf16[2048,128]{1,0:T(8,128)(2,1)S(1)}, u32[]{:S(2)}, u32[]{:S(2)}) collective-permute-start(bf16[2048,128]{1,0:T(8,128)(2,1)S(1)} %glue.4.after.mine), channel_id=1, source_target_pairs={{0,8},{8,0},{16,24},{24,16},{32,40},{40,32},{48,56},{56,48},{64,72... | collective-permute-start | bytes 1572872 | tf_op jit(solution)/shard_map/ppermute | solution.py:42
  17.4 0.7 copy-start.6
  18.1 0.7 copy-start.7
  18.8 0.7 copy-start.8
  27.0 4.5 %collective-permute-start.8 = (bf16[2048,128]{1,0:T(8,128)(2,1)S(1)}, bf16[2048,128]{1,0:T(8,128)(2,1)S(1)}, u32[]{:S(2)}, u32[]{:S(2)}) collective-permute-start(bf16[2048,128]{1,0:T(8,128)(2,1)S(1)} %glue.5.after.mine), channel_id=1, source_target_pairs={{0,8},{8,0},{16,24},{24,16},{32,40},{40,32},{48,56},{56,48},{64,72... | collective-permute-start | bytes 1572872 | tf_op jit(solution)/shard_map/ppermute | solution.py:42
  34.9 22.5 %copy-start.1 = (bf16[512,128]{1,0:T(8,128)(2,1)S(1)}, bf16[512,128]{1,0:T(8,128)(2,1)}, u32[]{:S(2)}) copy-start(bf16[512,128]{1,0:T(8,128)(2,1)} %features.1) | copy-start | bytes 393220
  34.9 22.5 %copy-start.2 = (bf16[512,128]{1,0:T(8,128)(2,1)S(1)}, bf16[512,128]{1,0:T(8,128)(2,1)}, u32[]{:S(2)}) copy-start(bf16[512,128]{1,0:T(8,128)(2,1)} %cotangent.1) | copy-start | bytes 393220
  35.0 22.5 %copy-start.3 = (bf16[128,128]{1,0:T(8,128)(2,1)S(1)}, bf16[128,128]{1,0:T(8,128)(2,1)}, u32[]{:S(2)}) copy-start(bf16[128,128]{1,0:T(8,128)(2,1)} %w_self.1) | copy-start | bytes 98308
  35.0 22.5 %copy-start.4 = (bf16[128,128]{1,0:T(8,128)(2,1)S(1)}, bf16[128,128]{1,0:T(8,128)(2,1)}, u32[]{:S(2)}) copy-start(bf16[128,128]{1,0:T(8,128)(2,1)} %w_neigh.1) | copy-start | bytes 98308
  35.0 22.5 %copy-start.5 = (f32[128]{0:T(128)S(1)}, f32[128]{0:T(128)}, u32[]{:S(2)}) copy-start(f32[128]{0:T(128)} %param.13) | copy-start | bytes 1540
  80.4 6.2 %collective-permute-start.9 = (bf16[144,128]{1,0:T(8,128)(2,1)S(1)}, bf16[144,128]{1,0:T(8,128)(2,1)S(1)}, u32[]{:S(2)}, u32[]{:S(2)}) collective-permute-start(bf16[144,128]{1,0:T(8,128)(2,1)S(1)} %member_segments.1.refs_1_), channel_id=1, source_target_pairs={{0,64},{8,72},{16,80},{24,88},{32,96},{40,104},{48,112},{56,120},{... | collective-permute-start | bytes 110600 | tf_op jit(solution)/shard_map/ppermute | solution.py:42
  86.7 2.8 %collective-permute-start.10 = (bf16[4240,128]{1,0:T(8,128)(2,1)S(1)}, bf16[4240,128]{1,0:T(8,128)(2,1)S(1)}, u32[]{:S(2)}, u32[]{:S(2)}) collective-permute-start(bf16[4240,128]{1,0:T(8,128)(2,1)S(1)} %append.1.refs_2_), channel_id=1, source_target_pairs={{0,8},{8,0},{16,24},{24,16},{32,40},{40,32},{48,56},{56,48},{64,72... | collective-permute-start | bytes 3256328 | tf_op jit(solution)/shard_map/ppermute | solution.py:42
  89.7 14.1 %collective-permute-start.12 = (bf16[656,128]{1,0:T(8,128)(2,1)S(1)}, bf16[656,128]{1,0:T(8,128)(2,1)S(1)}, u32[]{:S(2)}, u32[]{:S(2)}) collective-permute-start(bf16[656,128]{1,0:T(8,128)(2,1)S(1)} %get-tuple-element.36), channel_id=1, source_target_pairs={{0,16},{8,24},{16,32},{24,40},{32,48},{40,56},{48,0},{56,8},{64,80... | collective-permute-start | bytes 503816 | tf_op jit(solution)/shard_map/ppermute | solution.py:42
  90.1 14.1 %collective-permute-start.13 = (bf16[656,128]{1,0:T(8,128)(2,1)S(1)}, bf16[656,128]{1,0:T(8,128)(2,1)S(1)}, u32[]{:S(2)}, u32[]{:S(2)}) collective-permute-start(bf16[656,128]{1,0:T(8,128)(2,1)S(1)} %get-tuple-element.37), channel_id=1, source_target_pairs={{0,48},{8,56},{16,0},{24,8},{32,16},{40,24},{48,32},{56,40},{64,11... | collective-permute-start | bytes 503816 | tf_op jit(solution)/shard_map/ppermute | solution.py:42
  93.0 11.1 %collective-permute-start.11 = (bf16[656,128]{1,0:T(8,128)(2,1)S(1)}, bf16[656,128]{1,0:T(8,128)(2,1)S(1)}, u32[]{:S(2)}, u32[]{:S(2)}) collective-permute-start(bf16[656,128]{1,0:T(8,128)(2,1)S(1)} %get-tuple-element.35.refs_0_), channel_id=1, source_target_pairs={{0,32},{8,40},{16,48},{24,56},{32,0},{40,8},{48,16},{56,24},{64,96... | collective-permute-start | bytes 503816 | tf_op jit(solution)/shard_map/ppermute | solution.py:42
  93.0 15.8 %collective-permute-start.18 = (bf16[512,128]{1,0:T(8,128)(2,1)S(1)}, bf16[512,128]{1,0:T(8,128)(2,1)S(1)}, u32[]{:S(2)}, u32[]{:S(2)}) collective-permute-start(bf16[512,128]{1,0:T(8,128)(2,1)S(1)} %get-tuple-element.42), channel_id=1, source_target_pairs={{0,32},{8,40},{16,48},{24,56},{32,0},{40,8},{48,16},{56,24},{64,96... | collective-permute-start | bytes 393224 | tf_op jit(solution)/shard_map/ppermute | solution.py:42
  96.6 14.5 %collective-permute-start.19 = (bf16[512,128]{1,0:T(8,128)(2,1)S(1)}, bf16[512,128]{1,0:T(8,128)(2,1)S(1)}, u32[]{:S(2)}, u32[]{:S(2)}) collective-permute-start(bf16[512,128]{1,0:T(8,128)(2,1)S(1)} %get-tuple-element.43), channel_id=1, source_target_pairs={{0,16},{8,24},{16,32},{24,40},{32,48},{40,56},{48,0},{56,8},{64,80... | collective-permute-start | bytes 393224 | tf_op jit(solution)/shard_map/ppermute | solution.py:42
  103.8 8.3 %collective-permute-start.20 = (bf16[512,128]{1,0:T(8,128)(2,1)S(1)}, bf16[512,128]{1,0:T(8,128)(2,1)S(1)}, u32[]{:S(2)}, u32[]{:S(2)}) collective-permute-start(bf16[512,128]{1,0:T(8,128)(2,1)S(1)} %get-tuple-element.44), channel_id=1, source_target_pairs={{0,48},{8,56},{16,0},{24,8},{32,16},{40,24},{48,32},{56,40},{64,11... | collective-permute-start | bytes 393224 | tf_op jit(solution)/shard_map/ppermute | solution.py:42
  104.2 12.0 %collective-permute-start.17 = (bf16[512,128]{1,0:T(8,128)(2,1)S(1)}, bf16[512,128]{1,0:T(8,128)(2,1)S(1)}, u32[]{:S(2)}, u32[]{:S(2)}) collective-permute-start(bf16[512,128]{1,0:T(8,128)(2,1)S(1)} %z_sum.1.refs_4_), channel_id=1, source_target_pairs={{0,64},{8,72},{16,80},{24,88},{32,96},{40,104},{48,112},{56,120},{... | collective-permute-start | bytes 393224 | tf_op jit(solution)/shard_map/ppermute | solution.py:42
  108.3 3.9 %collective-permute-start.16 = (f32[64,128]{1,0:T(8,128)S(1)}, f32[64,128]{1,0:T(8,128)S(1)}, u32[]{:S(2)}, u32[]{:S(2)}) collective-permute-start(f32[64,128]{1,0:T(8,128)S(1)} %get-tuple-element.39.refs_0_), channel_id=1, source_target_pairs={{0,6},{1,7},{2,0},{3,1},{4,2},{5,3},{6,4},{7,5},{8,14},{9,15},{10,... | collective-permute-start | bytes 98312 | tf_op jit(solution)/shard_map/ppermute | solution.py:46
  108.8 5.4 %collective-permute-start.15 = (f32[64,128]{1,0:T(8,128)S(1)}, f32[64,128]{1,0:T(8,128)S(1)}, u32[]{:S(2)}, u32[]{:S(2)}) collective-permute-start(f32[64,128]{1,0:T(8,128)S(1)} %get-tuple-element.39.refs_0_), channel_id=1, source_target_pairs={{0,4},{1,5},{2,6},{3,7},{4,0},{5,1},{6,2},{7,3},{8,12},{9,13},{10,... | collective-permute-start | bytes 98312 | tf_op jit(solution)/shard_map/ppermute | solution.py:46
  111.1 5.1 %collective-permute-start.14 = (f32[64,128]{1,0:T(8,128)S(1)}, f32[64,128]{1,0:T(8,128)S(1)}, u32[]{:S(2)}, u32[]{:S(2)}) collective-permute-start(f32[64,128]{1,0:T(8,128)S(1)} %get-tuple-element.39.refs_0_), channel_id=1, source_target_pairs={{0,2},{1,3},{2,4},{3,5},{4,6},{5,7},{6,0},{7,1},{8,10},{9,11},{10,... | collective-permute-start | bytes 98312 | tf_op jit(solution)/shard_map/ppermute | solution.py:46

commit v3 on v2

--- a/solution.py
+++ b/solution.py
@@ -14,10 +14,12 @@
 NDST = 32
 REP = 8
 CH = 8
-BIG, SMALL = 32, 8
+STEP_SIZES = (64, 32, 16, 8)
+SMALL = STEP_SIZES[-1]
 DEG = 16
 WROWS = 72
 WX = 2 * WROWS
+WB = 80
 SMEM = pl.BlockSpec(memory_space=pltpu.SMEM)
 VMEM = pl.BlockSpec(memory_space=pltpu.VMEM)
 ANY = pl.BlockSpec(memory_space=pl.ANY)
@@ -56,18 +58,19 @@
         group([entries[first + u] for u in range(size)])
         return 0
 
-    whole = count // BIG
-    lax.fori_loop(0, whole, lambda g, _: step(base + g * BIG, BIG), 0)
-    rest = (count - whole * BIG + SMALL - 1) // SMALL
-    lax.fori_loop(0, rest, lambda g, _: step(base + whole * BIG + g * SMALL, SMALL), 0)
+    end = base + count
+    for size in STEP_SIZES:
+        steps = (end - base + (size - 1 if size == SMALL else 0)) // size
+        lax.fori_loop(0, steps, lambda g, _, base=base, size=size: step(base + g * size, size), 0)
+        base = base + steps * size
 
 
 STEPS = (2, 1, 3, 0)
 CAP = 8 * SLOTS + SMALL
 
 
-def group_parts(dx):
-    return [blk_at(dx, dz, dc) for dc in (0, 1) for dz in STEPS]
+def group_parts(dc):
+    return [blk_at(dx, dz, dc) for dx in (1, 0) for dz in STEPS]
 
 
 def slot_of(entry):
@@ -84,9 +87,9 @@
 
 def make_plan(dests, srcs, counts, entries, totals):
     none = lax.axis_index("blk") * SLOTS + NSRC * 512 + NDST * 4096
-    for dx in range(2):
-        end = dx * CAP
-        for p in group_parts(dx):
+    for dc in range(2):
+        end = dc * CAP
+        for p in group_parts(dc):
 
             def put(g, _, p=p, end=end):
                 for u in range(8):
@@ -99,7 +102,7 @@
             end = end + count
         for u in range(SMALL):
             entries[end + u] = none
-        totals[dx] = end - dx * CAP
+        totals[dc] = end - dc * CAP
 
 
 def load_kernel(
@@ -185,29 +188,34 @@
 
 
 def glue(parts, after=()):
+    arrays = []
+    for array, _, _ in parts:
+        if not any(array is a for a in arrays):
+            arrays.append(array)
+
     def body(*refs):
-        *parts, out = refs
+        *refs, out = refs
         row = 0
-        for part in parts:
-            out[row : row + part.shape[0], :] = part[...]
-            row += part.shape[0]
-
-    shape = jax.ShapeDtypeStruct((sum(p.shape[0] for p in parts), T), bf16)
-    return small_call(body, "glue", shape, *parts, after=after)
-
-
-def forward_kernel(dx, after, entries, totals, tiles, mine, other, *refs):
-    rows = NSRC * T
-    if dx:
+        for array, first, rows in parts:
+            ref = refs[[array is a for a in arrays].index(True)]
+            out[row : row + rows, :] = ref[first : first + rows, :]
+            row += rows
+
+    shape = jax.ShapeDtypeStruct((sum(rows for _, _, rows in parts), T), bf16)
+    return small_call(body, "glue", shape, *arrays, after=after)
+
+
+def forward_kernel(dc, entries, totals, tiles, blocks, *refs):
+    rows = NSRC * T
+    if dc:
         acc_in, deg, out, acc, feat = refs
         acc[0:NDST] = acc_in[0:NDST]
     else:
         acc, feat = refs
         acc[...] = jnp.zeros_like(acc)
-    for j, p in enumerate(group_parts(dx)):
-        ref, first = (mine, other)[j // 4], j % 4 * rows
+    for j, p in enumerate(group_parts(dc)):
         for t in range(NSRC):
-            feat[t * 16 + p] = ref[first + t * T : first + (t + 1) * T, :]
+            feat[t * 16 + p] = blocks[j * rows + t * T : j * rows + (t + 1) * T, :]
 
     def group(words):
         sums = [
@@ -216,8 +224,8 @@
         for w, s in zip(words, sums):
             acc[dest_of(w)] += s
 
-    walk(entries, dx * CAP, totals[dx], group)
-    if dx:
+    walk(entries, dc * CAP, totals[dc], group)
+    if dc:
         for m in range(REP):
             out[m, 0:rows, :] = acc[m * NSRC : (m + 1) * NSRC].reshape(rows, T).astype(bf16)
             high, low = high_low(deg[m * NSRC : (m + 1) * NSRC, :])
@@ -226,25 +234,25 @@
             )
 
 
-def forward(dx, after, entries, totals, tiles, mine, other, *extra):
+def forward(dc, entries, totals, tiles, blocks, *extra):
     rows = NSRC * T
     sums = (NDST + 1, T, T)
-    if dx:
+    if dc:
         shape = jax.ShapeDtypeStruct((REP, rows + DEG, T), bf16)
     else:
         shape = jax.ShapeDtypeStruct(sums, f32)
     return pl.pallas_call(
-        functools.partial(forward_kernel, dx),
-        name=f"forward_{dx}",
+        functools.partial(forward_kernel, dc),
+        name=f"forward_{dc}",
         out_shape=shape,
-        in_specs=[ANY, SMEM, SMEM] + [VMEM] * (3 + len(extra)),
+        in_specs=[SMEM, SMEM] + [VMEM] * (2 + len(extra)),
         out_specs=VMEM,
-        scratch_shapes=([pltpu.VMEM(sums, f32)] if dx else []) + [pltpu.VMEM((80, T, T), bf16)],
+        scratch_shapes=([pltpu.VMEM(sums, f32)] if dc else []) + [pltpu.VMEM((80, T, T), bf16)],
         compiler_params=params(),
         cost_estimate=pl.CostEstimate(
             flops=4 * 10**9, bytes_accessed=8 * 17 * T * T * 2, transcendentals=0
         ),
-    )(after, entries, totals, tiles, mine, other, *extra)
+    )(entries, totals, tiles, blocks, *extra)
 
 
 def dense_kernel(recv, features, cotangent, w_self, w_neigh, bias, act, payload, self_t):
@@ -288,8 +296,8 @@
         for i in range(NSRC):
             payload[m, i * T : (i + 1) * T, :] = spread[i]
         piece = slice(m // 2 * 32, (m // 2 + 1) * 32)
-        segment = jnp.concatenate([g_self[piece], g_neigh[piece], bias_rows], axis=0)
-        payload[m, rows:, :] = jnp.concatenate(high_low(segment), axis=0)
+        segment = [g_self[piece], g_neigh[piece], bias_rows, jnp.zeros((WB - WROWS, T), f32)]
+        payload[m, rows:, :] = jnp.concatenate(segment, axis=0).astype(bf16)
 
 
 def dense(recv, features, cotangent, w_self, w_neigh, bias):
@@ -299,7 +307,7 @@
         name="dense",
         out_shape=(
             jax.ShapeDtypeStruct((rows, T), bf16),
-            jax.ShapeDtypeStruct((REP, rows + WX, T), bf16),
+            jax.ShapeDtypeStruct((REP, rows + WB, T), bf16),
             jax.ShapeDtypeStruct((NSRC, T, T), f32),
         ),
         in_specs=[VMEM] * 6,
@@ -313,10 +321,12 @@
     return wide[0:WROWS] + wide[WROWS:]
 
 
-def backward_kernel(entries, totals, tiles, recv, send, keep, acc):
-    rows = NSRC * T
-    parts = group_parts(1) + group_parts(0)
-    acc[...] = jnp.zeros_like(acc)
+def backward_kernel(dc, entries, totals, tiles, recv, after, out, acc):
+    rows = NSRC * T
+    parts = group_parts(dc)
+    for p in parts:
+        for t in range(NSRC):
+            acc[t * 16 + p] = jnp.zeros((T, T), f32)
 
     def group(words):
         sums = []
@@ -329,74 +339,90 @@
         for w, s in zip(words, sums):
             acc[column_of(w)] += s
 
-    for dx in (1, 0):
-        walk(entries, dx * CAP, totals[dx], group)
+    walk(entries, dc * CAP, totals[dc], group)
     for j, p in enumerate(parts):
-        first = (j // 8 * 4 + j % 4) * rows
         for t in range(NSRC):
-            to = slice(first + t * T, first + (t + 1) * T)
-            if j % 8 < 4:
-                keep[to, :] = acc[t * 16 + p]
-            else:
-                send[to, :] = acc[t * 16 + p].astype(bf16)
-
-
-def backward(entries, totals, tiles, recv):
+            out[j * rows + t * T : j * rows + (t + 1) * T, :] = acc[t * 16 + p].astype(out.dtype)
+
+
+def backward(dc, entries, totals, tiles, recv, after):
     rows = NSRC * T
     return pl.pallas_call(
-        backward_kernel,
-        name="backward",
-        out_shape=(
-            jax.ShapeDtypeStruct((8 * rows, T), bf16),
-            jax.ShapeDtypeStruct((8 * rows, T), f32),
-        ),
-        in_specs=[SMEM, SMEM, VMEM, VMEM],
-        out_specs=(VMEM, VMEM),
+        functools.partial(backward_kernel, dc),
+        name=f"backward_{dc}",
+        out_shape=jax.ShapeDtypeStruct((8 * rows, T), bf16 if dc else f32),
+        in_specs=[SMEM, SMEM, VMEM, VMEM, ANY],
+        out_specs=VMEM,
         scratch_shapes=[pltpu.VMEM((80, T, T), f32)],
         compiler_params=params(),
         cost_estimate=pl.CostEstimate(
-            flops=8 * 10**9, bytes_accessed=16 * 17 * T * T * 2, transcendentals=0
+            flops=4 * 10**9, bytes_accessed=8 * 17 * T * T * 2, transcendentals=0
         ),
-    )(entries, totals, tiles, recv)
+    )(entries, totals, tiles, recv, after)
 
 
 def append(send, seg, seg_got):
     n = send.shape[0]
 
-    def body(send, seg, got, out):
+    def body(send, seg, got, out, alone):
         out[0:n, :] = send[...]
-        out[n:, :] = jnp.concatenate(high_low(segment_of(seg[...]) + segment_of(got[...])), axis=0)
-
-    return small_call(body, "append", jax.ShapeDtypeStruct((n + WX, T), bf16), send, seg, seg_got)
-
-
-def core_sums(keep, got, sent):
-    rows = NSRC * T
-    high = rows + WX
-
-    def body(keep, got, sent, *out):
-        for i, ref in enumerate(out):
-            part = slice(i * rows, (i + 1) * rows)
+        total = jnp.concatenate(high_low(segment_of(seg[...]) + segment_of(got[...])), axis=0)
+        out[n:, :] = total
+        alone[...] = total
+
+    shapes = (jax.ShapeDtypeStruct((n + WX, T), bf16), jax.ShapeDtypeStruct((WX, T), bf16))
+    return small_call(body, "append", shapes, send, seg, seg_got)
+
+
+def first_sum(keep, got):
+    def body(keep, got, out):
+        out[...] = (keep[0 : NSRC * T, :] + got[0 : NSRC * T, :].astype(f32)).astype(bf16)
+
+    return small_call(body, "first_sum", jax.ShapeDtypeStruct((NSRC * T, T), bf16), keep, got)
+
+
+def core_sums(keep, got, *segs, after):
+    rows = NSRC * T
+    n = len(segs)
+
+    def body(*refs):
+        keep, got, *refs = refs
+        segs, (one, three, far, near_two, near, seg) = refs[:n], refs[n:]
+        total = segment_of(got[8 * rows :, :])
+        for ref in segs:
+            total += segment_of(ref[...])
+        total = jnp.concatenate(high_low(total), axis=0)
+        one[2 * rows :, :] = total
+        seg[...] = total
+        places = ((one, 0), (three, 0), (far, 0), (near_two, 0), (one, rows), (three, rows), (near, 0))
+        for i, (ref, first) in enumerate(places):
+            part = slice((i + 1) * rows, (i + 2) * rows)
             value = keep[part, :] + got[part, :].astype(f32)
-            ref[0:rows, :] = value.astype(ref.dtype)
-        total = segment_of(got[8 * rows :, :]) + segment_of(sent[8 * rows :, :])
-        total = jnp.concatenate(high_low(total), axis=0)
-        for ref in out[0:3]:
-            ref[rows:, :] = total
-
-    shapes = [jax.ShapeDtypeStruct((high, T), bf16)] * 3 + [jax.ShapeDtypeStruct((rows, T), f32)]
-    shapes += [jax.ShapeDtypeStruct((rows, T), bf16)] * 3 + [jax.ShapeDtypeStruct((rows, T), f32)]
-    return small_call(body, "core_sums", tuple(shapes), keep, got, sent)
+            ref[first : first + rows, :] = value.astype(ref.dtype)
+
+    def shape(height, kind):
+        return jax.ShapeDtypeStruct((height, T), kind)
+
+    shapes = (shape(2 * rows + WX, bf16), shape(2 * rows, bf16))
+    shapes += (shape(rows, f32),) * 3 + (shape(WX, bf16),)
+    return small_call(body, "core_sums", shapes, keep, got, *segs, after=after)
+
+
+def rounded_sum(a, b):
+    def body(a, b, out):
+        out[...] = (a[...] + b[...].astype(f32)).astype(bf16)
+
+    return small_call(body, "rounded_sum", jax.ShapeDtypeStruct(a.shape, bf16), a, b)
 
 
 def member_segments(spread):
     rows = NSRC * T
 
     def body(spread, out):
-        total = segment_of(spread[0, rows:, :])
+        total = spread[0, rows:, :].astype(f32)
         for m in range(1, REP):
-            total += segment_of(spread[m, rows:, :])
-        out[...] = jnp.concatenate(high_low(total), axis=0)
+            total += spread[m, rows:, :].astype(f32)
+        out[...] = jnp.concatenate(high_low(total[0:WROWS]), axis=0)
 
     return small_call(body, "member_segments", jax.ShapeDtypeStruct((WX, T), bf16), spread)
 
@@ -404,39 +430,34 @@
 def z_sum(near, *parts):
     rows = NSRC * T
 
-    def body(near, a, b, c, far):
-        block = near[...]
-        for ref in (a, b, c):
-            block += ref[0:rows, :].astype(f32)
-        far[...] = block.astype(bf16)
+    def body(near, a, b, far):
+        far[...] = (near[...] + a[0:rows, :].astype(f32) + b[0:rows, :].astype(f32)).astype(bf16)
 
     return small_call(body, "z_sum", jax.ShapeDtypeStruct((rows, T), bf16), near, *parts)
 
 
-def z_segments(own, *parts, after):
-    rows = NSRC * T
-
-    def body(own, a, b, c, pieces, bias):
-        total = segment_of(own[rows:, :])
-        for ref in (a, b, c):
-            total += segment_of(ref[rows:, :])
+def z_segments(own, got, after):
+    rows = NSRC * T
+
+    def body(own, got, pieces, bias):
+        total = segment_of(own[...]) + segment_of(got[2 * rows :, :])
         pieces[...] = total[0:64]
-        bias[...] = total[64:65]
-
-    shapes = (jax.ShapeDtypeStruct((64, T), f32), jax.ShapeDtypeStruct((1, T), f32))
-    return small_call(body, "z_segments", shapes, own, *parts, after=after)
-
-
-def final(pieces, near, self_t, *others):
-    rows = NSRC * T
-
-    def body(p0, p1, p2, p3, near, self_t, *refs):
-        *others, out, w_self, w_neigh = refs
+        bias[...] = total[64:]
+
+    shapes = (jax.ShapeDtypeStruct((64, T), f32), jax.ShapeDtypeStruct((WROWS - 64, T), f32))
+    return small_call(body, "z_segments", shapes, own, got, after=after)
+
+
+def final(pieces, bias_rows, near, self_t, far, two, one, three):
+    rows = NSRC * T
+
+    def body(p0, p1, p2, p3, bias_rows, near, self_t, far, two, one, three, out, w_self, w_neigh, bias):
+        bias[...] = bias_rows[0:1, :]
         for i in range(NSRC):
             part = slice(i * T, (i + 1) * T)
             block = near[part, :] + self_t[i]
-            for other in others:
-                block += other[part, :].astype(f32)
+            for ref, first in ((far, 0), (two, 0), (one, rows), (three, rows)):
+                block += ref[first + i * T : first + (i + 1) * T, :].astype(f32)
             out[part, :] = block.T
         y = lax.axis_index("rep") // 2
         for back, piece in enumerate((p0, p1, p2, p3)):
@@ -445,7 +466,8 @@
             w_neigh[to, :] = piece[32:64]
 
     shapes = (jax.ShapeDtypeStruct((rows, T), f32),) + (jax.ShapeDtypeStruct((T, T), f32),) * 2
-    return small_call(body, "final", shapes, *pieces, near, self_t, *others)
+    shapes += (jax.ShapeDtypeStruct((1, T), f32),)
+    return small_call(body, "final", shapes, *pieces, bias_rows, near, self_t, far, two, one, three)
 
 
 def shards(
@@ -453,13 +475,16 @@
 ):
     rows = NSRC * T
 
-    opposite = glue([moved(features, 1, 0, 0)])
-    near = glue([moved(features, 0, -dz, 0) if dz else features for dz in STEPS])
-    far = [moved(opposite, 0, -dz, 0) if dz else opposite for dz in STEPS]
-    tiles, deg, entries, totals = load(dest_tile, src_tile, tile_count, tile_values[0, 0], near)
-    far = glue(far, (deg,))
-    acc = forward(0, far, entries, totals, tiles, near, moved(near, 0, 0, 1))
-    sums = forward(1, acc, entries, totals, tiles, far, moved(far, 0, 0, 1), acc, deg)
+    two = moved(features, 0, 2, 0)
+    pair = glue([(moved(features, 1, 0, 0), 0, rows), (glue([(features, 0, rows)]), 0, rows)])
+    one, three = moved(pair, 0, -1, 0), moved(pair, 0, -3, 0)
+    far_two = moved(two, 1, 0, 0)
+    tiles, deg, entries, totals = load(dest_tile, src_tile, tile_count, tile_values[0, 0], pair)
+    held = [(v, 0, rows) for v in (far_two, one, three, pair, two)]
+    held += [(v, rows, rows) for v in (one, three, pair)]
+    held = glue(held, (deg,))
+    acc = forward(0, entries, totals, tiles, held)
+    sums = forward(1, entries, totals, tiles, moved(held, 0, 0, 1), acc, deg)
     recv = lax.all_to_all(sums, "rep", 0, 0)
 
     act, payload, self_t = dense(recv, features, cotangent, w_self, w_neigh, out_bias)
@@ -467,18 +492,21 @@
 
     seg = member_segments(spread)
     seg_got = moved(seg, 1, 0, 0)
-    send, keep = backward(entries, totals, tiles, spread)
-    send = append(send, seg, seg_got)
-    out = core_sums(keep, moved(send, 0, 0, 1), send)
-    far_out, far_block, near_out, near_block = out[0:3], out[3], out[4:7], out[7]
-    far_parts = [moved(v, 0, dz, 0) for v, dz in zip(far_out, STEPS)]
-    near_parts = [moved(v, 0, dz, 0) for v, dz in zip(near_out, STEPS)]
-    far = z_sum(far_block, *far_parts)
-    pieces, bias = z_segments(far_out[0], *far_parts, after=(far,))
+    send = backward(1, entries, totals, tiles, spread, seg)
+    send, seg = append(send, seg, seg_got)
+    keep = backward(0, entries, totals, tiles, spread, seg)
+    segs = (seg, moved(seg, 0, 2, 0), moved(seg, 0, 2, 1))
+    got = moved(send, 0, 0, 1)
+    two = first_sum(keep, got)
+    one, three, far, near_two, near, seg = core_sums(keep, got, *segs, after=(two,))
+    two = moved(two, 1, 0, 0)
+    one, three = moved(one, 0, 1, 0), moved(three, 0, 3, 0)
+    two = moved(rounded_sum(near_two, two), 0, 2, 0)
+    far = z_sum(far, one, three)
+    pieces, bias = z_segments(seg, one, (far,))
     pieces = [pieces] + [moved_y(pieces, dy) for dy in (1, 2, 3)]
-    grad_features, grad_w_self, grad_w_neigh = final(
-        pieces, near_block, self_t, moved(far, 1, 0, 0), *near_parts
-    )
+    far = moved(far, 1, 0, 0)
+    grad_features, grad_w_self, grad_w_neigh, bias = final(pieces, bias, near, self_t, far, two, one, three)
     return (act, grad_features, grad_w_self, grad_w_neigh, bias.reshape(T))
 
 

time: 117 us -> 110 us (0.940)
  waiting for transfers between devices: 17 us -> 10.1 us
  starting transfers between devices: 28.8 us -> 33.7 us
  blocking collectives: 44.1 us -> 40.6 us
  Pallas kernels: 23.4 us -> 21.5 us
    ppermute x18 -> x15, waiting for transfers between devices: 13 us -> 5.57 us  [moved(): return lax.ppermute(value, 'blk', pairs)]
    ppermute x18 -> x15, starting transfers between devices: 24.9 us -> 31.1 us  [moved(): return lax.ppermute(value, 'blk', pairs)]
    all_to_all x1, blocking collectives: 21.7 us -> 18.6 us  [shards(): spread = lax.all_to_all(payload, 'rep', 0, 0)]
    ppermute x3, starting transfers between devices: 3.83 us -> 2.54 us  [moved_y(): lax.ppermute(value, 'rep', [(i, (i // 2 + dy) % 4 * 2 + i % 2) for i in r...]
    pallas_call x3 -> x4, Pallas kernels: 12.8 us -> 11.8 us  [the longest x2 5.94 us: backward(): pl.pallas_call(functools.partial(backward_kernel, dc), name=f'backward_{d...]
  transfers between devices with their start and end apart: 21 -> 18, of which waited for: 7 -> 6; matrix products, arithmetic and copies ran while one was open for 0% -> 0% of each run, Pallas kernels for 15% -> 14%
where the time goes in v3:
time: 110 us
  blocking collectives  40.6 us (37%)
  starting transfers between devices  33.7 us (31%)
  Pallas kernels  21.5 us (20%)
  waiting for transfers between devices  10.1 us (9%)
  local copies, waits for them, and re-layouts  3.02 us (3%)
    ppermute x15, starting transfers between devices, moved(): return lax.ppermute(value, 'blk', pairs)  31.1 us
    all_to_all x1, blocking collectives, shards(): recv = lax.all_to_all(sums, 'rep', 0, 0)  21.9 us
    all_to_all x1, blocking collectives, shards(): spread = lax.all_to_all(payload, 'rep', 0, 0)  18.6 us
    pallas_call x1, Pallas kernels, load(): pl.pallas_call(load_kernel, name='load', out_shape=(jax.ShapeDtypeStruct(...  7.11 us
    pallas_call x2, Pallas kernels, backward(): pl.pallas_call(functools.partial(backward_kernel, dc), name=f'backward_{d...  5.94 us
    pallas_call x2, Pallas kernels, forward(): pl.pallas_call(functools.partial(forward_kernel, dc), name=f'forward_{dc}...  5.88 us
    ppermute x15, waiting for transfers between devices, moved(): return lax.ppermute(value, 'blk', pairs)  5.57 us
    ppermute x3, waiting for transfers between devices, moved_y(): lax.ppermute(value, 'rep', [(i, (i // 2 + dy) % 4 * 2 + i % 2) for i in r...  4.51 us
  transfers between devices with their start and end apart: 18, of which 6 were waited for; matrix products, arithmetic and copies ran while one was open for 0% of the time, Pallas kernels for 14%

profile of v3, /device:TPU:0, one launch (start us, length us, event | category | flops | bytes accessed | tf_op | source)
XLA Modules:
  0.0 109.7 jit_solution(3624268105919421678)
XLA Ops:
  0.6 3.2 %collective-permute-start = (bf16[512,128]{1,0:T(8,128)(2,1)}, bf16[512,128]{1,0:T(8,128)(2,1)S(1)}, u32[]{:S(2)}, u32[]{:S(2)}) collective-permute-start(bf16[512,128]{1,0:T(8,128)(2,1)} %features.1), channel_id=1, source_target_pairs={{0,64},{8,72},{16,80},{24,88},{32,96},{40,104},{48,112},{56,120},{... | collective-permute-start | bytes 393224 | tf_op jit(solution)/shard_map/ppermute | solution.py:44
  3.8 3.9 %collective-permute-start.1 = (bf16[512,128]{1,0:T(8,128)(2,1)}, bf16[512,128]{1,0:T(8,128)(2,1)S(1)}, u32[]{:S(2)}, u32[]{:S(2)}) collective-permute-start(bf16[512,128]{1,0:T(8,128)(2,1)} %features.1), channel_id=1, source_target_pairs={{0,32},{8,40},{16,48},{24,56},{32,0},{40,8},{48,16},{56,24},{64,96... | collective-permute-start | bytes 393224 | tf_op jit(solution)/shard_map/ppermute | solution.py:44
  7.7 0.9 copy-done
  8.7 1.1 collective-permute-start.4
  9.8 2.2 %collective-permute-start.3 = (bf16[1024,128]{1,0:T(8,128)(2,1)S(1)}, bf16[1024,128]{1,0:T(8,128)(2,1)S(1)}, u32[]{:S(2)}, u32[]{:S(2)}) collective-permute-start(bf16[1024,128]{1,0:T(8,128)(2,1)S(1)} %glue.4.after.refs_3_), channel_id=1, source_target_pairs={{0,48},{8,56},{16,0},{24,8},{32,16},{40,24},{48,32},{56,40},{64,11... | collective-permute-start | bytes 786440 | tf_op jit(solution)/shard_map/ppermute | solution.py:44
  12.0 3.0 %collective-permute-start.2 = (bf16[512,128]{1,0:T(8,128)(2,1)S(1)}, bf16[512,128]{1,0:T(8,128)(2,1)S(1)}, u32[]{:S(2)}, u32[]{:S(2)}) collective-permute-start(bf16[512,128]{1,0:T(8,128)(2,1)S(1)} %collective-permute-done.1.refs_4_), channel_id=1, source_target_pairs={{0,64},{8,72},{16,80},{24,88},{32,96},{40,104},{48,112},{56,120},{... | collective-permute-start | bytes 393224 | tf_op jit(solution)/shard_map/ppermute | solution.py:44
  15.0 0.7 copy-done.6
  15.7 0.7 copy-done.7
  16.4 0.7 copy-done.8
  17.0 7.1 %load.1 = (bf16[512,128,128]{2,1,0:T(8,128)(2,1)S(1)}, f32[32,128]{1,0:T(8,128)S(1)}, s32[528]{0:T(1024)S(1)}, s32[2]{0:T(128)S(1)}) custom-call(s32[1,1,16,32]{3,2,1,0:T(8,128)S(1)} %copy-done.6, s32[1,1,16,32]{3,2,1,0:T(8,128)S(1)} %copy-done.7, s32[1,1,16]{2,1,0:T(1,128)S(1)} %copy-done.8, bf16[16,32,128,128]{3,2,1,0:T(8,128)(2,1)} %bitcast.4, ...), custom_call_target="tpu_custom_call" | custom-call | flops 10000000000 | bytes 12000000 | tf_op jit(solution)/shard_map/load/pallas_call | solution.py:154
  24.4 2.7 %forward_0.1.refs_0_ = f32[33,128,128]{2,1,0:T(8,128)S(1)} custom-call(s32[528]{0:T(1024)S(1)} %get-tuple-element.26.entries, s32[2]{0:T(128)S(1)} %get-tuple-element.27.totals, bf16[512,128,128]{2,1,0:T(8,128)(2,1)S(1)} %get-tuple-element.28.tiles, bf16[4096,128]{1,0:T(8,128)(2,1)S(1)} %glue.5.blocks), custom_call_target="tpu_custom_call" | custom-call | flops 4000000000 | bytes 4456448 | tf_op jit(solution)/shard_map/forward_0/pallas_call | solution.py:244
  27.1 3.2 %forward_1.1 = bf16[8,528,128]{2,1,0:T(8,128)(2,1)S(1)} custom-call(s32[528]{0:T(1024)S(1)} %get-tuple-element.26.entries, s32[2]{0:T(128)S(1)} %get-tuple-element.27.totals, bf16[512,128,128]{2,1,0:T(8,128)(2,1)S(1)} %get-tuple-element.28.tiles, bf16[4096,128]{1,0:T(8,128)(2,1)S(1)} %collective-permute-done.5.blocks, f32[33,128,128]{2,1,0:T(8,128)S(1)} %forward_0.1.refs_0_, ...), custom_call_target="tpu_custom_call" | custom-call | flops 4000000000 | bytes 4456448 | tf_op jit(solution)/shard_map/forward_1/pallas_call | solution.py:244
  30.3 21.9 %all_to_all.10.recv = bf16[8,528,128]{2,1,0:T(8,128)(2,1)S(1)} all-to-all(bf16[8,528,128]{2,1,0:T(8,128)(2,1)S(1)} %forward_1.1), channel_id=1, replica_groups=mesh['blk'=16,'rep'=8] {'rep'}, dimensions={0} | all-to-all | bytes 2162688 | tf_op jit(solution)/shard_map/all_to_all | solution.py:488
  52.3 1.2 %dense.1 = (bf16[512,128]{1,0:T(8,128)(2,1)}, bf16[8,592,128]{2,1,0:T(8,128)(2,1)S(1)}, f32[4,128,128]{2,1,0:T(8,128)S(1)}) custom-call(bf16[8,528,128]{2,1,0:T(8,128)(2,1)S(1)} %all_to_all.10.recv, bf16[512,128]{1,0:T(8,128)(2,1)S(1)} %copy-done.1, bf16[512,128]{1,0:T(8,128)(2,1)S(1)} %copy-done.2, bf16[128,128]{1,0:T(8,128)(2,1)S(1)} %copy-done.3, ...), custom_call_target="tpu_custom_call" | custom-call | tf_op jit(solution)/shard_map/dense/pallas_call | solution.py:305
  53.5 18.6 %all_to_all.11.refs_0_.recv = bf16[8,592,128]{2,1,0:T(8,128)(2,1)S(1)} all-to-all(bf16[8,592,128]{2,1,0:T(8,128)(2,1)S(1)} %get-tuple-element.31), channel_id=1, replica_groups=mesh['blk'=16,'rep'=8] {'rep'}, dimensions={0} | all-to-all | bytes 2424832 | tf_op jit(solution)/shard_map/all_to_all | solution.py:491
  72.1 4.1 %collective-permute-start.6 = (bf16[144,128]{1,0:T(8,128)(2,1)S(1)}, bf16[144,128]{1,0:T(8,128)(2,1)S(1)}, u32[]{:S(2)}, u32[]{:S(2)}) collective-permute-start(bf16[144,128]{1,0:T(8,128)(2,1)S(1)} %member_segments.1.after.refs_1_), channel_id=1, source_target_pairs={{0,64},{8,72},{16,80},{24,88},{32,96},{40,104},{48,112},{56,120},{... | collective-permute-start | bytes 110600 | tf_op jit(solution)/shard_map/ppermute | solution.py:44
  76.2 3.1 %backward_1.1.refs_0_ = bf16[4096,128]{1,0:T(8,128)(2,1)S(1)} custom-call(s32[528]{0:T(1024)S(1)} %get-tuple-element.26.entries, s32[2]{0:T(128)S(1)} %get-tuple-element.27.totals, bf16[512,128,128]{2,1,0:T(8,128)(2,1)S(1)} %get-tuple-element.28.tiles, bf16[8,592,128]{2,1,0:T(8,128)(2,1)S(1)} %all_to_all.11.refs_0_.recv, ...), custom_call_target="tpu_custom_call" | custom-call | flops 4000000000 | bytes 4456448 | tf_op jit(solution)/shard_map/backward_1/pallas_call | solution.py:350
  79.7 2.6 %collective-permute-start.9 = (bf16[144,128]{1,0:T(8,128)(2,1)S(1)}, bf16[144,128]{1,0:T(8,128)(2,1)S(1)}, u32[]{:S(2)}, u32[]{:S(2)}) collective-permute-start(bf16[144,128]{1,0:T(8,128)(2,1)S(1)} %get-tuple-element.32.after.refs_2_), channel_id=1, source_target_pairs={{0,40},{8,32},{16,56},{24,48},{32,8},{40,0},{48,24},{56,16},{64,10... | collective-permute-start | bytes 110600 | tf_op jit(solution)/shard_map/ppermute | solution.py:44
  82.3 1.0 collective-permute-start.8
  83.4 2.8 %backward_0.1.refs_0_ = f32[4096,128]{1,0:T(8,128)S(1)} custom-call(s32[528]{0:T(1024)S(1)} %get-tuple-element.26.entries, s32[2]{0:T(128)S(1)} %get-tuple-element.27.totals, bf16[512,128,128]{2,1,0:T(8,128)(2,1)S(1)} %get-tuple-element.28.tiles, bf16[8,592,128]{2,1,0:T(8,128)(2,1)S(1)} %all_to_all.11.refs_0_.recv, ...), custom_call_target="tpu_custom_call" | custom-call | flops 4000000000 | bytes 4456448 | tf_op jit(solution)/shard_map/backward_0/pallas_call | solution.py:350
  86.2 1.6 %collective-permute-done.8.refs_3_ = bf16[144,128]{1,0:T(8,128)(2,1)S(1)} collective-permute-done((bf16[144,128]{1,0:T(8,128)(2,1)S(1)}, bf16[144,128]{1,0:T(8,128)(2,1)S(1)}, u32[]{:S(2)}, u32[]{:S(2)}) %collective-permute-start.8) | collective-permute-done | bytes 36896 | tf_op jit(solution)/shard_map/ppermute | solution.py:44
  88.4 2.9 %collective-permute-start.11 = (bf16[1024,128]{1,0:T(8,128)(2,1)S(1)}, bf16[1024,128]{1,0:T(8,128)(2,1)S(1)}, u32[]{:S(2)}, u32[]{:S(2)}) collective-permute-start(bf16[1024,128]{1,0:T(8,128)(2,1)S(1)} %get-tuple-element.37), channel_id=1, source_target_pairs={{0,48},{8,56},{16,0},{24,8},{32,16},{40,24},{48,32},{56,40},{64,11... | collective-permute-start | bytes 786440 | tf_op jit(solution)/shard_map/ppermute | solution.py:44
  91.3 2.9 %collective-permute-start.16 = (bf16[512,128]{1,0:T(8,128)(2,1)S(1)}, bf16[512,128]{1,0:T(8,128)(2,1)S(1)}, u32[]{:S(2)}, u32[]{:S(2)}) collective-permute-start(bf16[512,128]{1,0:T(8,128)(2,1)S(1)} %first_sum.1.refs_5_), channel_id=1, source_target_pairs={{0,64},{8,72},{16,80},{24,88},{32,96},{40,104},{48,112},{56,120},{... | collective-permute-start | bytes 393224 | tf_op jit(solution)/shard_map/ppermute | solution.py:44
  94.2 3.6 %collective-permute-done.16.refs_1_ = bf16[512,128]{1,0:T(8,128)(2,1)S(1)} collective-permute-done((bf16[512,128]{1,0:T(8,128)(2,1)S(1)}, bf16[512,128]{1,0:T(8,128)(2,1)S(1)}, u32[]{:S(2)}, u32[]{:S(2)}) %collective-permute-start.16) | collective-permute-done | bytes 131104 | tf_op jit(solution)/shard_map/ppermute | solution.py:44
  98.2 3.2 %collective-permute-start.15 = (bf16[512,128]{1,0:T(8,128)(2,1)S(1)}, bf16[512,128]{1,0:T(8,128)(2,1)S(1)}, u32[]{:S(2)}, u32[]{:S(2)}) collective-permute-start(bf16[512,128]{1,0:T(8,128)(2,1)S(1)} %z_sum.1.refs_2_), channel_id=1, source_target_pairs={{0,64},{8,72},{16,80},{24,88},{32,96},{40,104},{48,112},{56,120},{... | collective-permute-start | bytes 393224 | tf_op jit(solution)/shard_map/ppermute | solution.py:44
  101.4 1.0 collective-permute-start.14
  102.4 1.4 %collective-permute-start.13 = (f32[64,128]{1,0:T(8,128)S(1)}, f32[64,128]{1,0:T(8,128)S(1)}, u32[]{:S(2)}, u32[]{:S(2)}) collective-permute-start(f32[64,128]{1,0:T(8,128)S(1)} %get-tuple-element.38.refs_0_), channel_id=1, source_target_pairs={{0,4},{1,5},{2,6},{3,7},{4,0},{5,1},{6,2},{7,3},{8,12},{9,13},{10,... | collective-permute-start | bytes 98312 | tf_op jit(solution)/shard_map/ppermute | solution.py:48
  103.9 0.4 collective-permute-done.17.refs_8_
  104.4 1.0 collective-permute-done.14.refs_3_
  105.4 2.4 %collective-permute-done.13.refs_2_ = f32[64,128]{1,0:T(8,128)S(1)} collective-permute-done((f32[64,128]{1,0:T(8,128)S(1)}, f32[64,128]{1,0:T(8,128)S(1)}, u32[]{:S(2)}, u32[]{:S(2)}) %collective-permute-start.13) | collective-permute-done | bytes 32800 | tf_op jit(solution)/shard_map/ppermute | solution.py:48
  107.8 1.1 collective-permute-done.12.refs_1_
  108.9 0.9 final.1
  (41 shorter events, 1.9 us)
Async XLA Ops:
  0.6 8.0 %collective-permute-start = (bf16[512,128]{1,0:T(8,128)(2,1)}, bf16[512,128]{1,0:T(8,128)(2,1)S(1)}, u32[]{:S(2)}, u32[]{:S(2)}) collective-permute-start(bf16[512,128]{1,0:T(8,128)(2,1)} %features.1), channel_id=1, source_target_pairs={{0,64},{8,72},{16,80},{24,88},{32,96},{40,104},{48,112},{56,120},{... | collective-permute-start | bytes 393224 | tf_op jit(solution)/shard_map/ppermute | solution.py:44
  3.8 8.2 %collective-permute-start.1 = (bf16[512,128]{1,0:T(8,128)(2,1)}, bf16[512,128]{1,0:T(8,128)(2,1)S(1)}, u32[]{:S(2)}, u32[]{:S(2)}) collective-permute-start(bf16[512,128]{1,0:T(8,128)(2,1)} %features.1), channel_id=1, source_target_pairs={{0,32},{8,40},{16,48},{24,56},{32,0},{40,8},{48,16},{56,24},{64,96... | collective-permute-start | bytes 393224 | tf_op jit(solution)/shard_map/ppermute | solution.py:44
  7.7 0.9 copy-start
  8.7 15.5 %collective-permute-start.4 = (bf16[1024,128]{1,0:T(8,128)(2,1)S(1)}, bf16[1024,128]{1,0:T(8,128)(2,1)S(1)}, u32[]{:S(2)}, u32[]{:S(2)}) collective-permute-start(bf16[1024,128]{1,0:T(8,128)(2,1)S(1)} %glue.4.after.refs_3_), channel_id=1, source_target_pairs={{0,16},{8,24},{16,32},{24,40},{32,48},{40,56},{48,0},{56,8},{64,80... | collective-permute-start | bytes 786440 | tf_op jit(solution)/shard_map/ppermute | solution.py:44
  9.8 14.4 %collective-permute-start.3 = (bf16[1024,128]{1,0:T(8,128)(2,1)S(1)}, bf16[1024,128]{1,0:T(8,128)(2,1)S(1)}, u32[]{:S(2)}, u32[]{:S(2)}) collective-permute-start(bf16[1024,128]{1,0:T(8,128)(2,1)S(1)} %glue.4.after.refs_3_), channel_id=1, source_target_pairs={{0,48},{8,56},{16,0},{24,8},{32,16},{40,24},{48,32},{56,40},{64,11... | collective-permute-start | bytes 786440 | tf_op jit(solution)/shard_map/ppermute | solution.py:44
  12.0 12.2 %collective-permute-start.2 = (bf16[512,128]{1,0:T(8,128)(2,1)S(1)}, bf16[512,128]{1,0:T(8,128)(2,1)S(1)}, u32[]{:S(2)}, u32[]{:S(2)}) collective-permute-start(bf16[512,128]{1,0:T(8,128)(2,1)S(1)} %collective-permute-done.1.refs_4_), channel_id=1, source_target_pairs={{0,64},{8,72},{16,80},{24,88},{32,96},{40,104},{48,112},{56,120},{... | collective-permute-start | bytes 393224 | tf_op jit(solution)/shard_map/ppermute | solution.py:44
  15.0 0.7 copy-start.6
  15.7 0.7 copy-start.7
  16.4 0.7 copy-start.8
  24.3 2.8 %collective-permute-start.5 = (bf16[4096,128]{1,0:T(8,128)(2,1)S(1)}, bf16[4096,128]{1,0:T(8,128)(2,1)S(1)}, u32[]{:S(2)}, u32[]{:S(2)}) collective-permute-start(bf16[4096,128]{1,0:T(8,128)(2,1)S(1)} %glue.5.blocks), channel_id=1, source_target_pairs={{0,8},{8,0},{16,24},{24,16},{32,40},{40,32},{48,56},{56,48},{64,72... | collective-permute-start | bytes 3145736 | tf_op jit(solution)/shard_map/ppermute | solution.py:44
  30.3 22.0 %copy-start.1 = (bf16[512,128]{1,0:T(8,128)(2,1)S(1)}, bf16[512,128]{1,0:T(8,128)(2,1)}, u32[]{:S(2)}) copy-start(bf16[512,128]{1,0:T(8,128)(2,1)} %features.1) | copy-start | bytes 393220
  30.3 22.0 %copy-start.2 = (bf16[512,128]{1,0:T(8,128)(2,1)S(1)}, bf16[512,128]{1,0:T(8,128)(2,1)}, u32[]{:S(2)}) copy-start(bf16[512,128]{1,0:T(8,128)(2,1)} %cotangent.1) | copy-start | bytes 393220
  30.3 22.0 %copy-start.3 = (bf16[128,128]{1,0:T(8,128)(2,1)S(1)}, bf16[128,128]{1,0:T(8,128)(2,1)}, u32[]{:S(2)}) copy-start(bf16[128,128]{1,0:T(8,128)(2,1)} %w_self.1) | copy-start | bytes 98308
  30.3 22.0 %copy-start.4 = (bf16[128,128]{1,0:T(8,128)(2,1)S(1)}, bf16[128,128]{1,0:T(8,128)(2,1)}, u32[]{:S(2)}) copy-start(bf16[128,128]{1,0:T(8,128)(2,1)} %w_neigh.1) | copy-start | bytes 98308
  30.3 22.0 %copy-start.5 = (f32[128]{0:T(128)S(1)}, f32[128]{0:T(128)}, u32[]{:S(2)}) copy-start(f32[128]{0:T(128)} %param.13) | copy-start | bytes 1540
  72.1 7.2 %collective-permute-start.6 = (bf16[144,128]{1,0:T(8,128)(2,1)S(1)}, bf16[144,128]{1,0:T(8,128)(2,1)S(1)}, u32[]{:S(2)}, u32[]{:S(2)}) collective-permute-start(bf16[144,128]{1,0:T(8,128)(2,1)S(1)} %member_segments.1.after.refs_1_), channel_id=1, source_target_pairs={{0,64},{8,72},{16,80},{24,88},{32,96},{40,104},{48,112},{56,120},{... | collective-permute-start | bytes 110600 | tf_op jit(solution)/shard_map/ppermute | solution.py:44
  79.4 6.7 %collective-permute-start.7 = (bf16[4240,128]{1,0:T(8,128)(2,1)S(1)}, bf16[4240,128]{1,0:T(8,128)(2,1)S(1)}, u32[]{:S(2)}, u32[]{:S(2)}) collective-permute-start(bf16[4240,128]{1,0:T(8,128)(2,1)S(1)} %get-tuple-element.33), channel_id=1, source_target_pairs={{0,8},{8,0},{16,24},{24,16},{32,40},{40,32},{48,56},{56,48},{64,72... | collective-permute-start | bytes 3256328 | tf_op jit(solution)/shard_map/ppermute | solution.py:44
  79.7 6.5 %collective-permute-start.9 = (bf16[144,128]{1,0:T(8,128)(2,1)S(1)}, bf16[144,128]{1,0:T(8,128)(2,1)S(1)}, u32[]{:S(2)}, u32[]{:S(2)}) collective-permute-start(bf16[144,128]{1,0:T(8,128)(2,1)S(1)} %get-tuple-element.32.after.refs_2_), channel_id=1, source_target_pairs={{0,40},{8,32},{16,56},{24,48},{32,8},{40,0},{48,24},{56,16},{64,10... | collective-permute-start | bytes 110600 | tf_op jit(solution)/shard_map/ppermute | solution.py:44
  82.3 5.5 %collective-permute-start.8 = (bf16[144,128]{1,0:T(8,128)(2,1)S(1)}, bf16[144,128]{1,0:T(8,128)(2,1)S(1)}, u32[]{:S(2)}, u32[]{:S(2)}) collective-permute-start(bf16[144,128]{1,0:T(8,128)(2,1)S(1)} %get-tuple-element.32.after.refs_2_), channel_id=1, source_target_pairs={{0,32},{8,40},{16,48},{24,56},{32,0},{40,8},{48,16},{56,24},{64,96... | collective-permute-start | bytes 110600 | tf_op jit(solution)/shard_map/ppermute | solution.py:44
  88.0 10.1 %collective-permute-start.10 = (bf16[1168,128]{1,0:T(8,128)(2,1)S(1)}, bf16[1168,128]{1,0:T(8,128)(2,1)S(1)}, u32[]{:S(2)}, u32[]{:S(2)}) collective-permute-start(bf16[1168,128]{1,0:T(8,128)(2,1)S(1)} %get-tuple-element.35), channel_id=1, source_target_pairs={{0,16},{8,24},{16,32},{24,40},{32,48},{40,56},{48,0},{56,8},{64,80... | collective-permute-start | bytes 897032 | tf_op jit(solution)/shard_map/ppermute | solution.py:44
  88.4 9.7 %collective-permute-start.11 = (bf16[1024,128]{1,0:T(8,128)(2,1)S(1)}, bf16[1024,128]{1,0:T(8,128)(2,1)S(1)}, u32[]{:S(2)}, u32[]{:S(2)}) collective-permute-start(bf16[1024,128]{1,0:T(8,128)(2,1)S(1)} %get-tuple-element.37), channel_id=1, source_target_pairs={{0,48},{8,56},{16,0},{24,8},{32,16},{40,24},{48,32},{56,40},{64,11... | collective-permute-start | bytes 786440 | tf_op jit(solution)/shard_map/ppermute | solution.py:44
  91.3 6.5 %collective-permute-start.16 = (bf16[512,128]{1,0:T(8,128)(2,1)S(1)}, bf16[512,128]{1,0:T(8,128)(2,1)S(1)}, u32[]{:S(2)}, u32[]{:S(2)}) collective-permute-start(bf16[512,128]{1,0:T(8,128)(2,1)S(1)} %first_sum.1.refs_5_), channel_id=1, source_target_pairs={{0,64},{8,72},{16,80},{24,88},{32,96},{40,104},{48,112},{56,120},{... | collective-permute-start | bytes 393224 | tf_op jit(solution)/shard_map/ppermute | solution.py:44
  97.8 6.6 %collective-permute-start.17 = (bf16[512,128]{1,0:T(8,128)(2,1)S(1)}, bf16[512,128]{1,0:T(8,128)(2,1)S(1)}, u32[]{:S(2)}, u32[]{:S(2)}) collective-permute-start(bf16[512,128]{1,0:T(8,128)(2,1)S(1)} %rounded_sum.1), channel_id=1, source_target_pairs={{0,32},{8,40},{16,48},{24,56},{32,0},{40,8},{48,16},{56,24},{64,96... | collective-permute-start | bytes 393224 | tf_op jit(solution)/shard_map/ppermute | solution.py:44
  98.2 10.7 %collective-permute-start.15 = (bf16[512,128]{1,0:T(8,128)(2,1)S(1)}, bf16[512,128]{1,0:T(8,128)(2,1)S(1)}, u32[]{:S(2)}, u32[]{:S(2)}) collective-permute-start(bf16[512,128]{1,0:T(8,128)(2,1)S(1)} %z_sum.1.refs_2_), channel_id=1, source_target_pairs={{0,64},{8,72},{16,80},{24,88},{32,96},{40,104},{48,112},{56,120},{... | collective-permute-start | bytes 393224 | tf_op jit(solution)/shard_map/ppermute | solution.py:44
  101.4 4.0 %collective-permute-start.14 = (f32[64,128]{1,0:T(8,128)S(1)}, f32[64,128]{1,0:T(8,128)S(1)}, u32[]{:S(2)}, u32[]{:S(2)}) collective-permute-start(f32[64,128]{1,0:T(8,128)S(1)} %get-tuple-element.38.refs_0_), channel_id=1, source_target_pairs={{0,6},{1,7},{2,0},{3,1},{4,2},{5,3},{6,4},{7,5},{8,14},{9,15},{10,... | collective-permute-start | bytes 98312 | tf_op jit(solution)/shard_map/ppermute | solution.py:48
  102.4 5.4 %collective-permute-start.13 = (f32[64,128]{1,0:T(8,128)S(1)}, f32[64,128]{1,0:T(8,128)S(1)}, u32[]{:S(2)}, u32[]{:S(2)}) collective-permute-start(f32[64,128]{1,0:T(8,128)S(1)} %get-tuple-element.38.refs_0_), channel_id=1, source_target_pairs={{0,4},{1,5},{2,6},{3,7},{4,0},{5,1},{6,2},{7,3},{8,12},{9,13},{10,... | collective-permute-start | bytes 98312 | tf_op jit(solution)/shard_map/ppermute | solution.py:48
  103.7 5.1 %collective-permute-start.12 = (f32[64,128]{1,0:T(8,128)S(1)}, f32[64,128]{1,0:T(8,128)S(1)}, u32[]{:S(2)}, u32[]{:S(2)}) collective-permute-start(f32[64,128]{1,0:T(8,128)S(1)} %get-tuple-element.38.refs_0_), channel_id=1, source_target_pairs={{0,2},{1,3},{2,4},{3,5},{4,6},{5,7},{6,0},{7,1},{8,10},{9,11},{10,... | collective-permute-start | bytes 98312 | tf_op jit(solution)/shard_map/ppermute | solution.py:48

commit v4 on v3

--- a/solution.py
+++ b/solution.py
@@ -13,7 +13,7 @@
 NSRC = 4
 NDST = 32
 REP = 8
-CH = 8
+CH = 16
 STEP_SIZES = (64, 32, 16, 8)
 SMALL = STEP_SIZES[-1]
 DEG = 16
@@ -85,7 +85,7 @@
     return entry >> 12
 
 
-def make_plan(dests, srcs, counts, entries, totals):
+def make_plan(words, counts, entries, totals):
     none = lax.axis_index("blk") * SLOTS + NSRC * 512 + NDST * 4096
     for dc in range(2):
         end = dc * CAP
@@ -93,8 +93,7 @@
 
             def put(g, _, p=p, end=end):
                 for u in range(8):
-                    k = g * 8 + u
-                    entries[end + k] = p * SLOTS + k + (srcs[0, 0, p, k] << 9) + (dests[0, 0, p, k] << 12)
+                    entries[end + g * 8 + u] = words[0, 0, p, g * 8 + u]
                 return 0
 
             count = counts[0, 0, p]
@@ -106,9 +105,9 @@
 
 
 def load_kernel(
-    dests_in, srcs_in, counts_in, tiles, after, held, deg_out, entries, totals, acc, sem, dests, srcs, counts, small_sem
+    words_in, counts_in, tiles, after, held, deg_out, entries, totals, acc, sem, words, counts, small_sem
 ):
-    pairs = ((counts_in, counts), (dests_in, dests), (srcs_in, srcs))
+    pairs = ((counts_in, counts), (words_in, words))
     small = [pltpu.make_async_copy(a, b, small_sem.at[i]) for i, (a, b) in enumerate(pairs)]
     for copy in small:
         copy.start()
@@ -125,8 +124,7 @@
     for p in range(16):
         each_copy(p, lambda copy: copy.start())
     small[1].wait()
-    small[2].wait()
-    make_plan(dests, srcs, counts, entries, totals)
+    make_plan(words, counts, entries, totals)
     acc[...] = jnp.zeros_like(acc)
 
     def add(p, _):
@@ -136,7 +134,7 @@
         def step(g, _):
             for u in range(SMALL):
                 k = g * SMALL + u
-                d = jnp.where(k < count, dests[0, 0, p, k], NDST)
+                d = jnp.where(k < count, dest_of(words[0, 0, p, k]), NDST)
                 acc[d] += held[p * SLOTS + k].astype(f32)
             return 0
 
@@ -150,7 +148,7 @@
         deg_out[d : d + 1, :] = jnp.sum(jnp.where(eye, column, 0.0), axis=0, keepdims=True)
 
 
-def load(dest_tile, src_tile, tile_count, tiles, after):
+def load(words, tile_count, tiles, after):
     return pl.pallas_call(
         load_kernel,
         name="load",
@@ -160,19 +158,18 @@
             jax.ShapeDtypeStruct((2 * CAP,), jnp.int32),
             jax.ShapeDtypeStruct((2,), jnp.int32),
         ),
-        in_specs=[HBM] * 4 + [ANY],
+        in_specs=[ANY] * 2 + [HBM, ANY],
         out_specs=(VMEM, VMEM, SMEM, SMEM),
         scratch_shapes=[
             pltpu.VMEM((NDST + 1, T, T), f32),
             pltpu.SemaphoreType.DMA((16, SLOTS // CH)),
-            pltpu.SMEM(dest_tile.shape, jnp.int32),
-            pltpu.SMEM(src_tile.shape, jnp.int32),
+            pltpu.SMEM(words.shape, jnp.int32),
             pltpu.SMEM(tile_count.shape, jnp.int32),
-            pltpu.SemaphoreType.DMA((3,)),
+            pltpu.SemaphoreType.DMA((2,)),
         ],
         compiler_params=params(),
         cost_estimate=pl.CostEstimate(flops=10**10, bytes_accessed=12 * 10**6, transcendentals=0),
-    )(dest_tile, src_tile, tile_count, tiles, after)
+    )(words, tile_count, tiles, after)
 
 
 def small_call(body, name, shapes, *operands, after=()):
@@ -185,6 +182,18 @@
         out_specs=VMEM if isinstance(shapes, jax.ShapeDtypeStruct) else (VMEM,) * len(shapes),
         compiler_params=params(8),
     )(*operands, *after)
+
+
+def stage(features, dest_tile, src_tile, tile_count):
+    def body(features, dests, srcs, counts, feat, words, count_out):
+        feat[...] = features[...]
+        count_out[...] = counts[...]
+        shape = dests.shape[2:]
+        place = lax.broadcasted_iota(jnp.int32, shape, 0) * SLOTS + lax.broadcasted_iota(jnp.int32, shape, 1)
+        words[0, 0] = place + (srcs[0, 0] << 9) + (dests[0, 0] << 12)
+
+    shapes = tuple(jax.ShapeDtypeStruct(v.shape, v.dtype) for v in (features, dest_tile, tile_count))
+    return small_call(body, "stage", shapes, features, dest_tile, src_tile, tile_count)
 
 
 def glue(parts, after=()):
@@ -476,10 +485,11 @@
     rows = NSRC * T
 
     two = moved(features, 0, 2, 0)
-    pair = glue([(moved(features, 1, 0, 0), 0, rows), (glue([(features, 0, rows)]), 0, rows)])
+    own, words, counts = stage(features, dest_tile, src_tile, tile_count)
+    pair = glue([(moved(features, 1, 0, 0), 0, rows), (own, 0, rows)], (words,))
     one, three = moved(pair, 0, -1, 0), moved(pair, 0, -3, 0)
     far_two = moved(two, 1, 0, 0)
-    tiles, deg, entries, totals = load(dest_tile, src_tile, tile_count, tile_values[0, 0], pair)
+    tiles, deg, entries, totals = load(words, counts, tile_values[0, 0], pair)
     held = [(v, 0, rows) for v in (far_two, one, three, pair, two)]
     held += [(v, rows, rows) for v in (one, three, pair)]
     held = glue(held, (deg,))

time: 110 us -> 108 us (0.982)
  starting transfers between devices: 33.7 us -> 30.5 us
    ppermute x15, starting transfers between devices: 31.1 us -> 27.7 us  [moved(): return lax.ppermute(value, 'blk', pairs)]
    all_to_all x1, blocking collectives: 18.6 us -> 20.2 us  [shards(): spread = lax.all_to_all(payload, 'rep', 0, 0)]
  transfers between devices with their start and end apart: 18 -> 18, of which waited for: 6 -> 5; matrix products, arithmetic and copies ran while one was open for 0% -> 0% of each run, Pallas kernels for 14% -> 16%
where the time goes in v4:
time: 108 us; the launch traced here: 107 us
  blocking collectives  41.2 us (38%)
  starting transfers between devices  30.5 us (28%)
  Pallas kernels  22.4 us (21%)
  waiting for transfers between devices  9.24 us (9%)
  local copies, waits for them, and re-layouts  3.02 us (3%)
    ppermute x15, starting transfers between devices, moved(): return lax.ppermute(value, 'blk', pairs)  27.7 us
    all_to_all x1, blocking collectives, shards(): recv = lax.all_to_all(sums, 'rep', 0, 0)  21.1 us
    all_to_all x1, blocking collectives, shards(): spread = lax.all_to_all(payload, 'rep', 0, 0)  20.2 us
    pallas_call x1, Pallas kernels, load(): pl.pallas_call(load_kernel, name='load', out_shape=(jax.ShapeDtypeStruct(...  6.87 us
    pallas_call x2, Pallas kernels, backward(): pl.pallas_call(functools.partial(backward_kernel, dc), name=f'backward_{d...  6.48 us
    pallas_call x2, Pallas kernels, forward(): pl.pallas_call(functools.partial(forward_kernel, dc), name=f'forward_{dc}...  6.39 us
    ppermute x15, waiting for transfers between devices, moved(): return lax.ppermute(value, 'blk', pairs)  4.74 us
    ppermute x3, waiting for transfers between devices, moved_y(): lax.ppermute(value, 'rep', [(i, (i // 2 + dy) % 4 * 2 + i % 2) for i in r...  4.5 us
  transfers between devices with their start and end apart: 18, of which 5 were waited for; matrix products, arithmetic and copies ran while one was open for 0% of the time, Pallas kernels for 16%

profile of v4, /device:TPU:0, one launch (start us, length us, event | category | flops | bytes accessed | tf_op | source)
XLA Modules:
  0.0 107.2 jit_solution(7774387269287287951)
XLA Ops:
  0.6 3.2 %collective-permute-start = (bf16[512,128]{1,0:T(8,128)(2,1)}, bf16[512,128]{1,0:T(8,128)(2,1)S(1)}, u32[]{:S(2)}, u32[]{:S(2)}) collective-permute-start(bf16[512,128]{1,0:T(8,128)(2,1)} %features.1), channel_id=1, source_target_pairs={{0,64},{8,72},{16,80},{24,88},{32,96},{40,104},{48,112},{56,120},{... | collective-permute-start | bytes 393224 | tf_op jit(solution)/shard_map/ppermute | solution.py:44
  3.8 3.9 %collective-permute-start.1 = (bf16[512,128]{1,0:T(8,128)(2,1)}, bf16[512,128]{1,0:T(8,128)(2,1)S(1)}, u32[]{:S(2)}, u32[]{:S(2)}) collective-permute-start(bf16[512,128]{1,0:T(8,128)(2,1)} %features.1), channel_id=1, source_target_pairs={{0,32},{8,40},{16,48},{24,56},{32,0},{40,8},{48,16},{56,24},{64,96... | collective-permute-start | bytes 393224 | tf_op jit(solution)/shard_map/ppermute | solution.py:44
  7.7 0.9 copy-done
  8.6 0.7 copy-done.5
  9.3 0.7 copy-done.6
  10.0 0.7 copy-done.8
  10.7 1.1 %collective-permute-start.4 = (bf16[1024,128]{1,0:T(8,128)(2,1)S(1)}, bf16[1024,128]{1,0:T(8,128)(2,1)S(1)}, u32[]{:S(2)}, u32[]{:S(2)}) collective-permute-start(bf16[1024,128]{1,0:T(8,128)(2,1)S(1)} %glue.2.after.refs_3_), channel_id=1, source_target_pairs={{0,16},{8,24},{16,32},{24,40},{32,48},{40,56},{48,0},{56,8},{64,80... | collective-permute-start | bytes 786440 | tf_op jit(solution)/shard_map/ppermute | solution.py:44
  11.8 2.2 %collective-permute-start.3 = (bf16[1024,128]{1,0:T(8,128)(2,1)S(1)}, bf16[1024,128]{1,0:T(8,128)(2,1)S(1)}, u32[]{:S(2)}, u32[]{:S(2)}) collective-permute-start(bf16[1024,128]{1,0:T(8,128)(2,1)S(1)} %glue.2.after.refs_3_), channel_id=1, source_target_pairs={{0,48},{8,56},{16,0},{24,8},{32,16},{40,24},{48,32},{56,40},{64,11... | collective-permute-start | bytes 786440 | tf_op jit(solution)/shard_map/ppermute | solution.py:44
  14.0 0.9 collective-permute-start.2
  15.0 6.9 %load.1 = (bf16[512,128,128]{2,1,0:T(8,128)(2,1)S(1)}, f32[32,128]{1,0:T(8,128)S(1)}, s32[528]{0:T(1024)S(1)}, s32[2]{0:T(128)S(1)}) custom-call(s32[1,1,16,32]{3,2,1,0:T(8,128)S(1)} %get-tuple-element.29.refs_2_.words_in, s32[1,1,16]{2,1,0:T(1,128)S(1)} %get-tuple-element.30.counts_in, bf16[16,32,128,128]{3,2,1,0:T(8,128)(2,1)} %bitcast.4, ...), custom_call_target="tpu_custom_call" | custom-call | flops 10000000000 | bytes 12000000 | tf_op jit(solution)/shard_map/load/pallas_call | solution.py:152
  22.1 3.1 %forward_0.1.refs_0_ = f32[33,128,128]{2,1,0:T(8,128)S(1)} custom-call(s32[528]{0:T(1024)S(1)} %get-tuple-element.32.entries, s32[2]{0:T(128)S(1)} %get-tuple-element.33.totals, bf16[512,128,128]{2,1,0:T(8,128)(2,1)S(1)} %get-tuple-element.34.tiles, bf16[4096,128]{1,0:T(8,128)(2,1)S(1)} %glue.3.blocks), custom_call_target="tpu_custom_call" | custom-call | flops 4000000000 | bytes 4456448 | tf_op jit(solution)/shard_map/forward_0/pallas_call | solution.py:253
  25.2 3.3 %forward_1.1 = bf16[8,528,128]{2,1,0:T(8,128)(2,1)S(1)} custom-call(s32[528]{0:T(1024)S(1)} %get-tuple-element.32.entries, s32[2]{0:T(128)S(1)} %get-tuple-element.33.totals, bf16[512,128,128]{2,1,0:T(8,128)(2,1)S(1)} %get-tuple-element.34.tiles, bf16[4096,128]{1,0:T(8,128)(2,1)S(1)} %collective-permute-done.5.blocks, f32[33,128,128]{2,1,0:T(8,128)S(1)} %forward_0.1.refs_0_, ...), custom_call_target="tpu_custom_call" | custom-call | flops 4000000000 | bytes 4456448 | tf_op jit(solution)/shard_map/forward_1/pallas_call | solution.py:253
  28.5 21.1 %all_to_all.10.recv = bf16[8,528,128]{2,1,0:T(8,128)(2,1)S(1)} all-to-all(bf16[8,528,128]{2,1,0:T(8,128)(2,1)S(1)} %forward_1.1), channel_id=1, replica_groups=mesh['blk'=16,'rep'=8] {'rep'}, dimensions={0} | all-to-all | bytes 2162688 | tf_op jit(solution)/shard_map/all_to_all | solution.py:498
  49.6 1.2 %dense.1 = (bf16[512,128]{1,0:T(8,128)(2,1)}, bf16[8,592,128]{2,1,0:T(8,128)(2,1)S(1)}, f32[4,128,128]{2,1,0:T(8,128)S(1)}) custom-call(bf16[8,528,128]{2,1,0:T(8,128)(2,1)S(1)} %all_to_all.10.recv, bf16[512,128]{1,0:T(8,128)(2,1)S(1)} %copy-done.1, bf16[512,128]{1,0:T(8,128)(2,1)S(1)} %copy-done.2, bf16[128,128]{1,0:T(8,128)(2,1)S(1)} %copy-done.3, ...), custom_call_target="tpu_custom_call" | custom-call | tf_op jit(solution)/shard_map/dense/pallas_call | solution.py:314
  50.8 20.2 %all_to_all.11.refs_0_.recv = bf16[8,592,128]{2,1,0:T(8,128)(2,1)S(1)} all-to-all(bf16[8,592,128]{2,1,0:T(8,128)(2,1)S(1)} %get-tuple-element.37), channel_id=1, replica_groups=mesh['blk'=16,'rep'=8] {'rep'}, dimensions={0} | all-to-all | bytes 2424832 | tf_op jit(solution)/shard_map/all_to_all | solution.py:501
  71.0 3.8 %collective-permute-start.6 = (bf16[144,128]{1,0:T(8,128)(2,1)S(1)}, bf16[144,128]{1,0:T(8,128)(2,1)S(1)}, u32[]{:S(2)}, u32[]{:S(2)}) collective-permute-start(bf16[144,128]{1,0:T(8,128)(2,1)S(1)} %member_segments.1.after.refs_1_), channel_id=1, source_target_pairs={{0,64},{8,72},{16,80},{24,88},{32,96},{40,104},{48,112},{56,120},{... | collective-permute-start | bytes 110600 | tf_op jit(solution)/shard_map/ppermute | solution.py:44
  74.8 3.2 %backward_1.1.refs_0_ = bf16[4096,128]{1,0:T(8,128)(2,1)S(1)} custom-call(s32[528]{0:T(1024)S(1)} %get-tuple-element.32.entries, s32[2]{0:T(128)S(1)} %get-tuple-element.33.totals, bf16[512,128,128]{2,1,0:T(8,128)(2,1)S(1)} %get-tuple-element.34.tiles, bf16[8,592,128]{2,1,0:T(8,128)(2,1)S(1)} %all_to_all.11.refs_0_.recv, ...), custom_call_target="tpu_custom_call" | custom-call | flops 4000000000 | bytes 4456448 | tf_op jit(solution)/shard_map/backward_1/pallas_call | solution.py:359
  78.6 3.3 %collective-permute-start.8 = (bf16[144,128]{1,0:T(8,128)(2,1)S(1)}, bf16[144,128]{1,0:T(8,128)(2,1)S(1)}, u32[]{:S(2)}, u32[]{:S(2)}) collective-permute-start(bf16[144,128]{1,0:T(8,128)(2,1)S(1)} %get-tuple-element.38.after.refs_2_), channel_id=1, source_target_pairs={{0,32},{8,40},{16,48},{24,56},{32,0},{40,8},{48,16},{56,24},{64,96... | collective-permute-start | bytes 110600 | tf_op jit(solution)/shard_map/ppermute | solution.py:44
  81.9 3.3 %backward_0.1.refs_0_ = f32[4096,128]{1,0:T(8,128)S(1)} custom-call(s32[528]{0:T(1024)S(1)} %get-tuple-element.32.entries, s32[2]{0:T(128)S(1)} %get-tuple-element.33.totals, bf16[512,128,128]{2,1,0:T(8,128)(2,1)S(1)} %get-tuple-element.34.tiles, bf16[8,592,128]{2,1,0:T(8,128)(2,1)S(1)} %all_to_all.11.refs_0_.recv, ...), custom_call_target="tpu_custom_call" | custom-call | flops 4000000000 | bytes 4456448 | tf_op jit(solution)/shard_map/backward_0/pallas_call | solution.py:359
  85.4 0.8 collective-permute-start.10
  86.2 2.5 %collective-permute-start.11 = (bf16[1024,128]{1,0:T(8,128)(2,1)S(1)}, bf16[1024,128]{1,0:T(8,128)(2,1)S(1)}, u32[]{:S(2)}, u32[]{:S(2)}) collective-permute-start(bf16[1024,128]{1,0:T(8,128)(2,1)S(1)} %get-tuple-element.43), channel_id=1, source_target_pairs={{0,48},{8,56},{16,0},{24,8},{32,16},{40,24},{48,32},{56,40},{64,11... | collective-permute-start | bytes 786440 | tf_op jit(solution)/shard_map/ppermute | solution.py:44
  88.8 2.2 %collective-permute-start.16 = (bf16[512,128]{1,0:T(8,128)(2,1)S(1)}, bf16[512,128]{1,0:T(8,128)(2,1)S(1)}, u32[]{:S(2)}, u32[]{:S(2)}) collective-permute-start(bf16[512,128]{1,0:T(8,128)(2,1)S(1)} %first_sum.1.refs_5_), channel_id=1, source_target_pairs={{0,64},{8,72},{16,80},{24,88},{32,96},{40,104},{48,112},{56,120},{... | collective-permute-start | bytes 393224 | tf_op jit(solution)/shard_map/ppermute | solution.py:44
  91.0 4.3 %collective-permute-done.16.refs_1_ = bf16[512,128]{1,0:T(8,128)(2,1)S(1)} collective-permute-done((bf16[512,128]{1,0:T(8,128)(2,1)S(1)}, bf16[512,128]{1,0:T(8,128)(2,1)S(1)}, u32[]{:S(2)}, u32[]{:S(2)}) %collective-permute-start.16) | collective-permute-done | bytes 131104 | tf_op jit(solution)/shard_map/ppermute | solution.py:44
  95.3 1.0 collective-permute-start.17
  96.3 2.3 %collective-permute-start.15 = (bf16[512,128]{1,0:T(8,128)(2,1)S(1)}, bf16[512,128]{1,0:T(8,128)(2,1)S(1)}, u32[]{:S(2)}, u32[]{:S(2)}) collective-permute-start(bf16[512,128]{1,0:T(8,128)(2,1)S(1)} %z_sum.1.refs_2_), channel_id=1, source_target_pairs={{0,64},{8,72},{16,80},{24,88},{32,96},{40,104},{48,112},{56,120},{... | collective-permute-start | bytes 393224 | tf_op jit(solution)/shard_map/ppermute | solution.py:44
  98.6 1.1 %collective-permute-start.14 = (f32[64,128]{1,0:T(8,128)S(1)}, f32[64,128]{1,0:T(8,128)S(1)}, u32[]{:S(2)}, u32[]{:S(2)}) collective-permute-start(f32[64,128]{1,0:T(8,128)S(1)} %get-tuple-element.44.refs_0_), channel_id=1, source_target_pairs={{0,6},{1,7},{2,0},{3,1},{4,2},{5,3},{6,4},{7,5},{8,14},{9,15},{10,... | collective-permute-start | bytes 98312 | tf_op jit(solution)/shard_map/ppermute | solution.py:48
  99.7 1.5 %collective-permute-start.13 = (f32[64,128]{1,0:T(8,128)S(1)}, f32[64,128]{1,0:T(8,128)S(1)}, u32[]{:S(2)}, u32[]{:S(2)}) collective-permute-start(f32[64,128]{1,0:T(8,128)S(1)} %get-tuple-element.44.refs_0_), channel_id=1, source_target_pairs={{0,4},{1,5},{2,6},{3,7},{4,0},{5,1},{6,2},{7,3},{8,12},{9,13},{10,... | collective-permute-start | bytes 98312 | tf_op jit(solution)/shard_map/ppermute | solution.py:48
  101.4 0.4 collective-permute-done.17.refs_8_
  101.8 0.8 collective-permute-done.14.refs_3_
  102.6 2.5 %collective-permute-done.13.refs_2_ = f32[64,128]{1,0:T(8,128)S(1)} collective-permute-done((f32[64,128]{1,0:T(8,128)S(1)}, f32[64,128]{1,0:T(8,128)S(1)}, u32[]{:S(2)}, u32[]{:S(2)}) %collective-permute-start.13) | collective-permute-done | bytes 32800 | tf_op jit(solution)/shard_map/ppermute | solution.py:48
  105.1 1.2 %collective-permute-done.12.refs_1_ = f32[64,128]{1,0:T(8,128)S(1)} collective-permute-done((f32[64,128]{1,0:T(8,128)S(1)}, f32[64,128]{1,0:T(8,128)S(1)}, u32[]{:S(2)}, u32[]{:S(2)}) %collective-permute-start.12) | collective-permute-done | bytes 32800 | tf_op jit(solution)/shard_map/ppermute | solution.py:48
  106.3 0.9 final.1
  (41 shorter events, 1.4 us)
Async XLA Ops:
  0.6 10.1 %collective-permute-start = (bf16[512,128]{1,0:T(8,128)(2,1)}, bf16[512,128]{1,0:T(8,128)(2,1)S(1)}, u32[]{:S(2)}, u32[]{:S(2)}) collective-permute-start(bf16[512,128]{1,0:T(8,128)(2,1)} %features.1), channel_id=1, source_target_pairs={{0,64},{8,72},{16,80},{24,88},{32,96},{40,104},{48,112},{56,120},{... | collective-permute-start | bytes 393224 | tf_op jit(solution)/shard_map/ppermute | solution.py:44
  3.8 10.2 %collective-permute-start.1 = (bf16[512,128]{1,0:T(8,128)(2,1)}, bf16[512,128]{1,0:T(8,128)(2,1)S(1)}, u32[]{:S(2)}, u32[]{:S(2)}) collective-permute-start(bf16[512,128]{1,0:T(8,128)(2,1)} %features.1), channel_id=1, source_target_pairs={{0,32},{8,40},{16,48},{24,56},{32,0},{40,8},{48,16},{56,24},{64,96... | collective-permute-start | bytes 393224 | tf_op jit(solution)/shard_map/ppermute | solution.py:44
  7.7 0.9 copy-start
  8.6 0.7 copy-start.5
  9.3 0.7 copy-start.6
  10.0 0.7 copy-start.8
  10.7 11.1 %collective-permute-start.4 = (bf16[1024,128]{1,0:T(8,128)(2,1)S(1)}, bf16[1024,128]{1,0:T(8,128)(2,1)S(1)}, u32[]{:S(2)}, u32[]{:S(2)}) collective-permute-start(bf16[1024,128]{1,0:T(8,128)(2,1)S(1)} %glue.2.after.refs_3_), channel_id=1, source_target_pairs={{0,16},{8,24},{16,32},{24,40},{32,48},{40,56},{48,0},{56,8},{64,80... | collective-permute-start | bytes 786440 | tf_op jit(solution)/shard_map/ppermute | solution.py:44
  11.8 10.1 %collective-permute-start.3 = (bf16[1024,128]{1,0:T(8,128)(2,1)S(1)}, bf16[1024,128]{1,0:T(8,128)(2,1)S(1)}, u32[]{:S(2)}, u32[]{:S(2)}) collective-permute-start(bf16[1024,128]{1,0:T(8,128)(2,1)S(1)} %glue.2.after.refs_3_), channel_id=1, source_target_pairs={{0,48},{8,56},{16,0},{24,8},{32,16},{40,24},{48,32},{56,40},{64,11... | collective-permute-start | bytes 786440 | tf_op jit(solution)/shard_map/ppermute | solution.py:44
  14.0 7.8 %collective-permute-start.2 = (bf16[512,128]{1,0:T(8,128)(2,1)S(1)}, bf16[512,128]{1,0:T(8,128)(2,1)S(1)}, u32[]{:S(2)}, u32[]{:S(2)}) collective-permute-start(bf16[512,128]{1,0:T(8,128)(2,1)S(1)} %collective-permute-done.1.refs_4_), channel_id=1, source_target_pairs={{0,64},{8,72},{16,80},{24,88},{32,96},{40,104},{48,112},{56,120},{... | collective-permute-start | bytes 393224 | tf_op jit(solution)/shard_map/ppermute | solution.py:44
  22.0 3.2 %collective-permute-start.5 = (bf16[4096,128]{1,0:T(8,128)(2,1)S(1)}, bf16[4096,128]{1,0:T(8,128)(2,1)S(1)}, u32[]{:S(2)}, u32[]{:S(2)}) collective-permute-start(bf16[4096,128]{1,0:T(8,128)(2,1)S(1)} %glue.3.blocks), channel_id=1, source_target_pairs={{0,8},{8,0},{16,24},{24,16},{32,40},{40,32},{48,56},{56,48},{64,72... | collective-permute-start | bytes 3145736 | tf_op jit(solution)/shard_map/ppermute | solution.py:44
  28.5 21.1 %copy-start.1 = (bf16[512,128]{1,0:T(8,128)(2,1)S(1)}, bf16[512,128]{1,0:T(8,128)(2,1)}, u32[]{:S(2)}) copy-start(bf16[512,128]{1,0:T(8,128)(2,1)} %features.1) | copy-start | bytes 393220
  28.5 21.1 %copy-start.2 = (bf16[512,128]{1,0:T(8,128)(2,1)S(1)}, bf16[512,128]{1,0:T(8,128)(2,1)}, u32[]{:S(2)}) copy-start(bf16[512,128]{1,0:T(8,128)(2,1)} %cotangent.1) | copy-start | bytes 393220
  28.5 21.1 %copy-start.3 = (bf16[128,128]{1,0:T(8,128)(2,1)S(1)}, bf16[128,128]{1,0:T(8,128)(2,1)}, u32[]{:S(2)}) copy-start(bf16[128,128]{1,0:T(8,128)(2,1)} %w_self.1) | copy-start | bytes 98308
  28.5 21.1 %copy-start.4 = (bf16[128,128]{1,0:T(8,128)(2,1)S(1)}, bf16[128,128]{1,0:T(8,128)(2,1)}, u32[]{:S(2)}) copy-start(bf16[128,128]{1,0:T(8,128)(2,1)} %w_neigh.1) | copy-start | bytes 98308
  28.5 21.1 %copy-start.7 = (f32[128]{0:T(128)S(1)}, f32[128]{0:T(128)}, u32[]{:S(2)}) copy-start(f32[128]{0:T(128)} %param.13) | copy-start | bytes 1540
  71.0 7.0 %collective-permute-start.6 = (bf16[144,128]{1,0:T(8,128)(2,1)S(1)}, bf16[144,128]{1,0:T(8,128)(2,1)S(1)}, u32[]{:S(2)}, u32[]{:S(2)}) collective-permute-start(bf16[144,128]{1,0:T(8,128)(2,1)S(1)} %member_segments.1.after.refs_1_), channel_id=1, source_target_pairs={{0,64},{8,72},{16,80},{24,88},{32,96},{40,104},{48,112},{56,120},{... | collective-permute-start | bytes 110600 | tf_op jit(solution)/shard_map/ppermute | solution.py:44
  78.2 7.0 %collective-permute-start.7 = (bf16[4240,128]{1,0:T(8,128)(2,1)S(1)}, bf16[4240,128]{1,0:T(8,128)(2,1)S(1)}, u32[]{:S(2)}, u32[]{:S(2)}) collective-permute-start(bf16[4240,128]{1,0:T(8,128)(2,1)S(1)} %get-tuple-element.39), channel_id=1, source_target_pairs={{0,8},{8,0},{16,24},{24,16},{32,40},{40,32},{48,56},{56,48},{64,72... | collective-permute-start | bytes 3256328 | tf_op jit(solution)/shard_map/ppermute | solution.py:44
  78.3 7.0 %collective-permute-start.9 = (bf16[144,128]{1,0:T(8,128)(2,1)S(1)}, bf16[144,128]{1,0:T(8,128)(2,1)S(1)}, u32[]{:S(2)}, u32[]{:S(2)}) collective-permute-start(bf16[144,128]{1,0:T(8,128)(2,1)S(1)} %get-tuple-element.38.after.refs_2_), channel_id=1, source_target_pairs={{0,40},{8,32},{16,56},{24,48},{32,8},{40,0},{48,24},{56,16},{64,10... | collective-permute-start | bytes 110600 | tf_op jit(solution)/shard_map/ppermute | solution.py:44
  78.6 6.6 %collective-permute-start.8 = (bf16[144,128]{1,0:T(8,128)(2,1)S(1)}, bf16[144,128]{1,0:T(8,128)(2,1)S(1)}, u32[]{:S(2)}, u32[]{:S(2)}) collective-permute-start(bf16[144,128]{1,0:T(8,128)(2,1)S(1)} %get-tuple-element.38.after.refs_2_), channel_id=1, source_target_pairs={{0,32},{8,40},{16,48},{24,56},{32,0},{40,8},{48,16},{56,24},{64,96... | collective-permute-start | bytes 110600 | tf_op jit(solution)/shard_map/ppermute | solution.py:44
  85.4 10.8 %collective-permute-start.10 = (bf16[1168,128]{1,0:T(8,128)(2,1)S(1)}, bf16[1168,128]{1,0:T(8,128)(2,1)S(1)}, u32[]{:S(2)}, u32[]{:S(2)}) collective-permute-start(bf16[1168,128]{1,0:T(8,128)(2,1)S(1)} %get-tuple-element.41), channel_id=1, source_target_pairs={{0,16},{8,24},{16,32},{24,40},{32,48},{40,56},{48,0},{56,8},{64,80... | collective-permute-start | bytes 897032 | tf_op jit(solution)/shard_map/ppermute | solution.py:44
  86.2 10.0 %collective-permute-start.11 = (bf16[1024,128]{1,0:T(8,128)(2,1)S(1)}, bf16[1024,128]{1,0:T(8,128)(2,1)S(1)}, u32[]{:S(2)}, u32[]{:S(2)}) collective-permute-start(bf16[1024,128]{1,0:T(8,128)(2,1)S(1)} %get-tuple-element.43), channel_id=1, source_target_pairs={{0,48},{8,56},{16,0},{24,8},{32,16},{40,24},{48,32},{56,40},{64,11... | collective-permute-start | bytes 786440 | tf_op jit(solution)/shard_map/ppermute | solution.py:44
  88.8 6.5 %collective-permute-start.16 = (bf16[512,128]{1,0:T(8,128)(2,1)S(1)}, bf16[512,128]{1,0:T(8,128)(2,1)S(1)}, u32[]{:S(2)}, u32[]{:S(2)}) collective-permute-start(bf16[512,128]{1,0:T(8,128)(2,1)S(1)} %first_sum.1.refs_5_), channel_id=1, source_target_pairs={{0,64},{8,72},{16,80},{24,88},{32,96},{40,104},{48,112},{56,120},{... | collective-permute-start | bytes 393224 | tf_op jit(solution)/shard_map/ppermute | solution.py:44
  95.3 6.6 %collective-permute-start.17 = (bf16[512,128]{1,0:T(8,128)(2,1)S(1)}, bf16[512,128]{1,0:T(8,128)(2,1)S(1)}, u32[]{:S(2)}, u32[]{:S(2)}) collective-permute-start(bf16[512,128]{1,0:T(8,128)(2,1)S(1)} %rounded_sum.1), channel_id=1, source_target_pairs={{0,32},{8,40},{16,48},{24,56},{32,0},{40,8},{48,16},{56,24},{64,96... | collective-permute-start | bytes 393224 | tf_op jit(solution)/shard_map/ppermute | solution.py:44
  96.3 10.0 %collective-permute-start.15 = (bf16[512,128]{1,0:T(8,128)(2,1)S(1)}, bf16[512,128]{1,0:T(8,128)(2,1)S(1)}, u32[]{:S(2)}, u32[]{:S(2)}) collective-permute-start(bf16[512,128]{1,0:T(8,128)(2,1)S(1)} %z_sum.1.refs_2_), channel_id=1, source_target_pairs={{0,64},{8,72},{16,80},{24,88},{32,96},{40,104},{48,112},{56,120},{... | collective-permute-start | bytes 393224 | tf_op jit(solution)/shard_map/ppermute | solution.py:44
  98.6 4.0 %collective-permute-start.14 = (f32[64,128]{1,0:T(8,128)S(1)}, f32[64,128]{1,0:T(8,128)S(1)}, u32[]{:S(2)}, u32[]{:S(2)}) collective-permute-start(f32[64,128]{1,0:T(8,128)S(1)} %get-tuple-element.44.refs_0_), channel_id=1, source_target_pairs={{0,6},{1,7},{2,0},{3,1},{4,2},{5,3},{6,4},{7,5},{8,14},{9,15},{10,... | collective-permute-start | bytes 98312 | tf_op jit(solution)/shard_map/ppermute | solution.py:48
  99.7 5.4 %collective-permute-start.13 = (f32[64,128]{1,0:T(8,128)S(1)}, f32[64,128]{1,0:T(8,128)S(1)}, u32[]{:S(2)}, u32[]{:S(2)}) collective-permute-start(f32[64,128]{1,0:T(8,128)S(1)} %get-tuple-element.44.refs_0_), channel_id=1, source_target_pairs={{0,4},{1,5},{2,6},{3,7},{4,0},{5,1},{6,2},{7,3},{8,12},{9,13},{10,... | collective-permute-start | bytes 98312 | tf_op jit(solution)/shard_map/ppermute | solution.py:48
  101.2 5.1 %collective-permute-start.12 = (f32[64,128]{1,0:T(8,128)S(1)}, f32[64,128]{1,0:T(8,128)S(1)}, u32[]{:S(2)}, u32[]{:S(2)}) collective-permute-start(f32[64,128]{1,0:T(8,128)S(1)} %get-tuple-element.44.refs_0_), channel_id=1, source_target_pairs={{0,2},{1,3},{2,4},{3,5},{4,6},{5,7},{6,0},{7,1},{8,10},{9,11},{10,... | collective-permute-start | bytes 98312 | tf_op jit(solution)/shard_map/ppermute | solution.py:48

commit v5 on v4

--- a/solution.py
+++ b/solution.py
@@ -131,14 +131,17 @@
         each_copy(p, lambda copy: copy.wait())
         count = counts[0, 0, p]
 
-        def step(g, _):
-            for u in range(SMALL):
-                k = g * SMALL + u
+        def step(first, size):
+            for u in range(size):
+                k = first + u
                 d = jnp.where(k < count, dest_of(words[0, 0, p, k]), NDST)
                 acc[d] += held[p * SLOTS + k].astype(f32)
             return 0
 
-        lax.fori_loop(0, (count + SMALL - 1) // SMALL, step, 0)
+        whole = count // CH
+        lax.fori_loop(0, whole, lambda g, _: step(g * CH, CH), 0)
+        rest = (count - whole * CH + SMALL - 1) // SMALL
+        lax.fori_loop(0, rest, lambda g, _: step(whole * CH + g * SMALL, SMALL), 0)
         return 0
 
     lax.fori_loop(0, 16, add, 0)

time: 108 us -> 107 us (level)
  starting transfers between devices: 30.5 us -> 27.2 us
  Pallas kernels: 22.4 us -> 23.8 us
  waiting for transfers between devices: 9.24 us -> 10.4 us
    ppermute x15, starting transfers between devices: 27.7 us -> 24.5 us  [moved(): return lax.ppermute(value, 'blk', pairs)]
    ppermute x15, waiting for transfers between devices: 4.74 us -> 6.84 us  [moved(): return lax.ppermute(value, 'blk', pairs)]
  transfers between devices with their start and end apart: 18 -> 18, of which waited for: 5 -> 5; matrix products, arithmetic and copies ran while one was open for 0% -> 0% of each run, Pallas kernels for 16% -> 17%
where the time goes in v5:
time: 107 us
  blocking collectives  41.4 us (39%)
  starting transfers between devices  27.2 us (25%)
  Pallas kernels  23.8 us (22%)
  waiting for transfers between devices  10.4 us (10%)
  local copies, waits for them, and re-layouts  3.02 us (3%)
    ppermute x15, starting transfers between devices, moved(): return lax.ppermute(value, 'blk', pairs)  24.5 us
    all_to_all x1, blocking collectives, shards(): recv = lax.all_to_all(sums, 'rep', 0, 0)  21 us
    all_to_all x1, blocking collectives, shards(): spread = lax.all_to_all(payload, 'rep', 0, 0)  20.4 us
    pallas_call x1, Pallas kernels, load(): pl.pallas_call(load_kernel, name='load', out_shape=(jax.ShapeDtypeStruct(...  7.44 us
    pallas_call x2, Pallas kernels, backward(): pl.pallas_call(functools.partial(backward_kernel, dc), name=f'backward_{d...  6.9 us
    ppermute x15, waiting for transfers between devices, moved(): return lax.ppermute(value, 'blk', pairs)  6.84 us
    pallas_call x2, Pallas kernels, forward(): pl.pallas_call(functools.partial(forward_kernel, dc), name=f'forward_{dc}...  6.8 us
    ppermute x3, waiting for transfers between devices, moved_y(): lax.ppermute(value, 'rep', [(i, (i // 2 + dy) % 4 * 2 + i % 2) for i in r...  3.55 us
  transfers between devices with their start and end apart: 18, of which 5 were waited for; matrix products, arithmetic and copies ran while one was open for 0% of the time, Pallas kernels for 17%

profile of v5, /device:TPU:0, one launch (start us, length us, event | category | flops | bytes accessed | tf_op | source)
XLA Modules:
  0.0 106.6 jit_solution(16269943498027400786)
XLA Ops:
  0.6 3.2 %collective-permute-start = (bf16[512,128]{1,0:T(8,128)(2,1)}, bf16[512,128]{1,0:T(8,128)(2,1)S(1)}, u32[]{:S(2)}, u32[]{:S(2)}) collective-permute-start(bf16[512,128]{1,0:T(8,128)(2,1)} %features.1), channel_id=1, source_target_pairs={{0,64},{8,72},{16,80},{24,88},{32,96},{40,104},{48,112},{56,120},{... | collective-permute-start | bytes 393224 | tf_op jit(solution)/shard_map/ppermute | solution.py:44
  3.8 3.9 %collective-permute-start.1 = (bf16[512,128]{1,0:T(8,128)(2,1)}, bf16[512,128]{1,0:T(8,128)(2,1)S(1)}, u32[]{:S(2)}, u32[]{:S(2)}) collective-permute-start(bf16[512,128]{1,0:T(8,128)(2,1)} %features.1), channel_id=1, source_target_pairs={{0,32},{8,40},{16,48},{24,56},{32,0},{40,8},{48,16},{56,24},{64,96... | collective-permute-start | bytes 393224 | tf_op jit(solution)/shard_map/ppermute | solution.py:44
  7.7 0.9 copy-done
  8.6 0.7 copy-done.5
  9.3 0.7 copy-done.6
  10.0 0.7 copy-done.8
  10.7 1.1 %collective-permute-start.4 = (bf16[1024,128]{1,0:T(8,128)(2,1)S(1)}, bf16[1024,128]{1,0:T(8,128)(2,1)S(1)}, u32[]{:S(2)}, u32[]{:S(2)}) collective-permute-start(bf16[1024,128]{1,0:T(8,128)(2,1)S(1)} %glue.2.after.refs_3_), channel_id=1, source_target_pairs={{0,16},{8,24},{16,32},{24,40},{32,48},{40,56},{48,0},{56,8},{64,80... | collective-permute-start | bytes 786440 | tf_op jit(solution)/shard_map/ppermute | solution.py:44
  11.8 2.2 %collective-permute-start.3 = (bf16[1024,128]{1,0:T(8,128)(2,1)S(1)}, bf16[1024,128]{1,0:T(8,128)(2,1)S(1)}, u32[]{:S(2)}, u32[]{:S(2)}) collective-permute-start(bf16[1024,128]{1,0:T(8,128)(2,1)S(1)} %glue.2.after.refs_3_), channel_id=1, source_target_pairs={{0,48},{8,56},{16,0},{24,8},{32,16},{40,24},{48,32},{56,40},{64,11... | collective-permute-start | bytes 786440 | tf_op jit(solution)/shard_map/ppermute | solution.py:44
  14.0 0.9 collective-permute-start.2
  15.0 7.4 %load.1 = (bf16[512,128,128]{2,1,0:T(8,128)(2,1)S(1)}, f32[32,128]{1,0:T(8,128)S(1)}, s32[528]{0:T(1024)S(1)}, s32[2]{0:T(128)S(1)}) custom-call(s32[1,1,16,32]{3,2,1,0:T(8,128)S(1)} %get-tuple-element.29.refs_2_.words_in, s32[1,1,16]{2,1,0:T(1,128)S(1)} %get-tuple-element.30.counts_in, bf16[16,32,128,128]{3,2,1,0:T(8,128)(2,1)} %bitcast.4, ...), custom_call_target="tpu_custom_call" | custom-call | flops 10000000000 | bytes 12000000 | tf_op jit(solution)/shard_map/load/pallas_call | solution.py:155
  22.6 3.9 %forward_0.1.refs_0_ = f32[33,128,128]{2,1,0:T(8,128)S(1)} custom-call(s32[528]{0:T(1024)S(1)} %get-tuple-element.32.entries, s32[2]{0:T(128)S(1)} %get-tuple-element.33.totals, bf16[512,128,128]{2,1,0:T(8,128)(2,1)S(1)} %get-tuple-element.34.tiles, bf16[4096,128]{1,0:T(8,128)(2,1)S(1)} %glue.3.blocks), custom_call_target="tpu_custom_call" | custom-call | flops 4000000000 | bytes 4456448 | tf_op jit(solution)/shard_map/forward_0/pallas_call | solution.py:256
  26.5 2.9 %forward_1.1 = bf16[8,528,128]{2,1,0:T(8,128)(2,1)S(1)} custom-call(s32[528]{0:T(1024)S(1)} %get-tuple-element.32.entries, s32[2]{0:T(128)S(1)} %get-tuple-element.33.totals, bf16[512,128,128]{2,1,0:T(8,128)(2,1)S(1)} %get-tuple-element.34.tiles, bf16[4096,128]{1,0:T(8,128)(2,1)S(1)} %collective-permute-done.5.blocks, f32[33,128,128]{2,1,0:T(8,128)S(1)} %forward_0.1.refs_0_, ...), custom_call_target="tpu_custom_call" | custom-call | flops 4000000000 | bytes 4456448 | tf_op jit(solution)/shard_map/forward_1/pallas_call | solution.py:256
  29.5 21.0 %all_to_all.10.recv = bf16[8,528,128]{2,1,0:T(8,128)(2,1)S(1)} all-to-all(bf16[8,528,128]{2,1,0:T(8,128)(2,1)S(1)} %forward_1.1), channel_id=1, replica_groups=mesh['blk'=16,'rep'=8] {'rep'}, dimensions={0} | all-to-all | bytes 2162688 | tf_op jit(solution)/shard_map/all_to_all | solution.py:501
  50.5 1.2 %dense.1 = (bf16[512,128]{1,0:T(8,128)(2,1)}, bf16[8,592,128]{2,1,0:T(8,128)(2,1)S(1)}, f32[4,128,128]{2,1,0:T(8,128)S(1)}) custom-call(bf16[8,528,128]{2,1,0:T(8,128)(2,1)S(1)} %all_to_all.10.recv, bf16[512,128]{1,0:T(8,128)(2,1)S(1)} %copy-done.1, bf16[512,128]{1,0:T(8,128)(2,1)S(1)} %copy-done.2, bf16[128,128]{1,0:T(8,128)(2,1)S(1)} %copy-done.3, ...), custom_call_target="tpu_custom_call" | custom-call | tf_op jit(solution)/shard_map/dense/pallas_call | solution.py:317
  51.7 20.4 %all_to_all.11.refs_0_.recv = bf16[8,592,128]{2,1,0:T(8,128)(2,1)S(1)} all-to-all(bf16[8,592,128]{2,1,0:T(8,128)(2,1)S(1)} %get-tuple-element.37), channel_id=1, replica_groups=mesh['blk'=16,'rep'=8] {'rep'}, dimensions={0} | all-to-all | bytes 2424832 | tf_op jit(solution)/shard_map/all_to_all | solution.py:504
  72.1 2.1 %collective-permute-start.6 = (bf16[144,128]{1,0:T(8,128)(2,1)S(1)}, bf16[144,128]{1,0:T(8,128)(2,1)S(1)}, u32[]{:S(2)}, u32[]{:S(2)}) collective-permute-start(bf16[144,128]{1,0:T(8,128)(2,1)S(1)} %member_segments.1.after.refs_1_), channel_id=1, source_target_pairs={{0,64},{8,72},{16,80},{24,88},{32,96},{40,104},{48,112},{56,120},{... | collective-permute-start | bytes 110600 | tf_op jit(solution)/shard_map/ppermute | solution.py:44
  74.3 2.9 %backward_1.1.refs_0_ = bf16[4096,128]{1,0:T(8,128)(2,1)S(1)} custom-call(s32[528]{0:T(1024)S(1)} %get-tuple-element.32.entries, s32[2]{0:T(128)S(1)} %get-tuple-element.33.totals, bf16[512,128,128]{2,1,0:T(8,128)(2,1)S(1)} %get-tuple-element.34.tiles, bf16[8,592,128]{2,1,0:T(8,128)(2,1)S(1)} %all_to_all.11.refs_0_.recv, ...), custom_call_target="tpu_custom_call" | custom-call | flops 4000000000 | bytes 4456448 | tf_op jit(solution)/shard_map/backward_1/pallas_call | solution.py:362
  77.2 0.5 collective-permute-done.6.refs_2_
  77.9 0.9 collective-permute-start.9
  78.7 2.8 %collective-permute-start.8 = (bf16[144,128]{1,0:T(8,128)(2,1)S(1)}, bf16[144,128]{1,0:T(8,128)(2,1)S(1)}, u32[]{:S(2)}, u32[]{:S(2)}) collective-permute-start(bf16[144,128]{1,0:T(8,128)(2,1)S(1)} %get-tuple-element.38.after.refs_2_), channel_id=1, source_target_pairs={{0,32},{8,40},{16,48},{24,56},{32,0},{40,8},{48,16},{56,24},{64,96... | collective-permute-start | bytes 110600 | tf_op jit(solution)/shard_map/ppermute | solution.py:44
  81.5 4.0 %backward_0.1.refs_0_ = f32[4096,128]{1,0:T(8,128)S(1)} custom-call(s32[528]{0:T(1024)S(1)} %get-tuple-element.32.entries, s32[2]{0:T(128)S(1)} %get-tuple-element.33.totals, bf16[512,128,128]{2,1,0:T(8,128)(2,1)S(1)} %get-tuple-element.34.tiles, bf16[8,592,128]{2,1,0:T(8,128)(2,1)S(1)} %all_to_all.11.refs_0_.recv, ...), custom_call_target="tpu_custom_call" | custom-call | flops 4000000000 | bytes 4456448 | tf_op jit(solution)/shard_map/backward_0/pallas_call | solution.py:362
  85.8 0.5 collective-permute-start.10
  86.3 2.8 %collective-permute-start.11 = (bf16[1024,128]{1,0:T(8,128)(2,1)S(1)}, bf16[1024,128]{1,0:T(8,128)(2,1)S(1)}, u32[]{:S(2)}, u32[]{:S(2)}) collective-permute-start(bf16[1024,128]{1,0:T(8,128)(2,1)S(1)} %get-tuple-element.43), channel_id=1, source_target_pairs={{0,48},{8,56},{16,0},{24,8},{32,16},{40,24},{48,32},{56,40},{64,11... | collective-permute-start | bytes 786440 | tf_op jit(solution)/shard_map/ppermute | solution.py:44
  89.1 1.5 %collective-permute-start.16 = (bf16[512,128]{1,0:T(8,128)(2,1)S(1)}, bf16[512,128]{1,0:T(8,128)(2,1)S(1)}, u32[]{:S(2)}, u32[]{:S(2)}) collective-permute-start(bf16[512,128]{1,0:T(8,128)(2,1)S(1)} %first_sum.1.refs_5_), channel_id=1, source_target_pairs={{0,64},{8,72},{16,80},{24,88},{32,96},{40,104},{48,112},{56,120},{... | collective-permute-start | bytes 393224 | tf_op jit(solution)/shard_map/ppermute | solution.py:44
  90.6 4.9 %collective-permute-done.16.refs_1_ = bf16[512,128]{1,0:T(8,128)(2,1)S(1)} collective-permute-done((bf16[512,128]{1,0:T(8,128)(2,1)S(1)}, bf16[512,128]{1,0:T(8,128)(2,1)S(1)}, u32[]{:S(2)}, u32[]{:S(2)}) %collective-permute-start.16) | collective-permute-done | bytes 131104 | tf_op jit(solution)/shard_map/ppermute | solution.py:44
  95.9 2.1 %collective-permute-start.15 = (bf16[512,128]{1,0:T(8,128)(2,1)S(1)}, bf16[512,128]{1,0:T(8,128)(2,1)S(1)}, u32[]{:S(2)}, u32[]{:S(2)}) collective-permute-start(bf16[512,128]{1,0:T(8,128)(2,1)S(1)} %z_sum.1.refs_2_), channel_id=1, source_target_pairs={{0,64},{8,72},{16,80},{24,88},{32,96},{40,104},{48,112},{56,120},{... | collective-permute-start | bytes 393224 | tf_op jit(solution)/shard_map/ppermute | solution.py:44
  98.1 1.0 collective-permute-start.14
  99.1 1.5 %collective-permute-start.13 = (f32[64,128]{1,0:T(8,128)S(1)}, f32[64,128]{1,0:T(8,128)S(1)}, u32[]{:S(2)}, u32[]{:S(2)}) collective-permute-start(f32[64,128]{1,0:T(8,128)S(1)} %get-tuple-element.44.refs_0_), channel_id=1, source_target_pairs={{0,4},{1,5},{2,6},{3,7},{4,0},{5,1},{6,2},{7,3},{8,12},{9,13},{10,... | collective-permute-start | bytes 98312 | tf_op jit(solution)/shard_map/ppermute | solution.py:48
  100.7 1.4 %collective-permute-done.17.refs_8_ = bf16[512,128]{1,0:T(8,128)(2,1)S(1)} collective-permute-done((bf16[512,128]{1,0:T(8,128)(2,1)S(1)}, bf16[512,128]{1,0:T(8,128)(2,1)S(1)}, u32[]{:S(2)}, u32[]{:S(2)}) %collective-permute-start.17) | collective-permute-done | bytes 131104 | tf_op jit(solution)/shard_map/ppermute | solution.py:44
  102.1 2.4 %collective-permute-done.13.refs_2_ = f32[64,128]{1,0:T(8,128)S(1)} collective-permute-done((f32[64,128]{1,0:T(8,128)S(1)}, f32[64,128]{1,0:T(8,128)S(1)}, u32[]{:S(2)}, u32[]{:S(2)}) %collective-permute-start.13) | collective-permute-done | bytes 32800 | tf_op jit(solution)/shard_map/ppermute | solution.py:48
  104.5 1.2 %collective-permute-done.12.refs_1_ = f32[64,128]{1,0:T(8,128)S(1)} collective-permute-done((f32[64,128]{1,0:T(8,128)S(1)}, f32[64,128]{1,0:T(8,128)S(1)}, u32[]{:S(2)}, u32[]{:S(2)}) %collective-permute-start.12) | collective-permute-done | bytes 32800 | tf_op jit(solution)/shard_map/ppermute | solution.py:48
  105.7 0.9 final.1
  (41 shorter events, 1.2 us)
Async XLA Ops:
  0.6 10.1 %collective-permute-start = (bf16[512,128]{1,0:T(8,128)(2,1)}, bf16[512,128]{1,0:T(8,128)(2,1)S(1)}, u32[]{:S(2)}, u32[]{:S(2)}) collective-permute-start(bf16[512,128]{1,0:T(8,128)(2,1)} %features.1), channel_id=1, source_target_pairs={{0,64},{8,72},{16,80},{24,88},{32,96},{40,104},{48,112},{56,120},{... | collective-permute-start | bytes 393224 | tf_op jit(solution)/shard_map/ppermute | solution.py:44
  3.8 10.2 %collective-permute-start.1 = (bf16[512,128]{1,0:T(8,128)(2,1)}, bf16[512,128]{1,0:T(8,128)(2,1)S(1)}, u32[]{:S(2)}, u32[]{:S(2)}) collective-permute-start(bf16[512,128]{1,0:T(8,128)(2,1)} %features.1), channel_id=1, source_target_pairs={{0,32},{8,40},{16,48},{24,56},{32,0},{40,8},{48,16},{56,24},{64,96... | collective-permute-start | bytes 393224 | tf_op jit(solution)/shard_map/ppermute | solution.py:44
  7.7 0.9 copy-start
  8.6 0.7 copy-start.5
  9.3 0.7 copy-start.6
  10.0 0.7 copy-start.8
  10.7 11.7 %collective-permute-start.4 = (bf16[1024,128]{1,0:T(8,128)(2,1)S(1)}, bf16[1024,128]{1,0:T(8,128)(2,1)S(1)}, u32[]{:S(2)}, u32[]{:S(2)}) collective-permute-start(bf16[1024,128]{1,0:T(8,128)(2,1)S(1)} %glue.2.after.refs_3_), channel_id=1, source_target_pairs={{0,16},{8,24},{16,32},{24,40},{32,48},{40,56},{48,0},{56,8},{64,80... | collective-permute-start | bytes 786440 | tf_op jit(solution)/shard_map/ppermute | solution.py:44
  11.8 10.6 %collective-permute-start.3 = (bf16[1024,128]{1,0:T(8,128)(2,1)S(1)}, bf16[1024,128]{1,0:T(8,128)(2,1)S(1)}, u32[]{:S(2)}, u32[]{:S(2)}) collective-permute-start(bf16[1024,128]{1,0:T(8,128)(2,1)S(1)} %glue.2.after.refs_3_), channel_id=1, source_target_pairs={{0,48},{8,56},{16,0},{24,8},{32,16},{40,24},{48,32},{56,40},{64,11... | collective-permute-start | bytes 786440 | tf_op jit(solution)/shard_map/ppermute | solution.py:44
  14.0 8.4 %collective-permute-start.2 = (bf16[512,128]{1,0:T(8,128)(2,1)S(1)}, bf16[512,128]{1,0:T(8,128)(2,1)S(1)}, u32[]{:S(2)}, u32[]{:S(2)}) collective-permute-start(bf16[512,128]{1,0:T(8,128)(2,1)S(1)} %collective-permute-done.1.refs_4_), channel_id=1, source_target_pairs={{0,64},{8,72},{16,80},{24,88},{32,96},{40,104},{48,112},{56,120},{... | collective-permute-start | bytes 393224 | tf_op jit(solution)/shard_map/ppermute | solution.py:44
  22.5 4.0 %collective-permute-start.5 = (bf16[4096,128]{1,0:T(8,128)(2,1)S(1)}, bf16[4096,128]{1,0:T(8,128)(2,1)S(1)}, u32[]{:S(2)}, u32[]{:S(2)}) collective-permute-start(bf16[4096,128]{1,0:T(8,128)(2,1)S(1)} %glue.3.blocks), channel_id=1, source_target_pairs={{0,8},{8,0},{16,24},{24,16},{32,40},{40,32},{48,56},{56,48},{64,72... | collective-permute-start | bytes 3145736 | tf_op jit(solution)/shard_map/ppermute | solution.py:44
  29.5 21.0 %copy-start.1 = (bf16[512,128]{1,0:T(8,128)(2,1)S(1)}, bf16[512,128]{1,0:T(8,128)(2,1)}, u32[]{:S(2)}) copy-start(bf16[512,128]{1,0:T(8,128)(2,1)} %features.1) | copy-start | bytes 393220
  29.5 21.0 %copy-start.2 = (bf16[512,128]{1,0:T(8,128)(2,1)S(1)}, bf16[512,128]{1,0:T(8,128)(2,1)}, u32[]{:S(2)}) copy-start(bf16[512,128]{1,0:T(8,128)(2,1)} %cotangent.1) | copy-start | bytes 393220
  29.5 21.0 %copy-start.3 = (bf16[128,128]{1,0:T(8,128)(2,1)S(1)}, bf16[128,128]{1,0:T(8,128)(2,1)}, u32[]{:S(2)}) copy-start(bf16[128,128]{1,0:T(8,128)(2,1)} %w_self.1) | copy-start | bytes 98308
  29.5 21.0 %copy-start.4 = (bf16[128,128]{1,0:T(8,128)(2,1)S(1)}, bf16[128,128]{1,0:T(8,128)(2,1)}, u32[]{:S(2)}) copy-start(bf16[128,128]{1,0:T(8,128)(2,1)} %w_neigh.1) | copy-start | bytes 98308
  29.5 21.0 %copy-start.7 = (f32[128]{0:T(128)S(1)}, f32[128]{0:T(128)}, u32[]{:S(2)}) copy-start(f32[128]{0:T(128)} %param.13) | copy-start | bytes 1540
  72.1 5.5 %collective-permute-start.6 = (bf16[144,128]{1,0:T(8,128)(2,1)S(1)}, bf16[144,128]{1,0:T(8,128)(2,1)S(1)}, u32[]{:S(2)}, u32[]{:S(2)}) collective-permute-start(bf16[144,128]{1,0:T(8,128)(2,1)S(1)} %member_segments.1.after.refs_1_), channel_id=1, source_target_pairs={{0,64},{8,72},{16,80},{24,88},{32,96},{40,104},{48,112},{56,120},{... | collective-permute-start | bytes 110600 | tf_op jit(solution)/shard_map/ppermute | solution.py:44
  77.8 7.7 %collective-permute-start.7 = (bf16[4240,128]{1,0:T(8,128)(2,1)S(1)}, bf16[4240,128]{1,0:T(8,128)(2,1)S(1)}, u32[]{:S(2)}, u32[]{:S(2)}) collective-permute-start(bf16[4240,128]{1,0:T(8,128)(2,1)S(1)} %get-tuple-element.39), channel_id=1, source_target_pairs={{0,8},{8,0},{16,24},{24,16},{32,40},{40,32},{48,56},{56,48},{64,72... | collective-permute-start | bytes 3256328 | tf_op jit(solution)/shard_map/ppermute | solution.py:44
  77.9 7.7 %collective-permute-start.9 = (bf16[144,128]{1,0:T(8,128)(2,1)S(1)}, bf16[144,128]{1,0:T(8,128)(2,1)S(1)}, u32[]{:S(2)}, u32[]{:S(2)}) collective-permute-start(bf16[144,128]{1,0:T(8,128)(2,1)S(1)} %get-tuple-element.38.after.refs_2_), channel_id=1, source_target_pairs={{0,40},{8,32},{16,56},{24,48},{32,8},{40,0},{48,24},{56,16},{64,10... | collective-permute-start | bytes 110600 | tf_op jit(solution)/shard_map/ppermute | solution.py:44
  78.7 6.8 %collective-permute-start.8 = (bf16[144,128]{1,0:T(8,128)(2,1)S(1)}, bf16[144,128]{1,0:T(8,128)(2,1)S(1)}, u32[]{:S(2)}, u32[]{:S(2)}) collective-permute-start(bf16[144,128]{1,0:T(8,128)(2,1)S(1)} %get-tuple-element.38.after.refs_2_), channel_id=1, source_target_pairs={{0,32},{8,40},{16,48},{24,56},{32,0},{40,8},{48,16},{56,24},{64,96... | collective-permute-start | bytes 110600 | tf_op jit(solution)/shard_map/ppermute | solution.py:44
  85.8 10.1 %collective-permute-start.10 = (bf16[1168,128]{1,0:T(8,128)(2,1)S(1)}, bf16[1168,128]{1,0:T(8,128)(2,1)S(1)}, u32[]{:S(2)}, u32[]{:S(2)}) collective-permute-start(bf16[1168,128]{1,0:T(8,128)(2,1)S(1)} %get-tuple-element.41), channel_id=1, source_target_pairs={{0,16},{8,24},{16,32},{24,40},{32,48},{40,56},{48,0},{56,8},{64,80... | collective-permute-start | bytes 897032 | tf_op jit(solution)/shard_map/ppermute | solution.py:44
  86.3 9.6 %collective-permute-start.11 = (bf16[1024,128]{1,0:T(8,128)(2,1)S(1)}, bf16[1024,128]{1,0:T(8,128)(2,1)S(1)}, u32[]{:S(2)}, u32[]{:S(2)}) collective-permute-start(bf16[1024,128]{1,0:T(8,128)(2,1)S(1)} %get-tuple-element.43), channel_id=1, source_target_pairs={{0,48},{8,56},{16,0},{24,8},{32,16},{40,24},{48,32},{56,40},{64,11... | collective-permute-start | bytes 786440 | tf_op jit(solution)/shard_map/ppermute | solution.py:44
  89.1 6.5 %collective-permute-start.16 = (bf16[512,128]{1,0:T(8,128)(2,1)S(1)}, bf16[512,128]{1,0:T(8,128)(2,1)S(1)}, u32[]{:S(2)}, u32[]{:S(2)}) collective-permute-start(bf16[512,128]{1,0:T(8,128)(2,1)S(1)} %first_sum.1.refs_5_), channel_id=1, source_target_pairs={{0,64},{8,72},{16,80},{24,88},{32,96},{40,104},{48,112},{56,120},{... | collective-permute-start | bytes 393224 | tf_op jit(solution)/shard_map/ppermute | solution.py:44
  95.6 6.6 %collective-permute-start.17 = (bf16[512,128]{1,0:T(8,128)(2,1)S(1)}, bf16[512,128]{1,0:T(8,128)(2,1)S(1)}, u32[]{:S(2)}, u32[]{:S(2)}) collective-permute-start(bf16[512,128]{1,0:T(8,128)(2,1)S(1)} %rounded_sum.1), channel_id=1, source_target_pairs={{0,32},{8,40},{16,48},{24,56},{32,0},{40,8},{48,16},{56,24},{64,96... | collective-permute-start | bytes 393224 | tf_op jit(solution)/shard_map/ppermute | solution.py:44
  95.9 9.8 %collective-permute-start.15 = (bf16[512,128]{1,0:T(8,128)(2,1)S(1)}, bf16[512,128]{1,0:T(8,128)(2,1)S(1)}, u32[]{:S(2)}, u32[]{:S(2)}) collective-permute-start(bf16[512,128]{1,0:T(8,128)(2,1)S(1)} %z_sum.1.refs_2_), channel_id=1, source_target_pairs={{0,64},{8,72},{16,80},{24,88},{32,96},{40,104},{48,112},{56,120},{... | collective-permute-start | bytes 393224 | tf_op jit(solution)/shard_map/ppermute | solution.py:44
  98.1 4.1 %collective-permute-start.14 = (f32[64,128]{1,0:T(8,128)S(1)}, f32[64,128]{1,0:T(8,128)S(1)}, u32[]{:S(2)}, u32[]{:S(2)}) collective-permute-start(f32[64,128]{1,0:T(8,128)S(1)} %get-tuple-element.44.refs_0_), channel_id=1, source_target_pairs={{0,6},{1,7},{2,0},{3,1},{4,2},{5,3},{6,4},{7,5},{8,14},{9,15},{10,... | collective-permute-start | bytes 98312 | tf_op jit(solution)/shard_map/ppermute | solution.py:48
  99.1 5.4 %collective-permute-start.13 = (f32[64,128]{1,0:T(8,128)S(1)}, f32[64,128]{1,0:T(8,128)S(1)}, u32[]{:S(2)}, u32[]{:S(2)}) collective-permute-start(f32[64,128]{1,0:T(8,128)S(1)} %get-tuple-element.44.refs_0_), channel_id=1, source_target_pairs={{0,4},{1,5},{2,6},{3,7},{4,0},{5,1},{6,2},{7,3},{8,12},{9,13},{10,... | collective-permute-start | bytes 98312 | tf_op jit(solution)/shard_map/ppermute | solution.py:48
  100.6 5.1 %collective-permute-start.12 = (f32[64,128]{1,0:T(8,128)S(1)}, f32[64,128]{1,0:T(8,128)S(1)}, u32[]{:S(2)}, u32[]{:S(2)}) collective-permute-start(f32[64,128]{1,0:T(8,128)S(1)} %get-tuple-element.44.refs_0_), channel_id=1, source_target_pairs={{0,2},{1,3},{2,4},{3,5},{4,6},{5,7},{6,0},{7,1},{8,10},{9,11},{10,... | collective-permute-start | bytes 98312 | tf_op jit(solution)/shard_map/ppermute | solution.py:48
